TPU v7x, 128 devices: a whole 4x4x4 slice. The times are simulated.
128 devices in a mesh: section: 16 (over y_lo, x, core), dp: 8 (over y_hi, z).
Axes of the slice: x: 4, y: 4 (y_hi: 2, y_lo: 2; y = y_hi * 2 + y_lo), z: 4, core: 2. Of those that a mesh axis runs over, the one named last changes fastest.
Arguments:
- pending_adjoints: bfloat16 [2, 16, 8, 16, 32, 256], P(None, 'section', 'dp'), may hold values from -6 to 6
- objective_adjoints: bfloat16 [3, 8, 16, 32, 256], P(None, 'dp'), may hold values from -6 to 6
- kept_block_entries: bfloat16 [2, 16, 4, 8, 16, 32, 256], P(None, 'section', None, 'dp'), may hold values from -6 to 6
- kept_early_presums: bfloat16 [2, 16, 4, 8, 16, 32, 256], P(None, 'section', None, 'dp'), may hold values from -6 to 6
- kept_later_presums: bfloat16 [2, 16, 4, 8, 16, 32, 256], P(None, 'section', None, 'dp'), may hold values from -6 to 6
- filter_taps: bfloat16 [2, 16, 2, 9, 256, 256], P(None, 'section'), may hold values from -0.1875 to 0.1875
- slot_timetable: int32 [4, 32], replicated, may hold values from 0 to 3, as said below
Outputs:
- final_grads: bfloat16 [2, 16, 8, 16, 32, 256], P(None, 'section', 'dp')
- weight_grads: float32 [2, 16, 2, 9, 256, 256], P(None, 'section', None, None, 'dp')
Inputs may be any that keep to these rules, and one draw needn't show every extreme that they name: `slot_timetable`: in each column the slot rises by one from tick to tick, modulo 4, from a starting slot drawn for each section, so each section visits every slot once.
All inputs are finite; a program needn't handle non-finite values.
Results may differ from a plain program's by a relative error of at most 0.017.
Values may be sent and summed in bfloat16 or wider, within the bound.
No kernel may reach another device: no remote copies, remote signals or barrier semaphores. Data moves between devices by JAX's collectives and lax.ppermute only.
A program may use at most 192 MiB of HBM per device.

v0:
```python
import functools
import math

import jax
import jax.numpy as jnp
from jax import lax
from jax.experimental import pallas as pl
from jax.experimental.pallas import tpu as pltpu
from jax.sharding import PartitionSpec as P

TICKS = 4
ROWS = 16
COLS = 32
PIX = ROWS * COLS
CH = 256
DP = 8
COST = 2 * 512 * 9 * 256 * 256
FOLD_COST = 16
SHARE = CH // DP
BF = jnp.bfloat16
F32 = jnp.float32
NT = (((1,), (1,)), ((), ()))

PAIRS = {
    "a": [(d, (d & 4) + ((d & 3) ^ 1)) for d in range(DP)],
    "b": [(d, (d & 4) + 3 - (d & 3)) for d in range(DP)],
    "y": [(d, d ^ 4) for d in range(DP)],
}
ORDERS = ("aby", "bya", "yab")

VM = pl.BlockSpec(memory_space=pltpu.VMEM)
SM = pl.BlockSpec(memory_space=pltpu.SMEM)
HB = pl.BlockSpec(memory_space=pltpu.HBM)
FIELD = jax.ShapeDtypeStruct((PIX, CH), BF)
SUMS = jax.ShapeDtypeStruct((9, CH, CH), F32)
WINDOWS = pltpu.VMEM((3, PIX + 2 * COLS, CH), BF)


def half_of(role):
    odd = lax.axis_index("section") & 1
    return odd if role == 0 else 1 - odd


def call(kernel, name, given, outs, specs=None, scratch=(), mib=8, aliases={}, ops=1):
    return pl.pallas_call(
        kernel,
        out_shape=outs,
        in_specs=specs or [VM] * len(given),
        out_specs=jax.tree.map(lambda _: VM, outs),
        scratch_shapes=list(scratch),
        input_output_aliases=aliases,
        compiler_params=pltpu.CompilerParams(vmem_limit_bytes=mib << 20),
        cost_estimate=pl.CostEstimate(flops=ops * COST, bytes_accessed=1024, transcendentals=0),
        name=name,
    )(*given)


def clear_edges(win):
    edge = jnp.zeros((3, COLS, CH), BF)
    win[:, 0:COLS, :] = edge
    win[:, COLS + PIX : 2 * COLS + PIX, :] = edge


def fill_windows(win, field):
    clear_edges(win)
    col = lax.broadcasted_iota(jnp.int32, field.shape, 0) & (COLS - 1)
    win[0, COLS : COLS + PIX, :] = jnp.where(col == 0, 0.0, pltpu.roll(field, 1, 0)).astype(BF)
    win[1, COLS : COLS + PIX, :] = field.astype(BF)
    win[2, COLS : COLS + PIX, :] = jnp.where(col == COLS - 1, 0.0, pltpu.roll(field, PIX - 1, 0)).astype(BF)


def tap_of(win, k):
    dy, dx = divmod(k, 3)
    return win[dx, dy * COLS : dy * COLS + PIX, :]


def conv(win, taps, base):
    total = None
    for k in range(9):
        term = lax.dot_general(tap_of(win, k), taps[base + 8 - k], NT, preferred_element_type=F32)
        total = term if total is None else total + term
    return total


def slot_of(table, role, tick):
    half = half_of(role)
    column = half * lax.axis_size("section") + lax.axis_index("section")
    place = lax.broadcasted_iota(jnp.int32, table.shape, 1) == column
    row = lax.broadcasted_iota(jnp.int32, table.shape, 0) == tick
    return half * 4 + jnp.sum(jnp.where(place & row, table[...], 0))


def add_up(role, tick, got, other, objective):
    total = got[...].astype(F32)
    encoder = half_of(role) == 0
    total = total + jnp.where(encoder, other[...].astype(F32), 0.0)
    if role == 1:
        first = lax.axis_index("section") == 0
        total = jnp.where(first, objective[tick - 1].astype(F32), total)
    return total


def early_of_kernel(role, mask, taps, g2, g1_out, win):
    fill_windows(win, g2[...].astype(F32))
    g1_out[...] = jnp.where(mask[...] > 0, conv(win, taps, 18 * half_of(role) + 9), 0.0).astype(BF)


def early_kernel(role, tick, table, pre1, pre2, taps, *refs):
    given = refs[:-3]
    g2_out, g1_out, win = refs[-3:]
    slot = slot_of(table, role, tick)
    g2 = add_up(role, tick, *given, *([None] * (3 - len(given))))
    g2 = jnp.where(pre2[slot] > 0, g2, 0.0)
    g2_out[...] = g2.astype(BF)
    fill_windows(win, g2)
    g1_out[...] = jnp.where(pre1[slot] > 0, conv(win, taps, 18 * half_of(role) + 9), 0.0).astype(BF)


def late_kernel(role, taps, g1, out, win):
    fill_windows(win, g1[...].astype(F32))
    out[...] = conv(win, taps, 18 * half_of(role)).astype(BF)


def tap_grads(win, x, field):
    fill_windows(win, field)
    xt = x.T
    for k in range(9):
        yield k, jnp.dot(xt, tap_of(win, 8 - k), preferred_element_type=F32)


def left_side(which, saved, slot):
    x = saved[slot]
    return jnp.maximum(x, jnp.zeros((), BF)) if which else x


def wgrad_kernel(which, role, tick, table, saved, field, *refs):
    old = None if tick == 0 else refs[0]
    new, win = refs[-2:]
    x = left_side(which, saved, slot_of(table, role, tick))
    for k, term in tap_grads(win, x, field[...].astype(F32)):
        new[k] = term if old is None else old[k] + term


def replica_at(order, r):
    me = lax.axis_index("dp")
    bit = {order[i]: (r >> (2 - i)) & 1 for i in range(3)}
    y = (me >> 2) & 1
    z = me & 3
    beta = (z >> 1) & 1
    alpha = (z & 1) ^ beta
    alpha = alpha ^ bit["a"]
    beta = beta ^ bit["b"]
    return (y ^ bit["y"]) * 4 + 2 * beta + (alpha ^ beta)


def put_shares(staged, k, sends, keeps, role):
    o, at = divmod(k, 3)
    for r in range(DP):
        row = pl.multiple_of(replica_at(ORDERS[o], r) * SHARE, SHARE)
        share = staged[k, pl.ds(row, SHARE), :].astype(BF)
        if r >= 4:
            sends[o][r - 4, role, at] = share
        else:
            keeps[o][r, role, at] = share


def last_two_kernel(table, pre1, pre2, objective, *refs):
    given, olds = refs[:4], refs[4:6]
    sends, keeps, g2s = refs[6:9], refs[9:12], refs[12:14]
    wins, staged = refs[14:16], refs[16:18]
    tick = TICKS - 1
    for role in range(2):
        slot = slot_of(table, role, tick)
        g2 = add_up(role, tick, given[role], given[3 - role], objective)
        g2 = jnp.where(pre2[slot] > 0, g2, 0.0)
        g2s[role][...] = g2.astype(BF)
        x = left_side(1, pre1, slot)
        for k, term in tap_grads(wins[role], x, g2):
            staged[role][k] = olds[role][k] + term
            put_shares(staged[role], k, sends, keeps, role)


def last_early_kernel(role, table, pre1, taps, g2, g1_out, win):
    slot = slot_of(table, role, TICKS - 1)
    fill_windows(win, g2[...].astype(F32))
    g1_out[...] = jnp.where(pre1[slot] > 0, conv(win, taps, 18 * half_of(role) + 9), 0.0).astype(BF)


def last_one_kernel(table, entries, *refs):
    g1s, olds = refs[:2], refs[2:4]
    sends, keeps = refs[4:7], refs[7:10]
    wins, staged = refs[10:12], refs[12:14]
    for role in range(2):
        x = left_side(0, entries, slot_of(table, role, TICKS - 1))
        for k, term in tap_grads(wins[role], x, g1s[role][...].astype(F32)):
            staged[role][k] = olds[role][k] + term
            put_shares(staged[role], k, sends, keeps, role)


def last_late_kernel(taps, g1_zero, g1_one, out, *wins):
    for role in range(2):
        half = half_of(role)
        fill_windows(wins[role], (g1_zero, g1_one)[role][...].astype(F32))
        out[half] = conv(wins[role], taps, 18 * half).astype(BF)


def fold_in(keep, got, send, left):
    half = keep.shape[0] // 2
    total = keep[...].astype(F32) + got[...].astype(F32)
    left[...] = total[:half].astype(BF)
    send[...] = total[half:].astype(BF)


def fold_two_kernel(*refs):
    for o in range(3):
        keep, got, send, left = refs[o::3]
        fold_in(keep, got, send.at[:, 1], left.at[:, 1])


def fold_one_kernel(keep, got, old_send, old_left, send, left):
    del old_send, old_left
    fold_in(keep, got, send.at[:, 0], left.at[:, 0])


def finish_kernel(scale, *refs):
    out = refs[-1]
    for o in range(3):
        keep, got = refs[2 * o : 2 * o + 2]
        total = keep[0].astype(F32) + got[0].astype(F32)
        for role in range(2):
            half = half_of(role)
            for piece in range(2):
                out[half, piece, 3 * o : 3 * o + 3] = total[piece, role] * scale


def relay(block, role):
    levels = lax.axis_size("section")
    pairs = [(i, i + 1) for i in range(1 - role, levels - 1, 2)]
    return lax.ppermute(block, "section", pairs + [(b, a) for a, b in pairs])


def exchange(block, step):
    return lax.ppermute(block, "dp", PAIRS[step])


def on_device(
    pending_adjoints,
    objective_adjoints,
    kept_block_entries,
    kept_early_presums,
    kept_later_presums,
    filter_taps,
    slot_timetable,
):
    table = slot_timetable
    entries = kept_block_entries.reshape(8, PIX, CH)
    pre1 = kept_early_presums.reshape(8, PIX, CH)
    pre2 = kept_later_presums.reshape(8, PIX, CH)
    taps = filter_taps.reshape(36, CH, CH)
    pending = pending_adjoints.reshape(2, PIX, CH)
    objective = objective_adjoints.reshape(TICKS - 1, PIX, CH)
    windows = [WINDOWS]

    sums1, sums2 = [(), ()], [(), ()]
    gots = outs = None
    for tick in range(TICKS - 1):
        g2s, g1s, new_outs, new_gots = [], [], [], []
        for role in range(2):
            if tick == 0:
                half = half_of(role)
                slot = 4 * half + table[0, half * lax.axis_size("section") + lax.axis_index("section")]
                field = lax.dynamic_index_in_dim(pending, half, 0, keepdims=False)
                g2 = jnp.where(lax.dynamic_index_in_dim(pre2, slot, 0, keepdims=False) > 0, field, jnp.zeros((), BF))
                mask = lax.dynamic_index_in_dim(pre1, slot, 0, keepdims=False)
                g1 = call(
                    functools.partial(early_of_kernel, role),
                    f"early_{role}_0",
                    (mask, taps, g2),
                    FIELD,
                    scratch=windows,
                )
            else:
                given = (gots[1 - role], outs[1 - role]) + ((objective,) if role else ())
                g2, g1 = call(
                    functools.partial(early_kernel, role, tick),
                    f"early_{role}_{tick}",
                    (table, pre1, pre2, taps, *given),
                    (FIELD, FIELD),
                    scratch=windows,
                )
            out = call(functools.partial(late_kernel, role), f"late_{role}_{tick}", (taps, g1), FIELD, scratch=windows)
            g2s.append(g2)
            g1s.append(g1)
            new_outs.append(out)
            new_gots.append(relay(out, role))
        gots, outs = new_gots, new_outs
        for role in range(2):
            for which, saved, fields, sums in ((1, pre1, g2s, sums2), (0, entries, g1s, sums1)):
                new = call(
                    functools.partial(wgrad_kernel, which, role, tick),
                    f"wgrad{which + 1}_{role}_{tick}",
                    (table, saved, fields[role], *sums[role]),
                    SUMS,
                    scratch=windows,
                    aliases={3: 0} if sums[role] else {},
                )
                sums[role] = (new,)

    part = jax.ShapeDtypeStruct((4, 2, 3, SHARE, CH), BF)
    staged = [pltpu.VMEM((9, CH, CH), F32)] * 2
    res = call(
        last_two_kernel,
        "last_two",
        (table, pre1, pre2, objective, gots[1], gots[0], *outs, *sums2[0], *sums2[1]),
        (part,) * 6 + (FIELD,) * 2,
        scratch=windows * 2 + staged,
        mib=16,
        ops=2,
    )
    keeps2, g2s = res[3:6], res[6:8]
    gots2 = [exchange(res[o], ORDERS[o][0]) for o in range(3)]
    g1s = [
        call(
            functools.partial(last_early_kernel, role),
            f"early_{role}_{TICKS - 1}",
            (table, pre1, taps, g2s[role]),
            FIELD,
            scratch=windows,
        )
        for role in range(2)
    ]
    res = call(
        last_one_kernel,
        "last_one",
        (table, entries, *g1s, *sums1[0], *sums1[1]),
        (part,) * 6,
        scratch=windows * 2 + staged,
        mib=16,
        ops=2,
    )
    keeps1 = res[3:6]
    gots1 = [exchange(res[o], ORDERS[o][0]) for o in range(3)]
    final = call(
        last_late_kernel,
        f"late_{TICKS - 1}",
        (taps, *g1s),
        jax.ShapeDtypeStruct((2, PIX, CH), BF),
        scratch=windows * 2,
        ops=2,
    )

    parts = []
    part2 = jax.ShapeDtypeStruct((2, 2, 2, 3, SHARE, CH), BF)
    part3 = jax.ShapeDtypeStruct((1, 2, 2, 3, SHARE, CH), BF)
    begun = call(fold_two_kernel, "fold_two", (*keeps2, *gots2), (part2,) * 6, ops=FOLD_COST)
    for o in range(3):
        send, keep = call(
            fold_one_kernel,
            f"fold_one_{o}",
            (keeps1[o], gots1[o], begun[o], begun[3 + o]),
            (part2, part2),
            aliases={2: 0, 3: 1},
        )
        got = exchange(send, ORDERS[o][1])
        send, keep = call(fold_in, f"fold_last_{o}", (keep, got), (part3, part3))
        parts += [keep, exchange(send, ORDERS[o][2])]
    scale = 1.0 / math.sqrt(TICKS * DP * PIX)
    grads = call(
        functools.partial(finish_kernel, scale),
        "finish",
        tuple(parts),
        jax.ShapeDtypeStruct((2, 2, 9, SHARE, CH), F32),
    )
    return (
        final.reshape(2, 1, 1, ROWS, COLS, CH),
        grads.reshape(2, 1, 2, 9, SHARE, CH),
    )


def solution(mesh):
    placed = (
        P(None, "section", "dp", None, None, None),
        P(None, "dp", None, None, None),
        P(None, "section", None, "dp", None, None, None),
        P(None, "section", None, "dp", None, None, None),
        P(None, "section", None, "dp", None, None, None),
        P(None, "section", None, None, None, None),
        P(),
    )
    return jax.shard_map(
        on_device,
        mesh=mesh,
        in_specs=placed,
        out_specs=(
            P(None, "section", "dp", None, None, None),
            P(None, "section", None, None, "dp", None),
        ),
        check_vma=False,
    )
```

profile of v0, /device:TPU:8, one launch (start us, length us, event | category | flops | bytes accessed | tf_op | source)
XLA Modules:
  0.0 95.8 jit_solution(9673342450861614420)
XLA Ops:
  0.6 1.3 %constant_dynamic-slice_fusion = (s32[1,1]{1,0:T(1,128)}, s32[1,1]{1,0:T(1,128)}) fusion(s32[4,32]{1,0:T(4,128)} %table.39, s32[]{:T(128)S(6)} %select_n.38, s32[]{:T(128)S(6)} %select_n.33), kind=kLoop, calls=%fused_computation.6 | loop fusion | bytes 24 | tf_op jit(solution)/shard_map/dynamic_slice | solution.py:271
  3.3 1.4 %fusion.1 = (bf16[512,256]{1,0:T(8,128)(2,1)S(1)}, bf16[512,256]{1,0:T(8,128)(2,1)S(1)}, bf16[512,256]{1,0:T(8,128)(2,1)S(1)}, bf16[512,256]{1,0:T(8,128)(2,1)S(1)}) fusion(bf16[2,512,256]{2,1,0:T(8,128)(2,1)} %bitcast.68, s32[]{:T(128)S(6)} %select_n.40, bf16[8,512,256]{2,1,0:T(8,128)(2,1)} %bitcast.58, s32[]{:T(128)S(6)} %select_n.39, s32[]{:T(128)S(6)} %select_n.35, ...), kind=kLoop, calls=%fused_computation.3 | loop fusion | flops 524288 | bytes 2621456 | tf_op jit(solution)/shard_map/jit(_where)/select_n | solution.py:273
  4.8 2.3 %copy-done = bf16[2,1,2,9,256,256]{5,4,3,2,1,0:T(8,128)(2,1)S(1)} copy-done((bf16[2,1,2,9,256,256]{5,4,3,2,1,0:T(8,128)(2,1)S(1)}, bf16[2,1,2,9,256,256]{5,4,3,2,1,0:T(8,128)(2,1)}, u32[]{:S(2)}) %copy-start) | copy-done | bytes 4718616
  7.9 0.8 late_0_0.1.refs_1_
  8.8 4.1 %collective-permute-start.3 = (bf16[512,256]{1,0:T(8,128)(2,1)S(1)}, bf16[512,256]{1,0:T(8,128)(2,1)S(1)}, u32[]{:S(2)}, u32[]{:S(2)}) collective-permute-start(bf16[512,256]{1,0:T(8,128)(2,1)S(1)} %late_0_0.1.refs_1_), channel_id=1, source_target_pairs={{8,16},{24,32},{40,48},{56,64},{72,80},{88,96},{104,112},{16,8},{3... | collective-permute-start | bytes 786440 | tf_op jit(solution)/shard_map/ppermute | solution.py:239
  12.9 0.8 early_1_0.1.g1.field
  13.7 0.8 late_1_0.1.refs_1_
  15.3 1.0 %wgrad2_1_0.1.refs_0_ = f32[9,256,256]{2,1,0:T(8,128)S(1)} custom-call(s32[4,32]{1,0:T(4,128)S(1)} %copy-done.6, bf16[8,512,256]{2,1,0:T(8,128)(2,1)S(1)} %bitcast.38, bf16[512,256]{1,0:T(8,128)(2,1)S(1)} %get-tuple-element.85.g2.field), custom_call_target="tpu_custom_call" | custom-call | flops 603979776 | bytes 1024 | tf_op jit(solution)/shard_map/wgrad2_1_0/pallas_call | solution.py:45
  16.3 2.4 %collective-permute-done.3.refs_0_ = bf16[512,256]{1,0:T(8,128)(2,1)S(1)} collective-permute-done((bf16[512,256]{1,0:T(8,128)(2,1)S(1)}, bf16[512,256]{1,0:T(8,128)(2,1)S(1)}, u32[]{:S(2)}, u32[]{:S(2)}) %collective-permute-start.3) | collective-permute-done | bytes 262176 | tf_op jit(solution)/shard_map/ppermute | solution.py:239
  18.7 1.0 %early_1_1.1 = (bf16[512,256]{1,0:T(8,128)(2,1)S(1)}, bf16[512,256]{1,0:T(8,128)(2,1)S(1)}) custom-call(s32[4,32]{1,0:T(4,128)S(1)} %copy-done.6, bf16[8,512,256]{2,1,0:T(8,128)(2,1)S(1)} %bitcast.39, bf16[8,512,256]{2,1,0:T(8,128)(2,1)S(1)} %bitcast.59, bf16[36,256,256]{2,1,0:T(8,128)(2,1)S(1)} %bitcast.26, ...), custom_call_target="tpu_custom_call" | custom-call | flops 603979776 | bytes 1024 | tf_op jit(solution)/shard_map/early_1_1/pallas_call | solution.py:45
  20.6 1.0 %early_0_1.1 = (bf16[512,256]{1,0:T(8,128)(2,1)S(1)}, bf16[512,256]{1,0:T(8,128)(2,1)S(1)}) custom-call(s32[4,32]{1,0:T(4,128)S(1)} %copy-done.6, bf16[8,512,256]{2,1,0:T(8,128)(2,1)S(1)} %bitcast.40, bf16[8,512,256]{2,1,0:T(8,128)(2,1)S(1)} %bitcast.60, bf16[36,256,256]{2,1,0:T(8,128)(2,1)S(1)} %bitcast.28, ...), custom_call_target="tpu_custom_call" | custom-call | flops 603979776 | bytes 1024 | tf_op jit(solution)/shard_map/early_0_1/pallas_call | solution.py:45
  22.5 4.1 %collective-permute-start.1 = (bf16[512,256]{1,0:T(8,128)(2,1)S(1)}, bf16[512,256]{1,0:T(8,128)(2,1)S(1)}, u32[]{:S(2)}, u32[]{:S(2)}) collective-permute-start(bf16[512,256]{1,0:T(8,128)(2,1)S(1)} %late_0_1.1.refs_1_), channel_id=1, source_target_pairs={{8,16},{24,32},{40,48},{56,64},{72,80},{88,96},{104,112},{16,8},{3... | collective-permute-start | bytes 786440 | tf_op jit(solution)/shard_map/ppermute | solution.py:239
  26.6 1.0 %wgrad2_0_0.1.refs_0_ = f32[9,256,256]{2,1,0:T(8,128)S(1)} custom-call(s32[4,32]{1,0:T(4,128)S(1)} %copy-done.6, bf16[8,512,256]{2,1,0:T(8,128)(2,1)S(1)} %bitcast.41, bf16[512,256]{1,0:T(8,128)(2,1)S(1)} %get-tuple-element.84.g2.field), custom_call_target="tpu_custom_call" | custom-call | flops 603979776 | bytes 1024 | tf_op jit(solution)/shard_map/wgrad2_0_0/pallas_call | solution.py:45
  27.6 1.0 %wgrad1_0_0.1.refs_0_ = f32[9,256,256]{2,1,0:T(8,128)S(1)} custom-call(s32[4,32]{1,0:T(4,128)S(1)} %copy-done.6, bf16[8,512,256]{2,1,0:T(8,128)(2,1)S(1)} %bitcast.51, bf16[512,256]{1,0:T(8,128)(2,1)S(1)} %early_0_0.1.g1.field), custom_call_target="tpu_custom_call" | custom-call | flops 603979776 | bytes 1024 | tf_op jit(solution)/shard_map/wgrad1_0_0/pallas_call | solution.py:45
  28.6 1.0 %wgrad1_1_0.1.refs_0_ = f32[9,256,256]{2,1,0:T(8,128)S(1)} custom-call(s32[4,32]{1,0:T(4,128)S(1)} %copy-done.6, bf16[8,512,256]{2,1,0:T(8,128)(2,1)S(1)} %bitcast.52, bf16[512,256]{1,0:T(8,128)(2,1)S(1)} %early_1_0.1.g1.field), custom_call_target="tpu_custom_call" | custom-call | flops 603979776 | bytes 1024 | tf_op jit(solution)/shard_map/wgrad1_1_0/pallas_call | solution.py:45
  29.6 1.0 %early_0_2.1 = (bf16[512,256]{1,0:T(8,128)(2,1)S(1)}, bf16[512,256]{1,0:T(8,128)(2,1)S(1)}) custom-call(s32[4,32]{1,0:T(4,128)S(1)} %copy-done.6, bf16[8,512,256]{2,1,0:T(8,128)(2,1)S(1)} %bitcast.42, bf16[8,512,256]{2,1,0:T(8,128)(2,1)S(1)} %bitcast.61, bf16[36,256,256]{2,1,0:T(8,128)(2,1)S(1)} %bitcast.30, ...), custom_call_target="tpu_custom_call" | custom-call | flops 603979776 | bytes 1024 | tf_op jit(solution)/shard_map/early_0_2/pallas_call | solution.py:45
  31.4 3.9 %collective-permute-start.5 = (bf16[512,256]{1,0:T(8,128)(2,1)S(1)}, bf16[512,256]{1,0:T(8,128)(2,1)S(1)}, u32[]{:S(2)}, u32[]{:S(2)}) collective-permute-start(bf16[512,256]{1,0:T(8,128)(2,1)S(1)} %late_0_2.1.refs_2_), channel_id=1, source_target_pairs={{8,16},{24,32},{40,48},{56,64},{72,80},{88,96},{104,112},{16,8},{3... | collective-permute-start | bytes 786440 | tf_op jit(solution)/shard_map/ppermute | solution.py:239
  35.3 1.0 %early_1_2.1 = (bf16[512,256]{1,0:T(8,128)(2,1)S(1)}, bf16[512,256]{1,0:T(8,128)(2,1)S(1)}) custom-call(s32[4,32]{1,0:T(4,128)S(1)} %copy-done.6, bf16[8,512,256]{2,1,0:T(8,128)(2,1)S(1)} %bitcast.43, bf16[8,512,256]{2,1,0:T(8,128)(2,1)S(1)} %bitcast.62, bf16[36,256,256]{2,1,0:T(8,128)(2,1)S(1)} %bitcast.32, ...), custom_call_target="tpu_custom_call" | custom-call | flops 603979776 | bytes 1024 | tf_op jit(solution)/shard_map/early_1_2/pallas_call | solution.py:45
  36.3 0.8 late_1_2.1.refs_3_
  37.2 1.1 %wgrad1_0_1.1.refs_0_ = f32[9,256,256]{2,1,0:T(8,128)S(1)} custom-call(s32[4,32]{1,0:T(4,128)S(1)} %copy-done.6, bf16[8,512,256]{2,1,0:T(8,128)(2,1)S(1)} %bitcast.53, bf16[512,256]{1,0:T(8,128)(2,1)S(1)} %get-tuple-element.42.g1.field, f32[9,256,256]{2,1,0:T(8,128)S(1)} %wgrad1_0_0.1.refs_0_), custom_call_target="tpu_custom_call", output_to_operand_aliasing={{}: (3, {})} | custom-call | flops 603979776 | bytes 1024 | tf_op jit(solution)/shard_map/wgrad1_0_1/pallas_call | solution.py:45
  38.3 1.1 %wgrad2_1_1.1.refs_0_ = f32[9,256,256]{2,1,0:T(8,128)S(1)} custom-call(s32[4,32]{1,0:T(4,128)S(1)} %copy-done.6, bf16[8,512,256]{2,1,0:T(8,128)(2,1)S(1)} %bitcast.44, bf16[512,256]{1,0:T(8,128)(2,1)S(1)} %get-tuple-element.49.field, f32[9,256,256]{2,1,0:T(8,128)S(1)} %wgrad2_1_0.1.refs_0_), custom_call_target="tpu_custom_call", output_to_operand_aliasing={{}: (3, {})} | custom-call | flops 603979776 | bytes 1024 | tf_op jit(solution)/shard_map/wgrad2_1_1/pallas_call | solution.py:45
  39.4 1.1 %wgrad2_0_1.1.refs_0_ = f32[9,256,256]{2,1,0:T(8,128)S(1)} custom-call(s32[4,32]{1,0:T(4,128)S(1)} %copy-done.6, bf16[8,512,256]{2,1,0:T(8,128)(2,1)S(1)} %bitcast.45, bf16[512,256]{1,0:T(8,128)(2,1)S(1)} %get-tuple-element.47.field, f32[9,256,256]{2,1,0:T(8,128)S(1)} %wgrad2_0_0.1.refs_0_), custom_call_target="tpu_custom_call", output_to_operand_aliasing={{}: (3, {})} | custom-call | flops 603979776 | bytes 1024 | tf_op jit(solution)/shard_map/wgrad2_0_1/pallas_call | solution.py:45
  40.4 1.1 %wgrad2_1_2.1.refs_5_ = f32[9,256,256]{2,1,0:T(8,128)S(1)} custom-call(s32[4,32]{1,0:T(4,128)S(1)} %copy-done.6, bf16[8,512,256]{2,1,0:T(8,128)(2,1)S(1)} %bitcast.46, bf16[512,256]{1,0:T(8,128)(2,1)S(1)} %get-tuple-element.48.field, f32[9,256,256]{2,1,0:T(8,128)S(1)} %wgrad2_1_1.1.refs_0_), custom_call_target="tpu_custom_call", output_to_operand_aliasing={{}: (3, {})} | custom-call | flops 603979776 | bytes 1024 | tf_op jit(solution)/shard_map/wgrad2_1_2/pallas_call | solution.py:45
  41.5 1.1 %wgrad2_0_2.1.refs_4_ = f32[9,256,256]{2,1,0:T(8,128)S(1)} custom-call(s32[4,32]{1,0:T(4,128)S(1)} %copy-done.6, bf16[8,512,256]{2,1,0:T(8,128)(2,1)S(1)} %bitcast.47, bf16[512,256]{1,0:T(8,128)(2,1)S(1)} %get-tuple-element.46.field, f32[9,256,256]{2,1,0:T(8,128)S(1)} %wgrad2_0_1.1.refs_0_), custom_call_target="tpu_custom_call", output_to_operand_aliasing={{}: (3, {})} | custom-call | flops 603979776 | bytes 1024 | tf_op jit(solution)/shard_map/wgrad2_0_2/pallas_call | solution.py:45
  42.6 2.4 %last_two.1 = (bf16[4,2,3,32,256]{4,3,2,1,0:T(8,128)(2,1)S(1)}, bf16[4,2,3,32,256]{4,3,2,1,0:T(8,128)(2,1)S(1)}, bf16[4,2,3,32,256]{4,3,2,1,0:T(8,128)(2,1)S(1)}...) custom-call(s32[4,32]{1,0:T(4,128)S(1)} %copy-done.6, ...), custom_call_target="tpu_custom_call" | custom-call | flops 1207959552 | bytes 1024 | tf_op jit(solution)/shard_map/last_two/pallas_call | solution.py:45
  45.0 2.0 %collective-permute-start.7 = (bf16[4,2,3,32,256]{4,3,2,1,0:T(8,128)(2,1)S(1)}, bf16[4,2,3,32,256]{4,3,2,1,0:T(8,128)(2,1)S(1)}, u32[]{:S(2)}, u32[]{:S(2)}) collective-permute-start(bf16[4,2,3,32,256]{4,3,2,1,0:T(8,128)(2,1)S(1)} %get-tuple-element.57), channel_id=1, source_target_pairs={{0,1},{1,0},{2,3},{3,2},{4,5},{5,4},{6,7},{7,6},{8,9},{9,8},{10,11... | collective-permute-start | bytes 1179656 | tf_op jit(solution)/shard_map/ppermute | solution.py:243
  47.0 2.5 %collective-permute-start.8 = (bf16[4,2,3,32,256]{4,3,2,1,0:T(8,128)(2,1)S(1)}, bf16[4,2,3,32,256]{4,3,2,1,0:T(8,128)(2,1)S(1)}, u32[]{:S(2)}, u32[]{:S(2)}) collective-permute-start(bf16[4,2,3,32,256]{4,3,2,1,0:T(8,128)(2,1)S(1)} %get-tuple-element.58), channel_id=1, source_target_pairs={{0,3},{1,2},{2,1},{3,0},{4,7},{5,6},{6,5},{7,4},{8,11},{9,10},{10,... | collective-permute-start | bytes 1179656 | tf_op jit(solution)/shard_map/ppermute | solution.py:243
  49.5 2.3 %collective-permute-start.9 = (bf16[4,2,3,32,256]{4,3,2,1,0:T(8,128)(2,1)S(1)}, bf16[4,2,3,32,256]{4,3,2,1,0:T(8,128)(2,1)S(1)}, u32[]{:S(2)}, u32[]{:S(2)}) collective-permute-start(bf16[4,2,3,32,256]{4,3,2,1,0:T(8,128)(2,1)S(1)} %get-tuple-element.59), channel_id=1, source_target_pairs={{0,4},{1,5},{2,6},{3,7},{4,0},{5,1},{6,2},{7,3},{8,12},{9,13},{10,... | collective-permute-start | bytes 1179656 | tf_op jit(solution)/shard_map/ppermute | solution.py:243
  51.8 1.0 %wgrad1_1_1.1.refs_0_ = f32[9,256,256]{2,1,0:T(8,128)S(1)} custom-call(s32[4,32]{1,0:T(4,128)S(1)} %copy-done.6, bf16[8,512,256]{2,1,0:T(8,128)(2,1)S(1)} %bitcast.54, bf16[512,256]{1,0:T(8,128)(2,1)S(1)} %get-tuple-element.44.g1.field, f32[9,256,256]{2,1,0:T(8,128)S(1)} %wgrad1_1_0.1.refs_0_), custom_call_target="tpu_custom_call", output_to_operand_aliasing={{}: (3, {})} | custom-call | flops 603979776 | bytes 1024 | tf_op jit(solution)/shard_map/wgrad1_1_1/pallas_call | solution.py:45
  52.8 1.0 %wgrad1_0_2.1.refs_2_ = f32[9,256,256]{2,1,0:T(8,128)S(1)} custom-call(s32[4,32]{1,0:T(4,128)S(1)} %copy-done.6, bf16[8,512,256]{2,1,0:T(8,128)(2,1)S(1)} %bitcast.55, bf16[512,256]{1,0:T(8,128)(2,1)S(1)} %get-tuple-element.45.g1.field, f32[9,256,256]{2,1,0:T(8,128)S(1)} %wgrad1_0_1.1.refs_0_), custom_call_target="tpu_custom_call", output_to_operand_aliasing={{}: (3, {})} | custom-call | flops 603979776 | bytes 1024 | tf_op jit(solution)/shard_map/wgrad1_0_2/pallas_call | solution.py:45
  53.9 1.0 %wgrad1_1_2.1.refs_3_ = f32[9,256,256]{2,1,0:T(8,128)S(1)} custom-call(s32[4,32]{1,0:T(4,128)S(1)} %copy-done.6, bf16[8,512,256]{2,1,0:T(8,128)(2,1)S(1)} %bitcast.56, bf16[512,256]{1,0:T(8,128)(2,1)S(1)} %get-tuple-element.43.g1.field, f32[9,256,256]{2,1,0:T(8,128)S(1)} %wgrad1_1_1.1.refs_0_), custom_call_target="tpu_custom_call", output_to_operand_aliasing={{}: (3, {})} | custom-call | flops 603979776 | bytes 1024 | tf_op jit(solution)/shard_map/wgrad1_1_2/pallas_call | solution.py:45
  54.9 0.8 early_0_3.1.g1_zero.refs_0_
  55.8 0.8 early_1_3.1.g1_one.refs_1_
  56.6 2.1 %last_one.1 = (bf16[4,2,3,32,256]{4,3,2,1,0:T(8,128)(2,1)S(1)}, bf16[4,2,3,32,256]{4,3,2,1,0:T(8,128)(2,1)S(1)}, bf16[4,2,3,32,256]{4,3,2,1,0:T(8,128)(2,1)S(1)}...) custom-call(s32[4,32]{1,0:T(4,128)S(1)} %copy-done.6, ...), custom_call_target="tpu_custom_call" | custom-call | flops 1207959552 | bytes 1024 | tf_op jit(solution)/shard_map/last_one/pallas_call | solution.py:45
  58.7 1.3 %collective-permute-start.15 = (bf16[4,2,3,32,256]{4,3,2,1,0:T(8,128)(2,1)S(1)}, bf16[4,2,3,32,256]{4,3,2,1,0:T(8,128)(2,1)S(1)}, u32[]{:S(2)}, u32[]{:S(2)}) collective-permute-start(bf16[4,2,3,32,256]{4,3,2,1,0:T(8,128)(2,1)S(1)} %get-tuple-element.75), channel_id=1, source_target_pairs={{0,4},{1,5},{2,6},{3,7},{4,0},{5,1},{6,2},{7,3},{8,12},{9,13},{10,... | collective-permute-start | bytes 1179656 | tf_op jit(solution)/shard_map/ppermute | solution.py:243
  61.1 0.9 collective-permute-done.9.refs_5_
  62.2 8.8 %collective-permute-done.15.got = bf16[4,2,3,32,256]{4,3,2,1,0:T(8,128)(2,1)S(1)} collective-permute-done((bf16[4,2,3,32,256]{4,3,2,1,0:T(8,128)(2,1)S(1)}, bf16[4,2,3,32,256]{4,3,2,1,0:T(8,128)(2,1)S(1)}, u32[]{:S(2)}, u32[]{:S(2)}) %collective-permute-start.15) | collective-permute-done | bytes 393248 | tf_op jit(solution)/shard_map/ppermute | solution.py:243
  71.1 1.1 %collective-permute-start.16 = (bf16[2,2,2,3,32,256]{5,4,3,2,1,0:T(8,128)(2,1)S(1)}, bf16[2,2,2,3,32,256]{5,4,3,2,1,0:T(8,128)(2,1)S(1)}, u32[]{:S(2)}, u32[]{:S(2)}) collective-permute-start(bf16[2,2,2,3,32,256]{5,4,3,2,1,0:T(8,128)(2,1)S(1)} %get-tuple-element.79), channel_id=1, source_target_pairs={{0,1},{1,0},{2,3},{3,2},{4,5},{5,4},{6,7},{7,6},{8,9},{9,8},{10,11... | collective-permute-start | bytes 1179656 | tf_op jit(solution)/shard_map/ppermute | solution.py:243
  72.3 1.8 %collective-permute-start.13 = (bf16[2,2,2,3,32,256]{5,4,3,2,1,0:T(8,128)(2,1)S(1)}, bf16[2,2,2,3,32,256]{5,4,3,2,1,0:T(8,128)(2,1)S(1)}, u32[]{:S(2)}, u32[]{:S(2)}) collective-permute-start(bf16[2,2,2,3,32,256]{5,4,3,2,1,0:T(8,128)(2,1)S(1)} %get-tuple-element.71), channel_id=1, source_target_pairs={{0,4},{1,5},{2,6},{3,7},{4,0},{5,1},{6,2},{7,3},{8,12},{9,13},{10,... | collective-permute-start | bytes 1179656 | tf_op jit(solution)/shard_map/ppermute | solution.py:243
  74.2 0.9 collective-permute-start.10
  75.1 5.8 %collective-permute-done.16.got = bf16[2,2,2,3,32,256]{5,4,3,2,1,0:T(8,128)(2,1)S(1)} collective-permute-done((bf16[2,2,2,3,32,256]{5,4,3,2,1,0:T(8,128)(2,1)S(1)}, bf16[2,2,2,3,32,256]{5,4,3,2,1,0:T(8,128)(2,1)S(1)}, u32[]{:S(2)}, u32[]{:S(2)}) %collective-permute-start.16) | collective-permute-done | bytes 393248 | tf_op jit(solution)/shard_map/ppermute | solution.py:243
  81.0 1.0 %collective-permute-start.17 = (bf16[1,2,2,3,32,256]{5,4,3,2,1,0:T(8,128)(2,1)S(1)}, bf16[1,2,2,3,32,256]{5,4,3,2,1,0:T(8,128)(2,1)S(1)}, u32[]{:S(2)}, u32[]{:S(2)}) collective-permute-start(bf16[1,2,2,3,32,256]{5,4,3,2,1,0:T(8,128)(2,1)S(1)} %get-tuple-element.81), channel_id=1, source_target_pairs={{0,3},{1,2},{2,1},{3,0},{4,7},{5,6},{6,5},{7,4},{8,11},{9,10},{10,... | collective-permute-start | bytes 589832 | tf_op jit(solution)/shard_map/ppermute | solution.py:243
  82.0 1.4 %collective-permute-done.13.got = bf16[2,2,2,3,32,256]{5,4,3,2,1,0:T(8,128)(2,1)S(1)} collective-permute-done((bf16[2,2,2,3,32,256]{5,4,3,2,1,0:T(8,128)(2,1)S(1)}, bf16[2,2,2,3,32,256]{5,4,3,2,1,0:T(8,128)(2,1)S(1)}, u32[]{:S(2)}, u32[]{:S(2)}) %collective-permute-start.13) | collective-permute-done | bytes 393248 | tf_op jit(solution)/shard_map/ppermute | solution.py:243
  83.5 1.1 %collective-permute-start.14 = (bf16[1,2,2,3,32,256]{5,4,3,2,1,0:T(8,128)(2,1)S(1)}, bf16[1,2,2,3,32,256]{5,4,3,2,1,0:T(8,128)(2,1)S(1)}, u32[]{:S(2)}, u32[]{:S(2)}) collective-permute-start(bf16[1,2,2,3,32,256]{5,4,3,2,1,0:T(8,128)(2,1)S(1)} %get-tuple-element.73), channel_id=1, source_target_pairs={{0,1},{1,0},{2,3},{3,2},{4,5},{5,4},{6,7},{7,6},{8,9},{9,8},{10,11... | collective-permute-start | bytes 589832 | tf_op jit(solution)/shard_map/ppermute | solution.py:243
  84.5 2.7 %collective-permute-done.10.got = bf16[2,2,2,3,32,256]{5,4,3,2,1,0:T(8,128)(2,1)S(1)} collective-permute-done((bf16[2,2,2,3,32,256]{5,4,3,2,1,0:T(8,128)(2,1)S(1)}, bf16[2,2,2,3,32,256]{5,4,3,2,1,0:T(8,128)(2,1)S(1)}, u32[]{:S(2)}, u32[]{:S(2)}) %collective-permute-start.10) | collective-permute-done | bytes 393248 | tf_op jit(solution)/shard_map/ppermute | solution.py:243
  87.8 2.2 %late_3.1 = bf16[2,512,256]{2,1,0:T(8,128)(2,1)} custom-call(bf16[36,256,256]{2,1,0:T(8,128)(2,1)S(1)} %bitcast.36, bf16[512,256]{1,0:T(8,128)(2,1)S(1)} %early_0_3.1.g1_zero.refs_0_, bf16[512,256]{1,0:T(8,128)(2,1)S(1)} %early_1_3.1.g1_one.refs_1_), custom_call_target="tpu_custom_call" | custom-call | flops 1207959552 | bytes 1024 | tf_op jit(solution)/shard_map/late_3/pallas_call | solution.py:45
  90.0 4.6 %collective-permute-done.11.refs_1_ = bf16[1,2,2,3,32,256]{5,4,3,2,1,0:T(8,128)(2,1)S(1)} collective-permute-done((bf16[1,2,2,3,32,256]{5,4,3,2,1,0:T(8,128)(2,1)S(1)}, bf16[1,2,2,3,32,256]{5,4,3,2,1,0:T(8,128)(2,1)S(1)}, u32[]{:S(2)}, u32[]{:S(2)}) %collective-permute-start.11) | collective-permute-done | bytes 196640 | tf_op jit(solution)/shard_map/ppermute | solution.py:243
  94.6 1.2 %finish.1 = f32[2,2,9,32,256]{4,3,2,1,0:T(8,128)} custom-call(bf16[1,2,2,3,32,256]{5,4,3,2,1,0:T(8,128)(2,1)S(1)} %get-tuple-element.64.refs_0_, bf16[1,2,2,3,32,256]{5,4,3,2,1,0:T(8,128)(2,1)S(1)} %collective-permute-done.11.refs_1_, bf16[1,2,2,3,32,256]{5,4,3,2,1,0:T(8,128)(2,1)S(1)} %get-tuple-element.72.refs_2_, ...), custom_call_target="tpu_custom_call" | custom-call | flops 603979776 | bytes 1024 | tf_op jit(solution)/shard_map/finish/pallas_call | solution.py:45
  (41 shorter events, 6.5 us)
Async XLA Ops:
  4.7 2.3 %copy-start = (bf16[2,1,2,9,256,256]{5,4,3,2,1,0:T(8,128)(2,1)S(1)}, bf16[2,1,2,9,256,256]{5,4,3,2,1,0:T(8,128)(2,1)}, u32[]{:S(2)}) copy-start(bf16[2,1,2,9,256,256]{5,4,3,2,1,0:T(8,128)(2,1)} %param.12) | copy-start | bytes 14155780
  7.9 5.0 %copy-start.1 = (bf16[2,1,2,9,256,256]{5,4,3,2,1,0:T(8,128)(2,1)S(1)}, bf16[2,1,2,9,256,256]{5,4,3,2,1,0:T(8,128)(2,1)}, u32[]{:S(2)}) copy-start(bf16[2,1,2,9,256,256]{5,4,3,2,1,0:T(8,128)(2,1)} %param.12) | copy-start | bytes 14155780
  8.8 9.9 %collective-permute-start.3 = (bf16[512,256]{1,0:T(8,128)(2,1)S(1)}, bf16[512,256]{1,0:T(8,128)(2,1)S(1)}, u32[]{:S(2)}, u32[]{:S(2)}) collective-permute-start(bf16[512,256]{1,0:T(8,128)(2,1)S(1)} %late_0_0.1.refs_1_), channel_id=1, source_target_pairs={{8,16},{24,32},{40,48},{56,64},{72,80},{88,96},{104,112},{16,8},{3... | collective-permute-start | bytes 786440 | tf_op jit(solution)/shard_map/ppermute | solution.py:239
  13.7 1.6 %copy-start.2 = (bf16[2,1,4,1,16,32,256]{6,5,4,3,2,1,0:T(8,128)(2,1)S(1)}, bf16[2,1,4,1,16,32,256]{6,5,4,3,2,1,0:T(8,128)(2,1)}, u32[]{:S(2)}) copy-start(bf16[2,1,4,1,16,32,256]{6,5,4,3,2,1,0:T(8,128)(2,1)} %param.10) | copy-start | bytes 6291460
  13.7 1.6 %copy-start.6 = (s32[4,32]{1,0:T(4,128)S(1)}, s32[4,32]{1,0:T(4,128)}, u32[]{:S(2)}) copy-start(s32[4,32]{1,0:T(4,128)} %table.39) | copy-start | bytes 1540
  14.6 4.1 %copy-start.4 = (bf16[2,1,4,1,16,32,256]{6,5,4,3,2,1,0:T(8,128)(2,1)S(1)}, bf16[2,1,4,1,16,32,256]{6,5,4,3,2,1,0:T(8,128)(2,1)}, u32[]{:S(2)}) copy-start(bf16[2,1,4,1,16,32,256]{6,5,4,3,2,1,0:T(8,128)(2,1)} %param.11) | copy-start | bytes 6291460
  14.6 4.1 %copy-start.5 = (bf16[3,1,16,32,256]{4,3,2,1,0:T(8,128)(2,1)S(1)}, bf16[3,1,16,32,256]{4,3,2,1,0:T(8,128)(2,1)}, u32[]{:S(2)}) copy-start(bf16[3,1,16,32,256]{4,3,2,1,0:T(8,128)(2,1)} %param.8) | copy-start | bytes 2359300
  14.6 6.0 %collective-permute-start = (bf16[512,256]{1,0:T(8,128)(2,1)S(1)}, bf16[512,256]{1,0:T(8,128)(2,1)S(1)}, u32[]{:S(2)}, u32[]{:S(2)}) collective-permute-start(bf16[512,256]{1,0:T(8,128)(2,1)S(1)} %late_1_0.1.refs_1_), channel_id=1, source_target_pairs={{0,8},{16,24},{32,40},{48,56},{64,72},{80,88},{96,104},{112,120},{... | collective-permute-start | bytes 786440 | tf_op jit(solution)/shard_map/ppermute | solution.py:239
  20.5 9.0 %collective-permute-start.4 = (bf16[512,256]{1,0:T(8,128)(2,1)S(1)}, bf16[512,256]{1,0:T(8,128)(2,1)S(1)}, u32[]{:S(2)}, u32[]{:S(2)}) collective-permute-start(bf16[512,256]{1,0:T(8,128)(2,1)S(1)} %late_1_1.1.refs_1_), channel_id=1, source_target_pairs={{0,8},{16,24},{32,40},{48,56},{64,72},{80,88},{96,104},{112,120},{... | collective-permute-start | bytes 786440 | tf_op jit(solution)/shard_map/ppermute | solution.py:239
  22.5 5.1 %copy-start.3 = (bf16[2,1,4,1,16,32,256]{6,5,4,3,2,1,0:T(8,128)(2,1)S(1)}, bf16[2,1,4,1,16,32,256]{6,5,4,3,2,1,0:T(8,128)(2,1)}, u32[]{:S(2)}) copy-start(bf16[2,1,4,1,16,32,256]{6,5,4,3,2,1,0:T(8,128)(2,1)} %param.9) | copy-start | bytes 6291460
  22.5 12.8 %collective-permute-start.1 = (bf16[512,256]{1,0:T(8,128)(2,1)S(1)}, bf16[512,256]{1,0:T(8,128)(2,1)S(1)}, u32[]{:S(2)}, u32[]{:S(2)}) collective-permute-start(bf16[512,256]{1,0:T(8,128)(2,1)S(1)} %late_0_1.1.refs_1_), channel_id=1, source_target_pairs={{8,16},{24,32},{40,48},{56,64},{72,80},{88,96},{104,112},{16,8},{3... | collective-permute-start | bytes 786440 | tf_op jit(solution)/shard_map/ppermute | solution.py:239
  31.4 11.2 %collective-permute-start.5 = (bf16[512,256]{1,0:T(8,128)(2,1)S(1)}, bf16[512,256]{1,0:T(8,128)(2,1)S(1)}, u32[]{:S(2)}, u32[]{:S(2)}) collective-permute-start(bf16[512,256]{1,0:T(8,128)(2,1)S(1)} %late_0_2.1.refs_2_), channel_id=1, source_target_pairs={{8,16},{24,32},{40,48},{56,64},{72,80},{88,96},{104,112},{16,8},{3... | collective-permute-start | bytes 786440 | tf_op jit(solution)/shard_map/ppermute | solution.py:239
  37.2 5.4 %collective-permute-start.2 = (bf16[512,256]{1,0:T(8,128)(2,1)S(1)}, bf16[512,256]{1,0:T(8,128)(2,1)S(1)}, u32[]{:S(2)}, u32[]{:S(2)}) collective-permute-start(bf16[512,256]{1,0:T(8,128)(2,1)S(1)} %late_1_2.1.refs_3_), channel_id=1, source_target_pairs={{0,8},{16,24},{32,40},{48,56},{64,72},{80,88},{96,104},{112,120},{... | collective-permute-start | bytes 786440 | tf_op jit(solution)/shard_map/ppermute | solution.py:239
  45.0 15.8 %collective-permute-start.7 = (bf16[4,2,3,32,256]{4,3,2,1,0:T(8,128)(2,1)S(1)}, bf16[4,2,3,32,256]{4,3,2,1,0:T(8,128)(2,1)S(1)}, u32[]{:S(2)}, u32[]{:S(2)}) collective-permute-start(bf16[4,2,3,32,256]{4,3,2,1,0:T(8,128)(2,1)S(1)} %get-tuple-element.57), channel_id=1, source_target_pairs={{0,1},{1,0},{2,3},{3,2},{4,5},{5,4},{6,7},{7,6},{8,9},{9,8},{10,11... | collective-permute-start | bytes 1179656 | tf_op jit(solution)/shard_map/ppermute | solution.py:243
  47.0 14.1 %collective-permute-start.8 = (bf16[4,2,3,32,256]{4,3,2,1,0:T(8,128)(2,1)S(1)}, bf16[4,2,3,32,256]{4,3,2,1,0:T(8,128)(2,1)S(1)}, u32[]{:S(2)}, u32[]{:S(2)}) collective-permute-start(bf16[4,2,3,32,256]{4,3,2,1,0:T(8,128)(2,1)S(1)} %get-tuple-element.58), channel_id=1, source_target_pairs={{0,3},{1,2},{2,1},{3,0},{4,7},{5,6},{6,5},{7,4},{8,11},{9,10},{10,... | collective-permute-start | bytes 1179656 | tf_op jit(solution)/shard_map/ppermute | solution.py:243
  49.5 12.5 %collective-permute-start.9 = (bf16[4,2,3,32,256]{4,3,2,1,0:T(8,128)(2,1)S(1)}, bf16[4,2,3,32,256]{4,3,2,1,0:T(8,128)(2,1)S(1)}, u32[]{:S(2)}, u32[]{:S(2)}) collective-permute-start(bf16[4,2,3,32,256]{4,3,2,1,0:T(8,128)(2,1)S(1)} %get-tuple-element.59), channel_id=1, source_target_pairs={{0,4},{1,5},{2,6},{3,7},{4,0},{5,1},{6,2},{7,3},{8,12},{9,13},{10,... | collective-permute-start | bytes 1179656 | tf_op jit(solution)/shard_map/ppermute | solution.py:243
  58.7 12.3 %collective-permute-start.15 = (bf16[4,2,3,32,256]{4,3,2,1,0:T(8,128)(2,1)S(1)}, bf16[4,2,3,32,256]{4,3,2,1,0:T(8,128)(2,1)S(1)}, u32[]{:S(2)}, u32[]{:S(2)}) collective-permute-start(bf16[4,2,3,32,256]{4,3,2,1,0:T(8,128)(2,1)S(1)} %get-tuple-element.75), channel_id=1, source_target_pairs={{0,4},{1,5},{2,6},{3,7},{4,0},{5,1},{6,2},{7,3},{8,12},{9,13},{10,... | collective-permute-start | bytes 1179656 | tf_op jit(solution)/shard_map/ppermute | solution.py:243
  60.0 12.2 %collective-permute-start.12 = (bf16[4,2,3,32,256]{4,3,2,1,0:T(8,128)(2,1)S(1)}, bf16[4,2,3,32,256]{4,3,2,1,0:T(8,128)(2,1)S(1)}, u32[]{:S(2)}, u32[]{:S(2)}) collective-permute-start(bf16[4,2,3,32,256]{4,3,2,1,0:T(8,128)(2,1)S(1)} %get-tuple-element.67), channel_id=1, source_target_pairs={{0,3},{1,2},{2,1},{3,0},{4,7},{5,6},{6,5},{7,4},{8,11},{9,10},{10,... | collective-permute-start | bytes 1179656 | tf_op jit(solution)/shard_map/ppermute | solution.py:243
  60.8 13.3 %collective-permute-start.6 = (bf16[4,2,3,32,256]{4,3,2,1,0:T(8,128)(2,1)S(1)}, bf16[4,2,3,32,256]{4,3,2,1,0:T(8,128)(2,1)S(1)}, u32[]{:S(2)}, u32[]{:S(2)}) collective-permute-start(bf16[4,2,3,32,256]{4,3,2,1,0:T(8,128)(2,1)S(1)} %get-tuple-element.53), channel_id=1, source_target_pairs={{0,1},{1,0},{2,3},{3,2},{4,5},{5,4},{6,7},{7,6},{8,9},{9,8},{10,11... | collective-permute-start | bytes 1179656 | tf_op jit(solution)/shard_map/ppermute | solution.py:243
  71.1 9.8 %collective-permute-start.16 = (bf16[2,2,2,3,32,256]{5,4,3,2,1,0:T(8,128)(2,1)S(1)}, bf16[2,2,2,3,32,256]{5,4,3,2,1,0:T(8,128)(2,1)S(1)}, u32[]{:S(2)}, u32[]{:S(2)}) collective-permute-start(bf16[2,2,2,3,32,256]{5,4,3,2,1,0:T(8,128)(2,1)S(1)} %get-tuple-element.79), channel_id=1, source_target_pairs={{0,1},{1,0},{2,3},{3,2},{4,5},{5,4},{6,7},{7,6},{8,9},{9,8},{10,11... | collective-permute-start | bytes 1179656 | tf_op jit(solution)/shard_map/ppermute | solution.py:243
  72.3 11.1 %collective-permute-start.13 = (bf16[2,2,2,3,32,256]{5,4,3,2,1,0:T(8,128)(2,1)S(1)}, bf16[2,2,2,3,32,256]{5,4,3,2,1,0:T(8,128)(2,1)S(1)}, u32[]{:S(2)}, u32[]{:S(2)}) collective-permute-start(bf16[2,2,2,3,32,256]{5,4,3,2,1,0:T(8,128)(2,1)S(1)} %get-tuple-element.71), channel_id=1, source_target_pairs={{0,4},{1,5},{2,6},{3,7},{4,0},{5,1},{6,2},{7,3},{8,12},{9,13},{10,... | collective-permute-start | bytes 1179656 | tf_op jit(solution)/shard_map/ppermute | solution.py:243
  74.2 13.0 %collective-permute-start.10 = (bf16[2,2,2,3,32,256]{5,4,3,2,1,0:T(8,128)(2,1)S(1)}, bf16[2,2,2,3,32,256]{5,4,3,2,1,0:T(8,128)(2,1)S(1)}, u32[]{:S(2)}, u32[]{:S(2)}) collective-permute-start(bf16[2,2,2,3,32,256]{5,4,3,2,1,0:T(8,128)(2,1)S(1)} %get-tuple-element.63), channel_id=1, source_target_pairs={{0,3},{1,2},{2,1},{3,0},{4,7},{5,6},{6,5},{7,4},{8,11},{9,10},{10,... | collective-permute-start | bytes 1179656 | tf_op jit(solution)/shard_map/ppermute | solution.py:243
  81.0 9.0 %collective-permute-start.17 = (bf16[1,2,2,3,32,256]{5,4,3,2,1,0:T(8,128)(2,1)S(1)}, bf16[1,2,2,3,32,256]{5,4,3,2,1,0:T(8,128)(2,1)S(1)}, u32[]{:S(2)}, u32[]{:S(2)}) collective-permute-start(bf16[1,2,2,3,32,256]{5,4,3,2,1,0:T(8,128)(2,1)S(1)} %get-tuple-element.81), channel_id=1, source_target_pairs={{0,3},{1,2},{2,1},{3,0},{4,7},{5,6},{6,5},{7,4},{8,11},{9,10},{10,... | collective-permute-start | bytes 589832 | tf_op jit(solution)/shard_map/ppermute | solution.py:243
  83.5 6.5 %collective-permute-start.14 = (bf16[1,2,2,3,32,256]{5,4,3,2,1,0:T(8,128)(2,1)S(1)}, bf16[1,2,2,3,32,256]{5,4,3,2,1,0:T(8,128)(2,1)S(1)}, u32[]{:S(2)}, u32[]{:S(2)}) collective-permute-start(bf16[1,2,2,3,32,256]{5,4,3,2,1,0:T(8,128)(2,1)S(1)} %get-tuple-element.73), channel_id=1, source_target_pairs={{0,1},{1,0},{2,3},{3,2},{4,5},{5,4},{6,7},{7,6},{8,9},{9,8},{10,11... | collective-permute-start | bytes 589832 | tf_op jit(solution)/shard_map/ppermute | solution.py:243
  87.3 7.3 %collective-permute-start.11 = (bf16[1,2,2,3,32,256]{5,4,3,2,1,0:T(8,128)(2,1)S(1)}, bf16[1,2,2,3,32,256]{5,4,3,2,1,0:T(8,128)(2,1)S(1)}, u32[]{:S(2)}, u32[]{:S(2)}) collective-permute-start(bf16[1,2,2,3,32,256]{5,4,3,2,1,0:T(8,128)(2,1)S(1)} %get-tuple-element.65), channel_id=1, source_target_pairs={{0,4},{1,5},{2,6},{3,7},{4,0},{5,1},{6,2},{7,3},{8,12},{9,13},{10,... | collective-permute-start | bytes 589832 | tf_op jit(solution)/shard_map/ppermute | solution.py:243
where the time goes:
time: 96 us; the launch traced here: 95.8 us
  Pallas kernels  33.3 us (35%)
  starting transfers between devices  27.8 us (29%)
  waiting for transfers between devices  26.5 us (28%)
  local copies, waits for them, and re-layouts  4.32 us (4%)
  between operations  2.34 us (2%)
  other arithmetic  1.45 us (2%)
    pallas_call x37, Pallas kernels, call(): pl.pallas_call(kernel, out_shape=outs, in_specs=specs or [VM] * len(given...  33.3 us
    ppermute x12, waiting for transfers between devices, exchange(): return lax.ppermute(block, 'dp', PAIRS[step])  24.1 us
    ppermute x12, starting transfers between devices, exchange(): return lax.ppermute(block, 'dp', PAIRS[step])  15.5 us
    ppermute x6, starting transfers between devices, relay(): return lax.ppermute(block, 'section', pairs + [(b, a) for a, b in pairs])  12.4 us
    unnamed x14, local copies, waits for them, and re-layouts  2.97 us
    ppermute x6, waiting for transfers between devices, relay(): return lax.ppermute(block, 'section', pairs + [(b, a) for a, b in pairs])  2.4 us
  transfers between devices with their start and end apart: 18, of which 7 were waited for; matrix products, arithmetic and copies ran while one was open for 0% of the time, Pallas kernels for 29%

commit v1 on v0

--- a/solution.py
+++ b/solution.py
@@ -16,6 +16,7 @@
 DP = 8
 COST = 2 * 512 * 9 * 256 * 256
 FOLD_COST = 16
+PREPARE_MIB = 53
 SHARE = CH // DP
 BF = jnp.bfloat16
 F32 = jnp.float32
@@ -41,18 +42,23 @@
     return odd if role == 0 else 1 - odd
 
 
-def call(kernel, name, given, outs, specs=None, scratch=(), mib=8, aliases={}, ops=1):
+def call(kernel, name, given, outs, scratch=(), mib=8, aliases={}, ops=1, after=()):
+    n_given = len(given)
+
+    def body(*refs):
+        kernel(*refs[:n_given], *refs[n_given + len(after) :])
+
     return pl.pallas_call(
-        kernel,
+        body if after else kernel,
         out_shape=outs,
-        in_specs=specs or [VM] * len(given),
+        in_specs=[VM] * n_given + [pl.BlockSpec(memory_space=pl.ANY)] * len(after),
         out_specs=jax.tree.map(lambda _: VM, outs),
         scratch_shapes=list(scratch),
         input_output_aliases=aliases,
         compiler_params=pltpu.CompilerParams(vmem_limit_bytes=mib << 20),
         cost_estimate=pl.CostEstimate(flops=ops * COST, bytes_accessed=1024, transcendentals=0),
         name=name,
-    )(*given)
+    )(*given, *after)
 
 
 def clear_edges(win):
@@ -98,6 +104,41 @@
         first = lax.axis_index("section") == 0
         total = jnp.where(first, objective[tick - 1].astype(F32), total)
     return total
+
+
+def prepare_kernel(table, *refs):
+    del table
+    fields, laters, earlies = refs[0:2], refs[2:4], refs[4:6]
+    g2s, masks = refs[6:8], refs[8:10]
+    for role in range(2):
+        g2s[role][...] = jnp.where(laters[role][0] > 0, fields[role][0], jnp.zeros((), BF))
+        masks[role][...] = earlies[role][0]
+
+
+def prepare(table, pending, pre1, pre2):
+    def at_half(role, i, table):
+        return half_of(role), 0, 0
+
+    def at_slot(role, i, table):
+        half = half_of(role)
+        return 4 * half + table[0, half * lax.axis_size("section") + lax.axis_index("section")], 0, 0
+
+    def blocks(place):
+        return [pl.BlockSpec((1, PIX, CH), functools.partial(place, role)) for role in range(2)]
+
+    return pl.pallas_call(
+        prepare_kernel,
+        grid_spec=pltpu.PrefetchScalarGridSpec(
+            num_scalar_prefetch=1,
+            grid=(1,),
+            in_specs=blocks(at_half) + blocks(at_slot) + blocks(at_slot),
+            out_specs=[VM] * 4,
+        ),
+        out_shape=[FIELD] * 4,
+        compiler_params=pltpu.CompilerParams(vmem_limit_bytes=PREPARE_MIB << 20),
+        cost_estimate=pl.CostEstimate(flops=1, bytes_accessed=1024, transcendentals=0),
+        name="prepare",
+    )(table, pending, pending, pre2, pre2, pre1, pre1)
 
 
 def early_of_kernel(role, mask, taps, g2, g1_out, win):
@@ -121,11 +162,13 @@
     out[...] = conv(win, taps, 18 * half_of(role)).astype(BF)
 
 
-def tap_grads(win, x, field):
-    fill_windows(win, field)
-    xt = x.T
+def tap_grads(wins, xs, fields):
+    for win, field in zip(wins, fields):
+        fill_windows(win, field)
+    xt = jnp.concatenate([x.T for x in xs], axis=1)
     for k in range(9):
-        yield k, jnp.dot(xt, tap_of(win, 8 - k), preferred_element_type=F32)
+        right = jnp.concatenate([tap_of(win, 8 - k) for win in wins], axis=0)
+        yield k, jnp.dot(xt, right, preferred_element_type=F32)
 
 
 def left_side(which, saved, slot):
@@ -133,12 +176,11 @@
     return jnp.maximum(x, jnp.zeros((), BF)) if which else x
 
 
-def wgrad_kernel(which, role, tick, table, saved, field, *refs):
-    old = None if tick == 0 else refs[0]
-    new, win = refs[-2:]
-    x = left_side(which, saved, slot_of(table, role, tick))
-    for k, term in tap_grads(win, x, field[...].astype(F32)):
-        new[k] = term if old is None else old[k] + term
+def wgrad_kernel(which, role, table, saved, *refs):
+    fields, new, wins = refs[:2], refs[2], refs[3:]
+    xs = [left_side(which, saved, slot_of(table, role, tick)) for tick in range(2)]
+    for k, term in tap_grads(wins, xs, [field[...].astype(F32) for field in fields]):
+        new[k] = term
 
 
 def replica_at(order, r):
@@ -165,17 +207,18 @@
 
 
 def last_two_kernel(table, pre1, pre2, objective, *refs):
-    given, olds = refs[:4], refs[4:6]
-    sends, keeps, g2s = refs[6:9], refs[9:12], refs[12:14]
-    wins, staged = refs[14:16], refs[16:18]
+    given, befores, olds = refs[:4], refs[4:6], refs[6:8]
+    sends, keeps, g2s = refs[8:11], refs[11:14], refs[14:16]
+    wins, staged = refs[16:20], refs[20:22]
     tick = TICKS - 1
     for role in range(2):
         slot = slot_of(table, role, tick)
         g2 = add_up(role, tick, given[role], given[3 - role], objective)
         g2 = jnp.where(pre2[slot] > 0, g2, 0.0)
         g2s[role][...] = g2.astype(BF)
-        x = left_side(1, pre1, slot)
-        for k, term in tap_grads(wins[role], x, g2):
+        xs = [left_side(1, pre1, slot_of(table, role, tick - 1)), left_side(1, pre1, slot)]
+        fields = [befores[role][...].astype(F32), g2]
+        for k, term in tap_grads(wins[2 * role : 2 * role + 2], xs, fields):
             staged[role][k] = olds[role][k] + term
             put_shares(staged[role], k, sends, keeps, role)
 
@@ -187,12 +230,13 @@
 
 
 def last_one_kernel(table, entries, *refs):
-    g1s, olds = refs[:2], refs[2:4]
-    sends, keeps = refs[4:7], refs[7:10]
-    wins, staged = refs[10:12], refs[12:14]
+    befores, g1s, olds = refs[:2], refs[2:4], refs[4:6]
+    sends, keeps = refs[6:9], refs[9:12]
+    wins, staged = refs[12:16], refs[16:18]
     for role in range(2):
-        x = left_side(0, entries, slot_of(table, role, TICKS - 1))
-        for k, term in tap_grads(wins[role], x, g1s[role][...].astype(F32)):
+        xs = [left_side(0, entries, slot_of(table, role, tick)) for tick in (TICKS - 2, TICKS - 1)]
+        fields = [befores[role][...].astype(F32), g1s[role][...].astype(F32)]
+        for k, term in tap_grads(wins[2 * role : 2 * role + 2], xs, fields):
             staged[role][k] = olds[role][k] + term
             put_shares(staged[role], k, sends, keeps, role)
 
@@ -213,11 +257,16 @@
 
 def fold_two_kernel(*refs):
     for o in range(3):
+        fold_in(*refs[o::3])
+
+
+def fold_two_last_kernel(*refs):
+    for o in range(3):
         keep, got, send, left = refs[o::3]
         fold_in(keep, got, send.at[:, 1], left.at[:, 1])
 
 
-def fold_one_kernel(keep, got, old_send, old_left, send, left):
+def fold_one_last_kernel(keep, got, old_send, old_left, send, left):
     del old_send, old_left
     fold_in(keep, got, send.at[:, 0], left.at[:, 0])
 
@@ -261,17 +310,28 @@
     objective = objective_adjoints.reshape(TICKS - 1, PIX, CH)
     windows = [WINDOWS]
 
-    sums1, sums2 = [(), ()], [(), ()]
+    all_g2s, all_g1s = [], []
+
+    def early_sums(which, saved, fields):
+        return [
+            call(
+                functools.partial(wgrad_kernel, which, role),
+                f"wgrad{which + 1}_{role}",
+                (table, saved, fields[0][role], fields[1][role]),
+                SUMS,
+                scratch=windows * 2,
+                ops=2,
+            )
+            for role in range(2)
+        ]
+
     gots = outs = None
+    prepared = prepare(table, pending, pre1, pre2)
     for tick in range(TICKS - 1):
         g2s, g1s, new_outs, new_gots = [], [], [], []
         for role in range(2):
             if tick == 0:
-                half = half_of(role)
-                slot = 4 * half + table[0, half * lax.axis_size("section") + lax.axis_index("section")]
-                field = lax.dynamic_index_in_dim(pending, half, 0, keepdims=False)
-                g2 = jnp.where(lax.dynamic_index_in_dim(pre2, slot, 0, keepdims=False) > 0, field, jnp.zeros((), BF))
-                mask = lax.dynamic_index_in_dim(pre1, slot, 0, keepdims=False)
+                g2, mask = prepared[role], prepared[2 + role]
                 g1 = call(
                     functools.partial(early_of_kernel, role),
                     f"early_{role}_0",
@@ -287,6 +347,7 @@
                     (table, pre1, pre2, taps, *given),
                     (FIELD, FIELD),
                     scratch=windows,
+                    after=sums2 if tick == 2 else (),
                 )
             out = call(functools.partial(late_kernel, role), f"late_{role}_{tick}", (taps, g1), FIELD, scratch=windows)
             g2s.append(g2)
@@ -294,28 +355,23 @@
             new_outs.append(out)
             new_gots.append(relay(out, role))
         gots, outs = new_gots, new_outs
-        for role in range(2):
-            for which, saved, fields, sums in ((1, pre1, g2s, sums2), (0, entries, g1s, sums1)):
-                new = call(
-                    functools.partial(wgrad_kernel, which, role, tick),
-                    f"wgrad{which + 1}_{role}_{tick}",
-                    (table, saved, fields[role], *sums[role]),
-                    SUMS,
-                    scratch=windows,
-                    aliases={3: 0} if sums[role] else {},
-                )
-                sums[role] = (new,)
+        all_g2s.append(g2s)
+        all_g1s.append(g1s)
+        if tick == 1:
+            sums2 = early_sums(1, pre1, all_g2s)
+            sums1 = early_sums(0, entries, all_g1s)
 
     part = jax.ShapeDtypeStruct((4, 2, 3, SHARE, CH), BF)
     staged = [pltpu.VMEM((9, CH, CH), F32)] * 2
     res = call(
         last_two_kernel,
         "last_two",
-        (table, pre1, pre2, objective, gots[1], gots[0], *outs, *sums2[0], *sums2[1]),
+        (table, pre1, pre2, objective, gots[1], gots[0], *outs, *g2s, *sums2),
         (part,) * 6 + (FIELD,) * 2,
-        scratch=windows * 2 + staged,
+        scratch=windows * 4 + staged,
         mib=16,
-        ops=2,
+        ops=4,
+        after=sums1,
     )
     keeps2, g2s = res[3:6], res[6:8]
     gots2 = [exchange(res[o], ORDERS[o][0]) for o in range(3)]
@@ -332,11 +388,11 @@
     res = call(
         last_one_kernel,
         "last_one",
-        (table, entries, *g1s, *sums1[0], *sums1[1]),
+        (table, entries, *all_g1s[-1], *g1s, *sums1),
         (part,) * 6,
-        scratch=windows * 2 + staged,
+        scratch=windows * 4 + staged,
         mib=16,
-        ops=2,
+        ops=4,
     )
     keeps1 = res[3:6]
     gots1 = [exchange(res[o], ORDERS[o][0]) for o in range(3)]
@@ -350,19 +406,21 @@
     )
 
     parts = []
-    part2 = jax.ShapeDtypeStruct((2, 2, 2, 3, SHARE, CH), BF)
+    part2 = jax.ShapeDtypeStruct((2, 2, 3, SHARE, CH), BF)
     part3 = jax.ShapeDtypeStruct((1, 2, 2, 3, SHARE, CH), BF)
-    begun = call(fold_two_kernel, "fold_two", (*keeps2, *gots2), (part2,) * 6, ops=FOLD_COST)
+    res = call(fold_two_kernel, "fold_two", (*keeps2, *gots2), (part2,) * 6, ops=FOLD_COST)
+    gots2 = [exchange(res[o], ORDERS[o][1]) for o in range(3)]
+    begun = call(fold_two_last_kernel, "fold_two_last", (*res[3:6], *gots2), (part3,) * 6, ops=FOLD_COST)
     for o in range(3):
+        send, keep = call(fold_in, f"fold_one_{o}", (keeps1[o], gots1[o]), (part2, part2))
+        got = exchange(send, ORDERS[o][1])
         send, keep = call(
-            fold_one_kernel,
-            f"fold_one_{o}",
-            (keeps1[o], gots1[o], begun[o], begun[3 + o]),
-            (part2, part2),
+            fold_one_last_kernel,
+            f"fold_one_last_{o}",
+            (keep, got, begun[o], begun[3 + o]),
+            (part3, part3),
             aliases={2: 0, 3: 1},
         )
-        got = exchange(send, ORDERS[o][1])
-        send, keep = call(fold_in, f"fold_last_{o}", (keep, got), (part3, part3))
         parts += [keep, exchange(send, ORDERS[o][2])]
     scale = 1.0 / math.sqrt(TICKS * DP * PIX)
     grads = call(

time: 96 us -> 89.1 us (0.928)
  waiting for transfers between devices: 26.5 us -> 19.1 us
  starting transfers between devices: 27.8 us -> 34.5 us
  local copies, waits for them, and re-layouts: 4.32 us -> 1.8 us
  other arithmetic: 1.45 us -> 0.01 us
  between operations: 2.34 us -> 0.99 us
    ppermute x12 -> x15, waiting for transfers between devices: 24.1 us -> 14.7 us  [exchange(): return lax.ppermute(block, 'dp', PAIRS[step])]
    ppermute x12 -> x15, starting transfers between devices: 15.5 us -> 22.7 us  [exchange(): return lax.ppermute(block, 'dp', PAIRS[step])]
    ppermute x6, waiting for transfers between devices: 2.4 us -> 4.42 us  [relay(): return lax.ppermute(block, 'section', pairs + [(b, a) for a, b in pairs])]
    select_n x1 -> x0, other arithmetic: 1.45 us -> none  [on_device(): jnp.where(lax.dynamic_index_in_dim(pre2, slot, 0, keepdims=False) > 0, fi...]
    dynamic_slice x1 -> x0, local copies, waits for them, and re-layouts: 1.35 us -> none  [on_device(): table[0, half * lax.axis_size('section') + lax.axis_index('section')]]
    unnamed x14 -> x16, local copies, waits for them, and re-layouts: 2.97 us -> 1.8 us
    pallas_call x37 -> x31, Pallas kernels: 33.3 us -> 32.5 us  [the longest x30 29.8 us: call(): pl.pallas_call(body if after else kernel, out_shape=outs, in_specs=[VM] *...]
  transfers between devices with their start and end apart: 18 -> 21, of which waited for: 7 -> 10; matrix products, arithmetic and copies ran while one was open for 0% -> 0% of each run, Pallas kernels for 29% -> 24%
where the time goes in v1:
time: 89.1 us; the launch traced here: 88.8 us
  starting transfers between devices  34.5 us (39%)
  Pallas kernels  32.5 us (36%)
  waiting for transfers between devices  19.1 us (21%)
  local copies, waits for them, and re-layouts  1.8 us (2%)
  between operations  0.99 us (1%)
    pallas_call x30, Pallas kernels, call(): pl.pallas_call(body if after else kernel, out_shape=outs, in_specs=[VM] *...  29.8 us
    ppermute x15, starting transfers between devices, exchange(): return lax.ppermute(block, 'dp', PAIRS[step])  22.7 us
    ppermute x15, waiting for transfers between devices, exchange(): return lax.ppermute(block, 'dp', PAIRS[step])  14.7 us
    ppermute x6, starting transfers between devices, relay(): return lax.ppermute(block, 'section', pairs + [(b, a) for a, b in pairs])  11.7 us
    ppermute x6, waiting for transfers between devices, relay(): return lax.ppermute(block, 'section', pairs + [(b, a) for a, b in pairs])  4.42 us
    pallas_call x1, Pallas kernels, prepare(): pl.pallas_call(prepare_kernel, grid_spec=pltpu.PrefetchScalarGridSpec(num...  2.7 us
    unnamed x16, local copies, waits for them, and re-layouts  1.8 us
  transfers between devices with their start and end apart: 21, of which 10 were waited for; matrix products, arithmetic and copies ran while one was open for 0% of the time, Pallas kernels for 24%

profile of v1, /device:TPU:8, one launch (start us, length us, event | category | flops | bytes accessed | tf_op | source)
XLA Modules:
  0.0 88.8 jit_solution(9935782883300418991)
XLA Ops:
  0.7 0.8 copy-done.4
  1.5 2.7 %prepare.1 = (bf16[512,256]{1,0:T(8,128)(2,1)S(1)}, bf16[512,256]{1,0:T(8,128)(2,1)S(1)}, bf16[512,256]{1,0:T(8,128)(2,1)S(1)}, bf16[512,256]{1,0:T(8,128)(2,1)}) custom-call(s32[4,32]{1,0:T(4,128)S(1)} %copy-done.4, bf16[2,512,256]{2,1,0:T(8,128)(2,1)} %bitcast.53, bf16[2,512,256]{2,1,0:T(8,128)(2,1)} %bitcast.54, bf16[8,512,256]{2,1,0:T(8,128)(2,1)} %bitcast.40, ...), custom_call_target="tpu_custom_call" | custom-call | flops 1 | bytes 1024 | tf_op jit(solution)/shard_map/prepare/pallas_call | solution.py:129
  4.2 0.9 %copy-done.5 = bf16[512,256]{1,0:T(8,128)(2,1)S(1)} copy-done((bf16[512,256]{1,0:T(8,128)(2,1)S(1)}, bf16[512,256]{1,0:T(8,128)(2,1)}, u32[]{:S(2)}) %copy-start.5) | copy-done | bytes 262168
  5.1 0.8 early_1_0.1.g1.refs_0_
  6.0 0.8 late_1_0.1.refs_1_
  6.9 0.8 early_0_0.1.g1.refs_0_
  7.7 0.8 late_0_0.1.refs_1_
  8.6 4.8 %collective-permute-start.2 = (bf16[512,256]{1,0:T(8,128)(2,1)S(1)}, bf16[512,256]{1,0:T(8,128)(2,1)S(1)}, u32[]{:S(2)}, u32[]{:S(2)}) collective-permute-start(bf16[512,256]{1,0:T(8,128)(2,1)S(1)} %late_0_0.1.refs_1_), channel_id=1, source_target_pairs={{8,16},{24,32},{40,48},{56,64},{72,80},{88,96},{104,112},{16,8},{3... | collective-permute-start | bytes 786440 | tf_op jit(solution)/shard_map/ppermute | solution.py:288
  13.4 1.0 %early_0_1.1 = (bf16[512,256]{1,0:T(8,128)(2,1)S(1)}, bf16[512,256]{1,0:T(8,128)(2,1)S(1)}) custom-call(s32[4,32]{1,0:T(4,128)S(1)} %copy-done.4, bf16[8,512,256]{2,1,0:T(8,128)(2,1)S(1)} %bitcast.31, bf16[8,512,256]{2,1,0:T(8,128)(2,1)S(1)} %bitcast.42, bf16[36,256,256]{2,1,0:T(8,128)(2,1)S(1)} %bitcast.18, ...), custom_call_target="tpu_custom_call" | custom-call | flops 603979776 | bytes 1024 | tf_op jit(solution)/shard_map/early_0_1/pallas_call | solution.py:51
  14.4 0.8 late_0_1.1.refs_5_
  15.2 3.0 %collective-permute-start.1 = (bf16[512,256]{1,0:T(8,128)(2,1)S(1)}, bf16[512,256]{1,0:T(8,128)(2,1)S(1)}, u32[]{:S(2)}, u32[]{:S(2)}) collective-permute-start(bf16[512,256]{1,0:T(8,128)(2,1)S(1)} %late_0_1.1.refs_5_), channel_id=1, source_target_pairs={{8,16},{24,32},{40,48},{56,64},{72,80},{88,96},{104,112},{16,8},{3... | collective-permute-start | bytes 786440 | tf_op jit(solution)/shard_map/ppermute | solution.py:288
  18.5 1.0 %early_1_1.1 = (bf16[512,256]{1,0:T(8,128)(2,1)S(1)}, bf16[512,256]{1,0:T(8,128)(2,1)S(1)}) custom-call(s32[4,32]{1,0:T(4,128)S(1)} %copy-done.4, bf16[8,512,256]{2,1,0:T(8,128)(2,1)S(1)} %bitcast.32, bf16[8,512,256]{2,1,0:T(8,128)(2,1)S(1)} %bitcast.43, bf16[36,256,256]{2,1,0:T(8,128)(2,1)S(1)} %bitcast.20, ...), custom_call_target="tpu_custom_call" | custom-call | flops 603979776 | bytes 1024 | tf_op jit(solution)/shard_map/early_1_1/pallas_call | solution.py:51
  19.5 0.8 late_1_1.1.refs_5_
  20.6 1.6 %wgrad2_1.1.refs_8_.refs_7_.refs_11_ = f32[9,256,256]{2,1,0:T(8,128)S(1)} custom-call(s32[4,32]{1,0:T(4,128)S(1)} %copy-done.4, bf16[8,512,256]{2,1,0:T(8,128)(2,1)S(1)} %bitcast.33, bf16[512,256]{1,0:T(8,128)(2,1)S(1)} %get-tuple-element.53.g2.refs_0_, bf16[512,256]{1,0:T(8,128)(2,1)S(1)} %get-tuple-element.58.refs_1_), custom_call_target="tpu_custom_call" | custom-call | flops 1207959552 | bytes 1024 | tf_op jit(solution)/shard_map/wgrad2_1/pallas_call | solution.py:51
  22.3 1.6 %wgrad2_0.1.refs_7_.refs_6_.refs_10_ = f32[9,256,256]{2,1,0:T(8,128)S(1)} custom-call(s32[4,32]{1,0:T(4,128)S(1)} %copy-done.4, bf16[8,512,256]{2,1,0:T(8,128)(2,1)S(1)} %bitcast.34, bf16[512,256]{1,0:T(8,128)(2,1)S(1)} %get-tuple-element.55.refs_0_.g2, bf16[512,256]{1,0:T(8,128)(2,1)S(1)} %get-tuple-element.56.refs_1_), custom_call_target="tpu_custom_call" | custom-call | flops 1207959552 | bytes 1024 | tf_op jit(solution)/shard_map/wgrad2_0/pallas_call | solution.py:51
  23.9 1.2 %collective-permute-done.1.refs_4_ = bf16[512,256]{1,0:T(8,128)(2,1)S(1)} collective-permute-done((bf16[512,256]{1,0:T(8,128)(2,1)S(1)}, bf16[512,256]{1,0:T(8,128)(2,1)S(1)}, u32[]{:S(2)}, u32[]{:S(2)}) %collective-permute-start.1) | collective-permute-done | bytes 262176 | tf_op jit(solution)/shard_map/ppermute | solution.py:288
  25.1 1.0 %early_1_2.1 = (bf16[512,256]{1,0:T(8,128)(2,1)S(1)}, bf16[512,256]{1,0:T(8,128)(2,1)S(1)}) custom-call(s32[4,32]{1,0:T(4,128)S(1)} %copy-done.4, bf16[8,512,256]{2,1,0:T(8,128)(2,1)S(1)} %bitcast.35, bf16[8,512,256]{2,1,0:T(8,128)(2,1)S(1)} %bitcast.44, bf16[36,256,256]{2,1,0:T(8,128)(2,1)S(1)} %bitcast.22, ...), custom_call_target="tpu_custom_call" | custom-call | flops 603979776 | bytes 1024 | tf_op jit(solution)/shard_map/early_1_2/pallas_call | solution.py:51
  26.1 0.8 late_1_2.1.refs_7_
  26.9 1.0 %early_0_2.1 = (bf16[512,256]{1,0:T(8,128)(2,1)S(1)}, bf16[512,256]{1,0:T(8,128)(2,1)S(1)}) custom-call(s32[4,32]{1,0:T(4,128)S(1)} %copy-done.4, bf16[8,512,256]{2,1,0:T(8,128)(2,1)S(1)} %bitcast.36, bf16[8,512,256]{2,1,0:T(8,128)(2,1)S(1)} %bitcast.45, bf16[36,256,256]{2,1,0:T(8,128)(2,1)S(1)} %bitcast.24, ...), custom_call_target="tpu_custom_call" | custom-call | flops 603979776 | bytes 1024 | tf_op jit(solution)/shard_map/early_0_2/pallas_call | solution.py:51
  27.9 0.8 late_0_2.1.refs_6_
  28.8 3.5 %collective-permute-start.5 = (bf16[512,256]{1,0:T(8,128)(2,1)S(1)}, bf16[512,256]{1,0:T(8,128)(2,1)S(1)}, u32[]{:S(2)}, u32[]{:S(2)}) collective-permute-start(bf16[512,256]{1,0:T(8,128)(2,1)S(1)} %late_0_2.1.refs_6_), channel_id=1, source_target_pairs={{8,16},{24,32},{40,48},{56,64},{72,80},{88,96},{104,112},{16,8},{3... | collective-permute-start | bytes 786440 | tf_op jit(solution)/shard_map/ppermute | solution.py:288
  32.4 1.6 %wgrad1_1.1.refs_13_.refs_5_ = f32[9,256,256]{2,1,0:T(8,128)S(1)} custom-call(s32[4,32]{1,0:T(4,128)S(1)} %copy-done.4, bf16[8,512,256]{2,1,0:T(8,128)(2,1)S(1)} %bitcast.47, bf16[512,256]{1,0:T(8,128)(2,1)S(1)} %early_1_0.1.g1.refs_0_, bf16[512,256]{1,0:T(8,128)(2,1)S(1)} %get-tuple-element.60.g1.refs_1_), custom_call_target="tpu_custom_call" | custom-call | flops 1207959552 | bytes 1024 | tf_op jit(solution)/shard_map/wgrad1_1/pallas_call | solution.py:51
  34.0 1.6 %wgrad1_0.1.refs_12_.refs_4_ = f32[9,256,256]{2,1,0:T(8,128)S(1)} custom-call(s32[4,32]{1,0:T(4,128)S(1)} %copy-done.4, bf16[8,512,256]{2,1,0:T(8,128)(2,1)S(1)} %bitcast.48, bf16[512,256]{1,0:T(8,128)(2,1)S(1)} %early_0_0.1.g1.refs_0_, bf16[512,256]{1,0:T(8,128)(2,1)S(1)} %get-tuple-element.54.g1.refs_1_), custom_call_target="tpu_custom_call" | custom-call | flops 1207959552 | bytes 1024 | tf_op jit(solution)/shard_map/wgrad1_0/pallas_call | solution.py:51
  35.6 3.0 %collective-permute-done.5.refs_5_ = bf16[512,256]{1,0:T(8,128)(2,1)S(1)} collective-permute-done((bf16[512,256]{1,0:T(8,128)(2,1)S(1)}, bf16[512,256]{1,0:T(8,128)(2,1)S(1)}, u32[]{:S(2)}, u32[]{:S(2)}) %collective-permute-start.5) | collective-permute-done | bytes 262176 | tf_op jit(solution)/shard_map/ppermute | solution.py:288
  38.6 3.5 %last_two.1 = (bf16[4,2,3,32,256]{4,3,2,1,0:T(8,128)(2,1)S(1)}, bf16[4,2,3,32,256]{4,3,2,1,0:T(8,128)(2,1)S(1)}, bf16[4,2,3,32,256]{4,3,2,1,0:T(8,128)(2,1)S(1)}...) custom-call(s32[4,32]{1,0:T(4,128)S(1)} %copy-done.4, ...), custom_call_target="tpu_custom_call" | custom-call | flops 2415919104 | bytes 1024 | tf_op jit(solution)/shard_map/last_two/pallas_call | solution.py:51
  42.1 2.0 %collective-permute-start.8 = (bf16[4,2,3,32,256]{4,3,2,1,0:T(8,128)(2,1)S(1)}, bf16[4,2,3,32,256]{4,3,2,1,0:T(8,128)(2,1)S(1)}, u32[]{:S(2)}, u32[]{:S(2)}) collective-permute-start(bf16[4,2,3,32,256]{4,3,2,1,0:T(8,128)(2,1)S(1)} %get-tuple-element.73), channel_id=1, source_target_pairs={{0,1},{1,0},{2,3},{3,2},{4,5},{5,4},{6,7},{7,6},{8,9},{9,8},{10,11... | collective-permute-start | bytes 1179656 | tf_op jit(solution)/shard_map/ppermute | solution.py:292
  44.1 2.5 %collective-permute-start.9 = (bf16[4,2,3,32,256]{4,3,2,1,0:T(8,128)(2,1)S(1)}, bf16[4,2,3,32,256]{4,3,2,1,0:T(8,128)(2,1)S(1)}, u32[]{:S(2)}, u32[]{:S(2)}) collective-permute-start(bf16[4,2,3,32,256]{4,3,2,1,0:T(8,128)(2,1)S(1)} %get-tuple-element.74), channel_id=1, source_target_pairs={{0,3},{1,2},{2,1},{3,0},{4,7},{5,6},{6,5},{7,4},{8,11},{9,10},{10,... | collective-permute-start | bytes 1179656 | tf_op jit(solution)/shard_map/ppermute | solution.py:292
  46.6 2.6 %collective-permute-start.10 = (bf16[4,2,3,32,256]{4,3,2,1,0:T(8,128)(2,1)S(1)}, bf16[4,2,3,32,256]{4,3,2,1,0:T(8,128)(2,1)S(1)}, u32[]{:S(2)}, u32[]{:S(2)}) collective-permute-start(bf16[4,2,3,32,256]{4,3,2,1,0:T(8,128)(2,1)S(1)} %get-tuple-element.75), channel_id=1, source_target_pairs={{0,4},{1,5},{2,6},{3,7},{4,0},{5,1},{6,2},{7,3},{8,12},{9,13},{10,... | collective-permute-start | bytes 1179656 | tf_op jit(solution)/shard_map/ppermute | solution.py:292
  49.3 0.8 early_0_3.1.g1_zero.refs_2_
  50.1 0.8 early_1_3.1.g1_one.refs_3_
  50.9 3.4 %last_one.1 = (bf16[4,2,3,32,256]{4,3,2,1,0:T(8,128)(2,1)S(1)}, bf16[4,2,3,32,256]{4,3,2,1,0:T(8,128)(2,1)S(1)}, bf16[4,2,3,32,256]{4,3,2,1,0:T(8,128)(2,1)S(1)}...) custom-call(s32[4,32]{1,0:T(4,128)S(1)} %copy-done.4, ...), custom_call_target="tpu_custom_call" | custom-call | flops 2415919104 | bytes 1024 | tf_op jit(solution)/shard_map/last_one/pallas_call | solution.py:51
  54.3 1.1 %collective-permute-start.6 = (bf16[4,2,3,32,256]{4,3,2,1,0:T(8,128)(2,1)S(1)}, bf16[4,2,3,32,256]{4,3,2,1,0:T(8,128)(2,1)S(1)}, u32[]{:S(2)}, u32[]{:S(2)}) collective-permute-start(bf16[4,2,3,32,256]{4,3,2,1,0:T(8,128)(2,1)S(1)} %get-tuple-element.67), channel_id=1, source_target_pairs={{0,1},{1,0},{2,3},{3,2},{4,5},{5,4},{6,7},{7,6},{8,9},{9,8},{10,11... | collective-permute-start | bytes 1179656 | tf_op jit(solution)/shard_map/ppermute | solution.py:292
  56.0 0.9 %collective-permute-start.18 = (bf16[4,2,3,32,256]{4,3,2,1,0:T(8,128)(2,1)S(1)}, bf16[4,2,3,32,256]{4,3,2,1,0:T(8,128)(2,1)S(1)}, u32[]{:S(2)}, u32[]{:S(2)}) collective-permute-start(bf16[4,2,3,32,256]{4,3,2,1,0:T(8,128)(2,1)S(1)} %get-tuple-element.95), channel_id=1, source_target_pairs={{0,4},{1,5},{2,6},{3,7},{4,0},{5,1},{6,2},{7,3},{8,12},{9,13},{10,... | collective-permute-start | bytes 1179656 | tf_op jit(solution)/shard_map/ppermute | solution.py:292
  57.2 2.7 %collective-permute-start.11 = (bf16[2,2,3,32,256]{4,3,2,1,0:T(8,128)(2,1)S(1)}, bf16[2,2,3,32,256]{4,3,2,1,0:T(8,128)(2,1)S(1)}, u32[]{:S(2)}, u32[]{:S(2)}) collective-permute-start(bf16[2,2,3,32,256]{4,3,2,1,0:T(8,128)(2,1)S(1)} %get-tuple-element.79), channel_id=1, source_target_pairs={{0,3},{1,2},{2,1},{3,0},{4,7},{5,6},{6,5},{7,4},{8,11},{9,10},{10,... | collective-permute-start | bytes 589832 | tf_op jit(solution)/shard_map/ppermute | solution.py:292
  59.9 2.6 %collective-permute-start.12 = (bf16[2,2,3,32,256]{4,3,2,1,0:T(8,128)(2,1)S(1)}, bf16[2,2,3,32,256]{4,3,2,1,0:T(8,128)(2,1)S(1)}, u32[]{:S(2)}, u32[]{:S(2)}) collective-permute-start(bf16[2,2,3,32,256]{4,3,2,1,0:T(8,128)(2,1)S(1)} %get-tuple-element.80), channel_id=1, source_target_pairs={{0,4},{1,5},{2,6},{3,7},{4,0},{5,1},{6,2},{7,3},{8,12},{9,13},{10,... | collective-permute-start | bytes 589832 | tf_op jit(solution)/shard_map/ppermute | solution.py:292
  62.6 1.3 %collective-permute-done.6.got = bf16[4,2,3,32,256]{4,3,2,1,0:T(8,128)(2,1)S(1)} collective-permute-done((bf16[4,2,3,32,256]{4,3,2,1,0:T(8,128)(2,1)S(1)}, bf16[4,2,3,32,256]{4,3,2,1,0:T(8,128)(2,1)S(1)}, u32[]{:S(2)}, u32[]{:S(2)}) %collective-permute-start.6) | collective-permute-done | bytes 393248 | tf_op jit(solution)/shard_map/ppermute | solution.py:292
  63.9 1.1 %collective-permute-start.13 = (bf16[2,2,3,32,256]{4,3,2,1,0:T(8,128)(2,1)S(1)}, bf16[2,2,3,32,256]{4,3,2,1,0:T(8,128)(2,1)S(1)}, u32[]{:S(2)}, u32[]{:S(2)}) collective-permute-start(bf16[2,2,3,32,256]{4,3,2,1,0:T(8,128)(2,1)S(1)} %get-tuple-element.81), channel_id=1, source_target_pairs={{0,1},{1,0},{2,3},{3,2},{4,5},{5,4},{6,7},{7,6},{8,9},{9,8},{10,11... | collective-permute-start | bytes 589832 | tf_op jit(solution)/shard_map/ppermute | solution.py:292
  65.1 3.1 %collective-permute-done.15.got = bf16[4,2,3,32,256]{4,3,2,1,0:T(8,128)(2,1)S(1)} collective-permute-done((bf16[4,2,3,32,256]{4,3,2,1,0:T(8,128)(2,1)S(1)}, bf16[4,2,3,32,256]{4,3,2,1,0:T(8,128)(2,1)S(1)}, u32[]{:S(2)}, u32[]{:S(2)}) %collective-permute-start.15) | collective-permute-done | bytes 393248 | tf_op jit(solution)/shard_map/ppermute | solution.py:292
  68.2 0.9 collective-permute-start.7
  69.2 1.2 %collective-permute-start.16 = (bf16[2,2,3,32,256]{4,3,2,1,0:T(8,128)(2,1)S(1)}, bf16[2,2,3,32,256]{4,3,2,1,0:T(8,128)(2,1)S(1)}, u32[]{:S(2)}, u32[]{:S(2)}) collective-permute-start(bf16[2,2,3,32,256]{4,3,2,1,0:T(8,128)(2,1)S(1)} %get-tuple-element.89), channel_id=1, source_target_pairs={{0,4},{1,5},{2,6},{3,7},{4,0},{5,1},{6,2},{7,3},{8,12},{9,13},{10,... | collective-permute-start | bytes 589832 | tf_op jit(solution)/shard_map/ppermute | solution.py:292
  71.4 6.8 %collective-permute-done.19.got = bf16[2,2,3,32,256]{4,3,2,1,0:T(8,128)(2,1)S(1)} collective-permute-done((bf16[2,2,3,32,256]{4,3,2,1,0:T(8,128)(2,1)S(1)}, bf16[2,2,3,32,256]{4,3,2,1,0:T(8,128)(2,1)S(1)}, u32[]{:S(2)}, u32[]{:S(2)}) %collective-permute-start.19) | collective-permute-done | bytes 196640 | tf_op jit(solution)/shard_map/ppermute | solution.py:292
  78.2 2.0 %collective-permute-start.20 = (bf16[1,2,2,3,32,256]{5,4,3,2,1,0:T(8,128)(2,1)S(1)}, bf16[1,2,2,3,32,256]{5,4,3,2,1,0:T(8,128)(2,1)S(1)}, u32[]{:S(2)}, u32[]{:S(2)}) collective-permute-start(bf16[1,2,2,3,32,256]{5,4,3,2,1,0:T(8,128)(2,1)S(1)} %get-tuple-element.101), channel_id=1, source_target_pairs={{0,3},{1,2},{2,1},{3,0},{4,7},{5,6},{6,5},{7,4},{8,11},{9,10},{10,... | collective-permute-start | bytes 589832 | tf_op jit(solution)/shard_map/ppermute | solution.py:292
  80.4 1.7 %collective-permute-start.14 = (bf16[1,2,2,3,32,256]{5,4,3,2,1,0:T(8,128)(2,1)S(1)}, bf16[1,2,2,3,32,256]{5,4,3,2,1,0:T(8,128)(2,1)S(1)}, u32[]{:S(2)}, u32[]{:S(2)}) collective-permute-start(bf16[1,2,2,3,32,256]{5,4,3,2,1,0:T(8,128)(2,1)S(1)} %get-tuple-element.85), channel_id=1, source_target_pairs={{0,4},{1,5},{2,6},{3,7},{4,0},{5,1},{6,2},{7,3},{8,12},{9,13},{10,... | collective-permute-start | bytes 589832 | tf_op jit(solution)/shard_map/ppermute | solution.py:292
  82.1 2.2 %late_3.1 = bf16[2,512,256]{2,1,0:T(8,128)(2,1)} custom-call(bf16[36,256,256]{2,1,0:T(8,128)(2,1)S(1)} %bitcast.28, bf16[512,256]{1,0:T(8,128)(2,1)S(1)} %early_0_3.1.g1_zero.refs_2_, bf16[512,256]{1,0:T(8,128)(2,1)S(1)} %early_1_3.1.g1_one.refs_3_), custom_call_target="tpu_custom_call" | custom-call | flops 1207959552 | bytes 1024 | tf_op jit(solution)/shard_map/late_3/pallas_call | solution.py:51
  84.3 0.9 collective-permute-done.20.refs_5_
  85.2 0.8 collective-permute-done.17.refs_3_
  86.0 1.7 %collective-permute-done.14.refs_1_ = bf16[1,2,2,3,32,256]{5,4,3,2,1,0:T(8,128)(2,1)S(1)} collective-permute-done((bf16[1,2,2,3,32,256]{5,4,3,2,1,0:T(8,128)(2,1)S(1)}, bf16[1,2,2,3,32,256]{5,4,3,2,1,0:T(8,128)(2,1)S(1)}, u32[]{:S(2)}, u32[]{:S(2)}) %collective-permute-start.14) | collective-permute-done | bytes 196640 | tf_op jit(solution)/shard_map/ppermute | solution.py:292
  87.7 1.2 %finish.1 = f32[2,2,9,32,256]{4,3,2,1,0:T(8,128)} custom-call(bf16[1,2,2,3,32,256]{5,4,3,2,1,0:T(8,128)(2,1)S(1)} %get-tuple-element.84.refs_0_, bf16[1,2,2,3,32,256]{5,4,3,2,1,0:T(8,128)(2,1)S(1)} %collective-permute-done.14.refs_1_, bf16[1,2,2,3,32,256]{5,4,3,2,1,0:T(8,128)(2,1)S(1)} %get-tuple-element.92.refs_2_, ...), custom_call_target="tpu_custom_call" | custom-call | flops 603979776 | bytes 1024 | tf_op jit(solution)/shard_map/finish/pallas_call | solution.py:51
  (42 shorter events, 3.0 us)
Async XLA Ops:
  0.6 3.5 %slice-start = ((s8[4718592]{0:T(1024)(128)(4,1)}), s8[4194304]{0:T(1024)(128)(4,1)S(1)}, s32[]{:S(2)}) async-start(s8[4718592]{0:T(1024)(128)(4,1)} %bitcast.12), calls=%async_computation | async-start | bytes 8388608
  0.6 0.8 copy-start.4
  1.5 2.7 %slice-start.1 = ((s8[4718592]{0:T(1024)(128)(4,1)}), s8[524288]{0:T(1024)(128)(4,1)S(1)}, s32[]{:S(2)}) async-start(s8[4718592]{0:T(1024)(128)(4,1)} %bitcast.12), calls=%async_computation.1 | async-start | bytes 1048576
  4.2 1.0 %copy-start.5 = (bf16[512,256]{1,0:T(8,128)(2,1)S(1)}, bf16[512,256]{1,0:T(8,128)(2,1)}, u32[]{:S(2)}) copy-start(bf16[512,256]{1,0:T(8,128)(2,1)} %get-tuple-element.52.mask) | copy-start | bytes 786436
  6.8 6.6 %collective-permute-start = (bf16[512,256]{1,0:T(8,128)(2,1)S(1)}, bf16[512,256]{1,0:T(8,128)(2,1)S(1)}, u32[]{:S(2)}, u32[]{:S(2)}) collective-permute-start(bf16[512,256]{1,0:T(8,128)(2,1)S(1)} %late_1_0.1.refs_1_), channel_id=1, source_target_pairs={{0,8},{16,24},{32,40},{48,56},{64,72},{80,88},{96,104},{112,120},{... | collective-permute-start | bytes 786440 | tf_op jit(solution)/shard_map/ppermute | solution.py:288
  7.7 5.7 %copy-start = (bf16[2,1,4,1,16,32,256]{6,5,4,3,2,1,0:T(8,128)(2,1)S(1)}, bf16[2,1,4,1,16,32,256]{6,5,4,3,2,1,0:T(8,128)(2,1)}, u32[]{:S(2)}) copy-start(bf16[2,1,4,1,16,32,256]{6,5,4,3,2,1,0:T(8,128)(2,1)} %param.10) | copy-start | bytes 6291460
  7.7 5.7 %copy-start.1 = (bf16[2,1,4,1,16,32,256]{6,5,4,3,2,1,0:T(8,128)(2,1)S(1)}, bf16[2,1,4,1,16,32,256]{6,5,4,3,2,1,0:T(8,128)(2,1)}, u32[]{:S(2)}) copy-start(bf16[2,1,4,1,16,32,256]{6,5,4,3,2,1,0:T(8,128)(2,1)} %param.11) | copy-start | bytes 6291460
  8.6 9.9 %collective-permute-start.2 = (bf16[512,256]{1,0:T(8,128)(2,1)S(1)}, bf16[512,256]{1,0:T(8,128)(2,1)S(1)}, u32[]{:S(2)}, u32[]{:S(2)}) collective-permute-start(bf16[512,256]{1,0:T(8,128)(2,1)S(1)} %late_0_0.1.refs_1_), channel_id=1, source_target_pairs={{8,16},{24,32},{40,48},{56,64},{72,80},{88,96},{104,112},{16,8},{3... | collective-permute-start | bytes 786440 | tf_op jit(solution)/shard_map/ppermute | solution.py:288
  14.4 4.1 %copy-start.3 = (bf16[3,1,16,32,256]{4,3,2,1,0:T(8,128)(2,1)S(1)}, bf16[3,1,16,32,256]{4,3,2,1,0:T(8,128)(2,1)}, u32[]{:S(2)}) copy-start(bf16[3,1,16,32,256]{4,3,2,1,0:T(8,128)(2,1)} %param.8) | copy-start | bytes 2359300
  15.2 9.8 %collective-permute-start.1 = (bf16[512,256]{1,0:T(8,128)(2,1)S(1)}, bf16[512,256]{1,0:T(8,128)(2,1)S(1)}, u32[]{:S(2)}, u32[]{:S(2)}) collective-permute-start(bf16[512,256]{1,0:T(8,128)(2,1)S(1)} %late_0_1.1.refs_5_), channel_id=1, source_target_pairs={{8,16},{24,32},{40,48},{56,64},{72,80},{88,96},{104,112},{16,8},{3... | collective-permute-start | bytes 786440 | tf_op jit(solution)/shard_map/ppermute | solution.py:288
  20.4 6.5 %collective-permute-start.4 = (bf16[512,256]{1,0:T(8,128)(2,1)S(1)}, bf16[512,256]{1,0:T(8,128)(2,1)S(1)}, u32[]{:S(2)}, u32[]{:S(2)}) collective-permute-start(bf16[512,256]{1,0:T(8,128)(2,1)S(1)} %late_1_1.1.refs_5_), channel_id=1, source_target_pairs={{0,8},{16,24},{32,40},{48,56},{64,72},{80,88},{96,104},{112,120},{... | collective-permute-start | bytes 786440 | tf_op jit(solution)/shard_map/ppermute | solution.py:288
  27.9 4.5 %copy-start.2 = (bf16[2,1,4,1,16,32,256]{6,5,4,3,2,1,0:T(8,128)(2,1)S(1)}, bf16[2,1,4,1,16,32,256]{6,5,4,3,2,1,0:T(8,128)(2,1)}, u32[]{:S(2)}) copy-start(bf16[2,1,4,1,16,32,256]{6,5,4,3,2,1,0:T(8,128)(2,1)} %param.9) | copy-start | bytes 6291460
  28.8 9.8 %collective-permute-start.5 = (bf16[512,256]{1,0:T(8,128)(2,1)S(1)}, bf16[512,256]{1,0:T(8,128)(2,1)S(1)}, u32[]{:S(2)}, u32[]{:S(2)}) collective-permute-start(bf16[512,256]{1,0:T(8,128)(2,1)S(1)} %late_0_2.1.refs_6_), channel_id=1, source_target_pairs={{8,16},{24,32},{40,48},{56,64},{72,80},{88,96},{104,112},{16,8},{3... | collective-permute-start | bytes 786440 | tf_op jit(solution)/shard_map/ppermute | solution.py:288
  32.3 6.3 %collective-permute-start.3 = (bf16[512,256]{1,0:T(8,128)(2,1)S(1)}, bf16[512,256]{1,0:T(8,128)(2,1)S(1)}, u32[]{:S(2)}, u32[]{:S(2)}) collective-permute-start(bf16[512,256]{1,0:T(8,128)(2,1)S(1)} %late_1_2.1.refs_7_), channel_id=1, source_target_pairs={{0,8},{16,24},{32,40},{48,56},{64,72},{80,88},{96,104},{112,120},{... | collective-permute-start | bytes 786440 | tf_op jit(solution)/shard_map/ppermute | solution.py:288
  42.1 13.9 %collective-permute-start.8 = (bf16[4,2,3,32,256]{4,3,2,1,0:T(8,128)(2,1)S(1)}, bf16[4,2,3,32,256]{4,3,2,1,0:T(8,128)(2,1)S(1)}, u32[]{:S(2)}, u32[]{:S(2)}) collective-permute-start(bf16[4,2,3,32,256]{4,3,2,1,0:T(8,128)(2,1)S(1)} %get-tuple-element.73), channel_id=1, source_target_pairs={{0,1},{1,0},{2,3},{3,2},{4,5},{5,4},{6,7},{7,6},{8,9},{9,8},{10,11... | collective-permute-start | bytes 1179656 | tf_op jit(solution)/shard_map/ppermute | solution.py:292
  44.1 12.8 %collective-permute-start.9 = (bf16[4,2,3,32,256]{4,3,2,1,0:T(8,128)(2,1)S(1)}, bf16[4,2,3,32,256]{4,3,2,1,0:T(8,128)(2,1)S(1)}, u32[]{:S(2)}, u32[]{:S(2)}) collective-permute-start(bf16[4,2,3,32,256]{4,3,2,1,0:T(8,128)(2,1)S(1)} %get-tuple-element.74), channel_id=1, source_target_pairs={{0,3},{1,2},{2,1},{3,0},{4,7},{5,6},{6,5},{7,4},{8,11},{9,10},{10,... | collective-permute-start | bytes 1179656 | tf_op jit(solution)/shard_map/ppermute | solution.py:292
  46.6 10.3 %collective-permute-start.10 = (bf16[4,2,3,32,256]{4,3,2,1,0:T(8,128)(2,1)S(1)}, bf16[4,2,3,32,256]{4,3,2,1,0:T(8,128)(2,1)S(1)}, u32[]{:S(2)}, u32[]{:S(2)}) collective-permute-start(bf16[4,2,3,32,256]{4,3,2,1,0:T(8,128)(2,1)S(1)} %get-tuple-element.75), channel_id=1, source_target_pairs={{0,4},{1,5},{2,6},{3,7},{4,0},{5,1},{6,2},{7,3},{8,12},{9,13},{10,... | collective-permute-start | bytes 1179656 | tf_op jit(solution)/shard_map/ppermute | solution.py:292
  54.3 9.6 %collective-permute-start.6 = (bf16[4,2,3,32,256]{4,3,2,1,0:T(8,128)(2,1)S(1)}, bf16[4,2,3,32,256]{4,3,2,1,0:T(8,128)(2,1)S(1)}, u32[]{:S(2)}, u32[]{:S(2)}) collective-permute-start(bf16[4,2,3,32,256]{4,3,2,1,0:T(8,128)(2,1)S(1)} %get-tuple-element.67), channel_id=1, source_target_pairs={{0,1},{1,0},{2,3},{3,2},{4,5},{5,4},{6,7},{7,6},{8,9},{9,8},{10,11... | collective-permute-start | bytes 1179656 | tf_op jit(solution)/shard_map/ppermute | solution.py:292
  55.4 12.8 %collective-permute-start.15 = (bf16[4,2,3,32,256]{4,3,2,1,0:T(8,128)(2,1)S(1)}, bf16[4,2,3,32,256]{4,3,2,1,0:T(8,128)(2,1)S(1)}, u32[]{:S(2)}, u32[]{:S(2)}) collective-permute-start(bf16[4,2,3,32,256]{4,3,2,1,0:T(8,128)(2,1)S(1)} %get-tuple-element.87), channel_id=1, source_target_pairs={{0,3},{1,2},{2,1},{3,0},{4,7},{5,6},{6,5},{7,4},{8,11},{9,10},{10,... | collective-permute-start | bytes 1179656 | tf_op jit(solution)/shard_map/ppermute | solution.py:292
  56.0 13.2 %collective-permute-start.18 = (bf16[4,2,3,32,256]{4,3,2,1,0:T(8,128)(2,1)S(1)}, bf16[4,2,3,32,256]{4,3,2,1,0:T(8,128)(2,1)S(1)}, u32[]{:S(2)}, u32[]{:S(2)}) collective-permute-start(bf16[4,2,3,32,256]{4,3,2,1,0:T(8,128)(2,1)S(1)} %get-tuple-element.95), channel_id=1, source_target_pairs={{0,4},{1,5},{2,6},{3,7},{4,0},{5,1},{6,2},{7,3},{8,12},{9,13},{10,... | collective-permute-start | bytes 1179656 | tf_op jit(solution)/shard_map/ppermute | solution.py:292
  57.2 13.3 %collective-permute-start.11 = (bf16[2,2,3,32,256]{4,3,2,1,0:T(8,128)(2,1)S(1)}, bf16[2,2,3,32,256]{4,3,2,1,0:T(8,128)(2,1)S(1)}, u32[]{:S(2)}, u32[]{:S(2)}) collective-permute-start(bf16[2,2,3,32,256]{4,3,2,1,0:T(8,128)(2,1)S(1)} %get-tuple-element.79), channel_id=1, source_target_pairs={{0,3},{1,2},{2,1},{3,0},{4,7},{5,6},{6,5},{7,4},{8,11},{9,10},{10,... | collective-permute-start | bytes 589832 | tf_op jit(solution)/shard_map/ppermute | solution.py:292
  59.9 11.3 %collective-permute-start.12 = (bf16[2,2,3,32,256]{4,3,2,1,0:T(8,128)(2,1)S(1)}, bf16[2,2,3,32,256]{4,3,2,1,0:T(8,128)(2,1)S(1)}, u32[]{:S(2)}, u32[]{:S(2)}) collective-permute-start(bf16[2,2,3,32,256]{4,3,2,1,0:T(8,128)(2,1)S(1)} %get-tuple-element.80), channel_id=1, source_target_pairs={{0,4},{1,5},{2,6},{3,7},{4,0},{5,1},{6,2},{7,3},{8,12},{9,13},{10,... | collective-permute-start | bytes 589832 | tf_op jit(solution)/shard_map/ppermute | solution.py:292
  63.9 7.4 %collective-permute-start.13 = (bf16[2,2,3,32,256]{4,3,2,1,0:T(8,128)(2,1)S(1)}, bf16[2,2,3,32,256]{4,3,2,1,0:T(8,128)(2,1)S(1)}, u32[]{:S(2)}, u32[]{:S(2)}) collective-permute-start(bf16[2,2,3,32,256]{4,3,2,1,0:T(8,128)(2,1)S(1)} %get-tuple-element.81), channel_id=1, source_target_pairs={{0,1},{1,0},{2,3},{3,2},{4,5},{5,4},{6,7},{7,6},{8,9},{9,8},{10,11... | collective-permute-start | bytes 589832 | tf_op jit(solution)/shard_map/ppermute | solution.py:292
  68.2 12.1 %collective-permute-start.7 = (bf16[2,2,3,32,256]{4,3,2,1,0:T(8,128)(2,1)S(1)}, bf16[2,2,3,32,256]{4,3,2,1,0:T(8,128)(2,1)S(1)}, u32[]{:S(2)}, u32[]{:S(2)}) collective-permute-start(bf16[2,2,3,32,256]{4,3,2,1,0:T(8,128)(2,1)S(1)} %get-tuple-element.69), channel_id=1, source_target_pairs={{0,3},{1,2},{2,1},{3,0},{4,7},{5,6},{6,5},{7,4},{8,11},{9,10},{10,... | collective-permute-start | bytes 589832 | tf_op jit(solution)/shard_map/ppermute | solution.py:292
  69.2 11.0 %collective-permute-start.16 = (bf16[2,2,3,32,256]{4,3,2,1,0:T(8,128)(2,1)S(1)}, bf16[2,2,3,32,256]{4,3,2,1,0:T(8,128)(2,1)S(1)}, u32[]{:S(2)}, u32[]{:S(2)}) collective-permute-start(bf16[2,2,3,32,256]{4,3,2,1,0:T(8,128)(2,1)S(1)} %get-tuple-element.89), channel_id=1, source_target_pairs={{0,4},{1,5},{2,6},{3,7},{4,0},{5,1},{6,2},{7,3},{8,12},{9,13},{10,... | collective-permute-start | bytes 589832 | tf_op jit(solution)/shard_map/ppermute | solution.py:292
  70.5 7.7 %collective-permute-start.19 = (bf16[2,2,3,32,256]{4,3,2,1,0:T(8,128)(2,1)S(1)}, bf16[2,2,3,32,256]{4,3,2,1,0:T(8,128)(2,1)S(1)}, u32[]{:S(2)}, u32[]{:S(2)}) collective-permute-start(bf16[2,2,3,32,256]{4,3,2,1,0:T(8,128)(2,1)S(1)} %get-tuple-element.97), channel_id=1, source_target_pairs={{0,1},{1,0},{2,3},{3,2},{4,5},{5,4},{6,7},{7,6},{8,9},{9,8},{10,11... | collective-permute-start | bytes 589832 | tf_op jit(solution)/shard_map/ppermute | solution.py:292
  78.2 7.0 %collective-permute-start.20 = (bf16[1,2,2,3,32,256]{5,4,3,2,1,0:T(8,128)(2,1)S(1)}, bf16[1,2,2,3,32,256]{5,4,3,2,1,0:T(8,128)(2,1)S(1)}, u32[]{:S(2)}, u32[]{:S(2)}) collective-permute-start(bf16[1,2,2,3,32,256]{5,4,3,2,1,0:T(8,128)(2,1)S(1)} %get-tuple-element.101), channel_id=1, source_target_pairs={{0,3},{1,2},{2,1},{3,0},{4,7},{5,6},{6,5},{7,4},{8,11},{9,10},{10,... | collective-permute-start | bytes 589832 | tf_op jit(solution)/shard_map/ppermute | solution.py:292
  80.3 5.8 %collective-permute-start.17 = (bf16[1,2,2,3,32,256]{5,4,3,2,1,0:T(8,128)(2,1)S(1)}, bf16[1,2,2,3,32,256]{5,4,3,2,1,0:T(8,128)(2,1)S(1)}, u32[]{:S(2)}, u32[]{:S(2)}) collective-permute-start(bf16[1,2,2,3,32,256]{5,4,3,2,1,0:T(8,128)(2,1)S(1)} %get-tuple-element.93), channel_id=1, source_target_pairs={{0,1},{1,0},{2,3},{3,2},{4,5},{5,4},{6,7},{7,6},{8,9},{9,8},{10,11... | collective-permute-start | bytes 589832 | tf_op jit(solution)/shard_map/ppermute | solution.py:292
  80.4 7.3 %collective-permute-start.14 = (bf16[1,2,2,3,32,256]{5,4,3,2,1,0:T(8,128)(2,1)S(1)}, bf16[1,2,2,3,32,256]{5,4,3,2,1,0:T(8,128)(2,1)S(1)}, u32[]{:S(2)}, u32[]{:S(2)}) collective-permute-start(bf16[1,2,2,3,32,256]{5,4,3,2,1,0:T(8,128)(2,1)S(1)} %get-tuple-element.85), channel_id=1, source_target_pairs={{0,4},{1,5},{2,6},{3,7},{4,0},{5,1},{6,2},{7,3},{8,12},{9,13},{10,... | collective-permute-start | bytes 589832 | tf_op jit(solution)/shard_map/ppermute | solution.py:292

commit v2 on v1

--- a/solution.py
+++ b/solution.py
@@ -16,7 +16,7 @@
 DP = 8
 COST = 2 * 512 * 9 * 256 * 256
 FOLD_COST = 16
-PREPARE_MIB = 53
+PREPARE_KIB = 54016
 SHARE = CH // DP
 BF = jnp.bfloat16
 F32 = jnp.float32
@@ -135,7 +135,7 @@
             out_specs=[VM] * 4,
         ),
         out_shape=[FIELD] * 4,
-        compiler_params=pltpu.CompilerParams(vmem_limit_bytes=PREPARE_MIB << 20),
+        compiler_params=pltpu.CompilerParams(vmem_limit_bytes=PREPARE_KIB << 10),
         cost_estimate=pl.CostEstimate(flops=1, bytes_accessed=1024, transcendentals=0),
         name="prepare",
     )(table, pending, pending, pre2, pre2, pre1, pre1)
@@ -177,8 +177,9 @@
 
 
 def wgrad_kernel(which, role, table, saved, *refs):
-    fields, new, wins = refs[:2], refs[2], refs[3:]
-    xs = [left_side(which, saved, slot_of(table, role, tick)) for tick in range(2)]
+    ticks = len(refs) // 2
+    fields, new, wins = refs[:ticks], refs[ticks], refs[ticks + 1 :]
+    xs = [left_side(which, saved, slot_of(table, role, tick)) for tick in range(ticks)]
     for k, term in tap_grads(wins, xs, [field[...].astype(F32) for field in fields]):
         new[k] = term
 
@@ -207,18 +208,16 @@
 
 
 def last_two_kernel(table, pre1, pre2, objective, *refs):
-    given, befores, olds = refs[:4], refs[4:6], refs[6:8]
-    sends, keeps, g2s = refs[8:11], refs[11:14], refs[14:16]
-    wins, staged = refs[16:20], refs[20:22]
+    given, olds = refs[:4], refs[4:6]
+    sends, keeps, g2s = refs[6:9], refs[9:12], refs[12:14]
+    wins, staged = refs[14:16], refs[16:18]
     tick = TICKS - 1
     for role in range(2):
         slot = slot_of(table, role, tick)
         g2 = add_up(role, tick, given[role], given[3 - role], objective)
         g2 = jnp.where(pre2[slot] > 0, g2, 0.0)
         g2s[role][...] = g2.astype(BF)
-        xs = [left_side(1, pre1, slot_of(table, role, tick - 1)), left_side(1, pre1, slot)]
-        fields = [befores[role][...].astype(F32), g2]
-        for k, term in tap_grads(wins[2 * role : 2 * role + 2], xs, fields):
+        for k, term in tap_grads(wins[role : role + 1], [left_side(1, pre1, slot)], [g2]):
             staged[role][k] = olds[role][k] + term
             put_shares(staged[role], k, sends, keeps, role)
 
@@ -255,7 +254,7 @@
     send[...] = total[half:].astype(BF)
 
 
-def fold_two_kernel(*refs):
+def fold_kernel(*refs):
     for o in range(3):
         fold_in(*refs[o::3])
 
@@ -317,10 +316,11 @@
             call(
                 functools.partial(wgrad_kernel, which, role),
                 f"wgrad{which + 1}_{role}",
-                (table, saved, fields[0][role], fields[1][role]),
+                (table, saved, *[field[role] for field in fields]),
                 SUMS,
-                scratch=windows * 2,
-                ops=2,
+                scratch=windows * len(fields),
+                mib=12,
+                ops=len(fields),
             )
             for role in range(2)
         ]
@@ -347,7 +347,7 @@
                     (table, pre1, pre2, taps, *given),
                     (FIELD, FIELD),
                     scratch=windows,
-                    after=sums2 if tick == 2 else (),
+                    after=sums1 if tick == 2 else (),
                 )
             out = call(functools.partial(late_kernel, role), f"late_{role}_{tick}", (taps, g1), FIELD, scratch=windows)
             g2s.append(g2)
@@ -358,20 +358,19 @@
         all_g2s.append(g2s)
         all_g1s.append(g1s)
         if tick == 1:
-            sums2 = early_sums(1, pre1, all_g2s)
             sums1 = early_sums(0, entries, all_g1s)
+    sums2 = early_sums(1, pre1, all_g2s)
 
     part = jax.ShapeDtypeStruct((4, 2, 3, SHARE, CH), BF)
     staged = [pltpu.VMEM((9, CH, CH), F32)] * 2
     res = call(
         last_two_kernel,
         "last_two",
-        (table, pre1, pre2, objective, gots[1], gots[0], *outs, *g2s, *sums2),
+        (table, pre1, pre2, objective, gots[1], gots[0], *outs, *sums2),
         (part,) * 6 + (FIELD,) * 2,
-        scratch=windows * 4 + staged,
+        scratch=windows * 2 + staged,
         mib=16,
-        ops=4,
-        after=sums1,
+        ops=2,
     )
     keeps2, g2s = res[3:6], res[6:8]
     gots2 = [exchange(res[o], ORDERS[o][0]) for o in range(3)]
@@ -408,7 +407,7 @@
     parts = []
     part2 = jax.ShapeDtypeStruct((2, 2, 3, SHARE, CH), BF)
     part3 = jax.ShapeDtypeStruct((1, 2, 2, 3, SHARE, CH), BF)
-    res = call(fold_two_kernel, "fold_two", (*keeps2, *gots2), (part2,) * 6, ops=FOLD_COST)
+    res = call(fold_kernel, "fold_two", (*keeps2, *gots2), (part2,) * 6, ops=FOLD_COST)
     gots2 = [exchange(res[o], ORDERS[o][1]) for o in range(3)]
     begun = call(fold_two_last_kernel, "fold_two_last", (*res[3:6], *gots2), (part3,) * 6, ops=FOLD_COST)
     for o in range(3):

time: 89.1 us -> 87.3 us (0.980); the launches traced: 88.8 us -> 85.8 us
  starting transfers between devices: 34.5 us -> 33 us
    ppermute x6, waiting for transfers between devices: 4.42 us -> 2.22 us  [relay(): return lax.ppermute(block, 'section', pairs + [(b, a) for a, b in pairs])]
    ppermute x15, starting transfers between devices: 22.7 us -> 20.8 us  [exchange(): return lax.ppermute(block, 'dp', PAIRS[step])]
    ppermute x15, waiting for transfers between devices: 14.7 us -> 16.3 us  [exchange(): return lax.ppermute(block, 'dp', PAIRS[step])]
    unnamed x16 -> x14, local copies, waits for them, and re-layouts: 1.8 us -> 1.33 us
  transfers between devices with their start and end apart: 21 -> 21, of which waited for: 10 -> 11; matrix products, arithmetic and copies ran while one was open for 0% -> 0% of each run, Pallas kernels for 24% -> 27%
where the time goes in v2:
time: 87.3 us; the launch traced here: 85.8 us
  starting transfers between devices  33 us (38%)
  Pallas kernels  32 us (37%)
  waiting for transfers between devices  18.5 us (21%)
  local copies, waits for them, and re-layouts  1.33 us (2%)
  between operations  0.99 us (1%)
    pallas_call x30, Pallas kernels, call(): pl.pallas_call(body if after else kernel, out_shape=outs, in_specs=[VM] *...  29.9 us
    ppermute x15, starting transfers between devices, exchange(): return lax.ppermute(block, 'dp', PAIRS[step])  20.8 us
    ppermute x15, waiting for transfers between devices, exchange(): return lax.ppermute(block, 'dp', PAIRS[step])  16.3 us
    ppermute x6, starting transfers between devices, relay(): return lax.ppermute(block, 'section', pairs + [(b, a) for a, b in pairs])  12.2 us
    ppermute x6, waiting for transfers between devices, relay(): return lax.ppermute(block, 'section', pairs + [(b, a) for a, b in pairs])  2.22 us
    pallas_call x1, Pallas kernels, prepare(): pl.pallas_call(prepare_kernel, grid_spec=pltpu.PrefetchScalarGridSpec(num...  2.04 us
  transfers between devices with their start and end apart: 21, of which 11 were waited for; matrix products, arithmetic and copies ran while one was open for 0% of the time, Pallas kernels for 27%

profile of v2, /device:TPU:8, one launch (start us, length us, event | category | flops | bytes accessed | tf_op | source)
XLA Modules:
  0.0 85.8 jit_solution(15924113703179439302)
XLA Ops:
  0.7 0.8 copy-done.4
  1.5 2.0 %prepare.1 = (bf16[512,256]{1,0:T(8,128)(2,1)S(1)}, bf16[512,256]{1,0:T(8,128)(2,1)S(1)}, bf16[512,256]{1,0:T(8,128)(2,1)S(1)}, bf16[512,256]{1,0:T(8,128)(2,1)S(1)}) custom-call(s32[4,32]{1,0:T(4,128)S(1)} %copy-done.4, bf16[2,512,256]{2,1,0:T(8,128)(2,1)} %bitcast.53, bf16[2,512,256]{2,1,0:T(8,128)(2,1)} %bitcast.54, bf16[8,512,256]{2,1,0:T(8,128)(2,1)} %bitcast.40, ...), custom_call_target="tpu_custom_call" | custom-call | flops 1 | bytes 1024 | tf_op jit(solution)/shard_map/prepare/pallas_call | solution.py:129
  3.5 0.8 early_1_0.1.g1.refs_0_
  4.4 0.8 late_1_0.1.refs_1_
  5.3 0.8 early_0_0.1.refs_0_.g1
  6.2 0.8 late_0_0.1.refs_1_
  7.0 4.8 %collective-permute-start.2 = (bf16[512,256]{1,0:T(8,128)(2,1)S(1)}, bf16[512,256]{1,0:T(8,128)(2,1)S(1)}, u32[]{:S(2)}, u32[]{:S(2)}) collective-permute-start(bf16[512,256]{1,0:T(8,128)(2,1)S(1)} %late_0_0.1.refs_1_), channel_id=1, source_target_pairs={{8,16},{24,32},{40,48},{56,64},{72,80},{88,96},{104,112},{16,8},{3... | collective-permute-start | bytes 786440 | tf_op jit(solution)/shard_map/ppermute | solution.py:287
  11.8 1.0 %early_0_1.1 = (bf16[512,256]{1,0:T(8,128)(2,1)S(1)}, bf16[512,256]{1,0:T(8,128)(2,1)S(1)}) custom-call(s32[4,32]{1,0:T(4,128)S(1)} %copy-done.4, bf16[8,512,256]{2,1,0:T(8,128)(2,1)S(1)} %bitcast.31, bf16[8,512,256]{2,1,0:T(8,128)(2,1)S(1)} %bitcast.42, bf16[36,256,256]{2,1,0:T(8,128)(2,1)S(1)} %bitcast.18, ...), custom_call_target="tpu_custom_call" | custom-call | flops 603979776 | bytes 1024 | tf_op jit(solution)/shard_map/early_0_1/pallas_call | solution.py:51
  12.8 0.8 late_0_1.1.refs_5_
  13.7 3.0 %collective-permute-start.1 = (bf16[512,256]{1,0:T(8,128)(2,1)S(1)}, bf16[512,256]{1,0:T(8,128)(2,1)S(1)}, u32[]{:S(2)}, u32[]{:S(2)}) collective-permute-start(bf16[512,256]{1,0:T(8,128)(2,1)S(1)} %late_0_1.1.refs_5_), channel_id=1, source_target_pairs={{8,16},{24,32},{40,48},{56,64},{72,80},{88,96},{104,112},{16,8},{3... | collective-permute-start | bytes 786440 | tf_op jit(solution)/shard_map/ppermute | solution.py:287
  16.9 1.0 %early_1_1.1 = (bf16[512,256]{1,0:T(8,128)(2,1)S(1)}, bf16[512,256]{1,0:T(8,128)(2,1)S(1)}) custom-call(s32[4,32]{1,0:T(4,128)S(1)} %copy-done.4, bf16[8,512,256]{2,1,0:T(8,128)(2,1)S(1)} %bitcast.32, bf16[8,512,256]{2,1,0:T(8,128)(2,1)S(1)} %bitcast.43, bf16[36,256,256]{2,1,0:T(8,128)(2,1)S(1)} %bitcast.20, ...), custom_call_target="tpu_custom_call" | custom-call | flops 603979776 | bytes 1024 | tf_op jit(solution)/shard_map/early_1_1/pallas_call | solution.py:51
  18.0 0.8 late_1_1.1.refs_5_
  19.6 1.6 %wgrad1_1.1.refs_8_.refs_7_.refs_5_ = f32[9,256,256]{2,1,0:T(8,128)S(1)} custom-call(s32[4,32]{1,0:T(4,128)S(1)} %copy-done.4, bf16[8,512,256]{2,1,0:T(8,128)(2,1)S(1)} %bitcast.47, bf16[512,256]{1,0:T(8,128)(2,1)S(1)} %early_1_0.1.g1.refs_0_, bf16[512,256]{1,0:T(8,128)(2,1)S(1)} %get-tuple-element.57.refs_1_.g1), custom_call_target="tpu_custom_call" | custom-call | flops 1207959552 | bytes 1024 | tf_op jit(solution)/shard_map/wgrad1_1/pallas_call | solution.py:51
  21.1 1.6 %wgrad1_0.1.refs_7_.refs_6_.refs_4_ = f32[9,256,256]{2,1,0:T(8,128)S(1)} custom-call(s32[4,32]{1,0:T(4,128)S(1)} %copy-done.4, bf16[8,512,256]{2,1,0:T(8,128)(2,1)S(1)} %bitcast.48, bf16[512,256]{1,0:T(8,128)(2,1)S(1)} %early_0_0.1.refs_0_.g1, bf16[512,256]{1,0:T(8,128)(2,1)S(1)} %get-tuple-element.54.g1.refs_1_), custom_call_target="tpu_custom_call" | custom-call | flops 1207959552 | bytes 1024 | tf_op jit(solution)/shard_map/wgrad1_0/pallas_call | solution.py:51
  22.7 0.7 collective-permute-done.1.refs_4_
  23.5 1.0 %early_1_2.1 = (bf16[512,256]{1,0:T(8,128)(2,1)S(1)}, bf16[512,256]{1,0:T(8,128)(2,1)S(1)}) custom-call(s32[4,32]{1,0:T(4,128)S(1)} %copy-done.4, bf16[8,512,256]{2,1,0:T(8,128)(2,1)S(1)} %bitcast.33, bf16[8,512,256]{2,1,0:T(8,128)(2,1)S(1)} %bitcast.44, bf16[36,256,256]{2,1,0:T(8,128)(2,1)S(1)} %bitcast.22, ...), custom_call_target="tpu_custom_call" | custom-call | flops 603979776 | bytes 1024 | tf_op jit(solution)/shard_map/early_1_2/pallas_call | solution.py:51
  24.5 0.8 late_1_2.1.refs_3_
  25.3 1.0 %early_0_2.1 = (bf16[512,256]{1,0:T(8,128)(2,1)S(1)}, bf16[512,256]{1,0:T(8,128)(2,1)S(1)}) custom-call(s32[4,32]{1,0:T(4,128)S(1)} %copy-done.4, bf16[8,512,256]{2,1,0:T(8,128)(2,1)S(1)} %bitcast.34, bf16[8,512,256]{2,1,0:T(8,128)(2,1)S(1)} %bitcast.45, bf16[36,256,256]{2,1,0:T(8,128)(2,1)S(1)} %bitcast.24, ...), custom_call_target="tpu_custom_call" | custom-call | flops 603979776 | bytes 1024 | tf_op jit(solution)/shard_map/early_0_2/pallas_call | solution.py:51
  26.3 0.8 late_0_2.1.refs_2_
  27.2 3.9 %collective-permute-start.5 = (bf16[512,256]{1,0:T(8,128)(2,1)S(1)}, bf16[512,256]{1,0:T(8,128)(2,1)S(1)}, u32[]{:S(2)}, u32[]{:S(2)}) collective-permute-start(bf16[512,256]{1,0:T(8,128)(2,1)S(1)} %late_0_2.1.refs_2_), channel_id=1, source_target_pairs={{8,16},{24,32},{40,48},{56,64},{72,80},{88,96},{104,112},{16,8},{3... | collective-permute-start | bytes 786440 | tf_op jit(solution)/shard_map/ppermute | solution.py:287
  31.2 2.3 %wgrad2_1.1.refs_5_ = f32[9,256,256]{2,1,0:T(8,128)S(1)} custom-call(s32[4,32]{1,0:T(4,128)S(1)} %copy-done.4, bf16[8,512,256]{2,1,0:T(8,128)(2,1)S(1)} %bitcast.35, bf16[512,256]{1,0:T(8,128)(2,1)S(1)} %get-tuple-element.53.g2.refs_0_, bf16[512,256]{1,0:T(8,128)(2,1)S(1)} %get-tuple-element.62.refs_1_, bf16[512,256]{1,0:T(8,128)(2,1)S(1)} %get-tuple-element.63.refs_2_), custom_call_target="tpu_custom_call" | custom-call | flops 1811939328 | bytes 1024 | tf_op jit(solution)/shard_map/wgrad2_1/pallas_call | solution.py:51
  33.5 2.3 %wgrad2_0.1.refs_4_ = f32[9,256,256]{2,1,0:T(8,128)S(1)} custom-call(s32[4,32]{1,0:T(4,128)S(1)} %copy-done.4, bf16[8,512,256]{2,1,0:T(8,128)(2,1)S(1)} %bitcast.36, bf16[512,256]{1,0:T(8,128)(2,1)S(1)} %get-tuple-element.56.g2.refs_0_, bf16[512,256]{1,0:T(8,128)(2,1)S(1)} %get-tuple-element.60.refs_1_, bf16[512,256]{1,0:T(8,128)(2,1)S(1)} %get-tuple-element.61.refs_2_), custom_call_target="tpu_custom_call" | custom-call | flops 1811939328 | bytes 1024 | tf_op jit(solution)/shard_map/wgrad2_0/pallas_call | solution.py:51
  35.7 1.2 %collective-permute-done.5.refs_1_ = bf16[512,256]{1,0:T(8,128)(2,1)S(1)} collective-permute-done((bf16[512,256]{1,0:T(8,128)(2,1)S(1)}, bf16[512,256]{1,0:T(8,128)(2,1)S(1)}, u32[]{:S(2)}, u32[]{:S(2)}) %collective-permute-start.5) | collective-permute-done | bytes 262176 | tf_op jit(solution)/shard_map/ppermute | solution.py:287
  37.0 2.3 %last_two.1 = (bf16[4,2,3,32,256]{4,3,2,1,0:T(8,128)(2,1)S(1)}, bf16[4,2,3,32,256]{4,3,2,1,0:T(8,128)(2,1)S(1)}, bf16[4,2,3,32,256]{4,3,2,1,0:T(8,128)(2,1)S(1)}...) custom-call(s32[4,32]{1,0:T(4,128)S(1)} %copy-done.4, ...), custom_call_target="tpu_custom_call" | custom-call | flops 1207959552 | bytes 1024 | tf_op jit(solution)/shard_map/last_two/pallas_call | solution.py:51
  39.3 2.0 %collective-permute-start.8 = (bf16[4,2,3,32,256]{4,3,2,1,0:T(8,128)(2,1)S(1)}, bf16[4,2,3,32,256]{4,3,2,1,0:T(8,128)(2,1)S(1)}, u32[]{:S(2)}, u32[]{:S(2)}) collective-permute-start(bf16[4,2,3,32,256]{4,3,2,1,0:T(8,128)(2,1)S(1)} %get-tuple-element.73), channel_id=1, source_target_pairs={{0,1},{1,0},{2,3},{3,2},{4,5},{5,4},{6,7},{7,6},{8,9},{9,8},{10,11... | collective-permute-start | bytes 1179656 | tf_op jit(solution)/shard_map/ppermute | solution.py:291
  41.3 2.5 %collective-permute-start.9 = (bf16[4,2,3,32,256]{4,3,2,1,0:T(8,128)(2,1)S(1)}, bf16[4,2,3,32,256]{4,3,2,1,0:T(8,128)(2,1)S(1)}, u32[]{:S(2)}, u32[]{:S(2)}) collective-permute-start(bf16[4,2,3,32,256]{4,3,2,1,0:T(8,128)(2,1)S(1)} %get-tuple-element.74), channel_id=1, source_target_pairs={{0,3},{1,2},{2,1},{3,0},{4,7},{5,6},{6,5},{7,4},{8,11},{9,10},{10,... | collective-permute-start | bytes 1179656 | tf_op jit(solution)/shard_map/ppermute | solution.py:291
  43.9 2.6 %collective-permute-start.10 = (bf16[4,2,3,32,256]{4,3,2,1,0:T(8,128)(2,1)S(1)}, bf16[4,2,3,32,256]{4,3,2,1,0:T(8,128)(2,1)S(1)}, u32[]{:S(2)}, u32[]{:S(2)}) collective-permute-start(bf16[4,2,3,32,256]{4,3,2,1,0:T(8,128)(2,1)S(1)} %get-tuple-element.75), channel_id=1, source_target_pairs={{0,4},{1,5},{2,6},{3,7},{4,0},{5,1},{6,2},{7,3},{8,12},{9,13},{10,... | collective-permute-start | bytes 1179656 | tf_op jit(solution)/shard_map/ppermute | solution.py:291
  46.4 0.8 early_0_3.1.g1_zero.refs_2_
  47.3 0.8 early_1_3.1.g1_one.refs_3_
  48.1 3.4 %last_one.1 = (bf16[4,2,3,32,256]{4,3,2,1,0:T(8,128)(2,1)S(1)}, bf16[4,2,3,32,256]{4,3,2,1,0:T(8,128)(2,1)S(1)}, bf16[4,2,3,32,256]{4,3,2,1,0:T(8,128)(2,1)S(1)}...) custom-call(s32[4,32]{1,0:T(4,128)S(1)} %copy-done.4, ...), custom_call_target="tpu_custom_call" | custom-call | flops 2415919104 | bytes 1024 | tf_op jit(solution)/shard_map/last_one/pallas_call | solution.py:51
  51.5 1.1 %collective-permute-start.6 = (bf16[4,2,3,32,256]{4,3,2,1,0:T(8,128)(2,1)S(1)}, bf16[4,2,3,32,256]{4,3,2,1,0:T(8,128)(2,1)S(1)}, u32[]{:S(2)}, u32[]{:S(2)}) collective-permute-start(bf16[4,2,3,32,256]{4,3,2,1,0:T(8,128)(2,1)S(1)} %get-tuple-element.67), channel_id=1, source_target_pairs={{0,1},{1,0},{2,3},{3,2},{4,5},{5,4},{6,7},{7,6},{8,9},{9,8},{10,11... | collective-permute-start | bytes 1179656 | tf_op jit(solution)/shard_map/ppermute | solution.py:291
  52.6 0.6 collective-permute-start.15
  53.2 0.9 %collective-permute-start.18 = (bf16[4,2,3,32,256]{4,3,2,1,0:T(8,128)(2,1)S(1)}, bf16[4,2,3,32,256]{4,3,2,1,0:T(8,128)(2,1)S(1)}, u32[]{:S(2)}, u32[]{:S(2)}) collective-permute-start(bf16[4,2,3,32,256]{4,3,2,1,0:T(8,128)(2,1)S(1)} %get-tuple-element.95), channel_id=1, source_target_pairs={{0,4},{1,5},{2,6},{3,7},{4,0},{5,1},{6,2},{7,3},{8,12},{9,13},{10,... | collective-permute-start | bytes 1179656 | tf_op jit(solution)/shard_map/ppermute | solution.py:291
  54.2 1.2 %collective-permute-done.10.refs_5_ = bf16[4,2,3,32,256]{4,3,2,1,0:T(8,128)(2,1)S(1)} collective-permute-done((bf16[4,2,3,32,256]{4,3,2,1,0:T(8,128)(2,1)S(1)}, bf16[4,2,3,32,256]{4,3,2,1,0:T(8,128)(2,1)S(1)}, u32[]{:S(2)}, u32[]{:S(2)}) %collective-permute-start.10) | collective-permute-done | bytes 393248 | tf_op jit(solution)/shard_map/ppermute | solution.py:291
  55.6 2.9 %collective-permute-start.11 = (bf16[2,2,3,32,256]{4,3,2,1,0:T(8,128)(2,1)S(1)}, bf16[2,2,3,32,256]{4,3,2,1,0:T(8,128)(2,1)S(1)}, u32[]{:S(2)}, u32[]{:S(2)}) collective-permute-start(bf16[2,2,3,32,256]{4,3,2,1,0:T(8,128)(2,1)S(1)} %get-tuple-element.79), channel_id=1, source_target_pairs={{0,3},{1,2},{2,1},{3,0},{4,7},{5,6},{6,5},{7,4},{8,11},{9,10},{10,... | collective-permute-start | bytes 589832 | tf_op jit(solution)/shard_map/ppermute | solution.py:291
  58.5 1.3 %collective-permute-start.12 = (bf16[2,2,3,32,256]{4,3,2,1,0:T(8,128)(2,1)S(1)}, bf16[2,2,3,32,256]{4,3,2,1,0:T(8,128)(2,1)S(1)}, u32[]{:S(2)}, u32[]{:S(2)}) collective-permute-start(bf16[2,2,3,32,256]{4,3,2,1,0:T(8,128)(2,1)S(1)} %get-tuple-element.80), channel_id=1, source_target_pairs={{0,4},{1,5},{2,6},{3,7},{4,0},{5,1},{6,2},{7,3},{8,12},{9,13},{10,... | collective-permute-start | bytes 589832 | tf_op jit(solution)/shard_map/ppermute | solution.py:291
  59.8 1.5 %collective-permute-done.6.got = bf16[4,2,3,32,256]{4,3,2,1,0:T(8,128)(2,1)S(1)} collective-permute-done((bf16[4,2,3,32,256]{4,3,2,1,0:T(8,128)(2,1)S(1)}, bf16[4,2,3,32,256]{4,3,2,1,0:T(8,128)(2,1)S(1)}, u32[]{:S(2)}, u32[]{:S(2)}) %collective-permute-start.6) | collective-permute-done | bytes 393248 | tf_op jit(solution)/shard_map/ppermute | solution.py:291
  61.2 0.8 collective-permute-start.13
  62.2 3.7 %collective-permute-done.15.got = bf16[4,2,3,32,256]{4,3,2,1,0:T(8,128)(2,1)S(1)} collective-permute-done((bf16[4,2,3,32,256]{4,3,2,1,0:T(8,128)(2,1)S(1)}, bf16[4,2,3,32,256]{4,3,2,1,0:T(8,128)(2,1)S(1)}, u32[]{:S(2)}, u32[]{:S(2)}) %collective-permute-start.15) | collective-permute-done | bytes 393248 | tf_op jit(solution)/shard_map/ppermute | solution.py:291
  65.9 0.6 collective-permute-start.7
  66.6 1.3 %collective-permute-start.16 = (bf16[2,2,3,32,256]{4,3,2,1,0:T(8,128)(2,1)S(1)}, bf16[2,2,3,32,256]{4,3,2,1,0:T(8,128)(2,1)S(1)}, u32[]{:S(2)}, u32[]{:S(2)}) collective-permute-start(bf16[2,2,3,32,256]{4,3,2,1,0:T(8,128)(2,1)S(1)} %get-tuple-element.89), channel_id=1, source_target_pairs={{0,4},{1,5},{2,6},{3,7},{4,0},{5,1},{6,2},{7,3},{8,12},{9,13},{10,... | collective-permute-start | bytes 589832 | tf_op jit(solution)/shard_map/ppermute | solution.py:291
  68.0 1.3 %collective-permute-done.11.refs_3_ = bf16[2,2,3,32,256]{4,3,2,1,0:T(8,128)(2,1)S(1)} collective-permute-done((bf16[2,2,3,32,256]{4,3,2,1,0:T(8,128)(2,1)S(1)}, bf16[2,2,3,32,256]{4,3,2,1,0:T(8,128)(2,1)S(1)}, u32[]{:S(2)}, u32[]{:S(2)}) %collective-permute-start.11) | collective-permute-done | bytes 196640 | tf_op jit(solution)/shard_map/ppermute | solution.py:291
  69.3 0.9 %collective-permute-done.12.refs_4_ = bf16[2,2,3,32,256]{4,3,2,1,0:T(8,128)(2,1)S(1)} collective-permute-done((bf16[2,2,3,32,256]{4,3,2,1,0:T(8,128)(2,1)S(1)}, bf16[2,2,3,32,256]{4,3,2,1,0:T(8,128)(2,1)S(1)}, u32[]{:S(2)}, u32[]{:S(2)}) %collective-permute-start.12) | collective-permute-done | bytes 196640 | tf_op jit(solution)/shard_map/ppermute | solution.py:291
  70.4 6.3 %collective-permute-done.19.got = bf16[2,2,3,32,256]{4,3,2,1,0:T(8,128)(2,1)S(1)} collective-permute-done((bf16[2,2,3,32,256]{4,3,2,1,0:T(8,128)(2,1)S(1)}, bf16[2,2,3,32,256]{4,3,2,1,0:T(8,128)(2,1)S(1)}, u32[]{:S(2)}, u32[]{:S(2)}) %collective-permute-start.19) | collective-permute-done | bytes 196640 | tf_op jit(solution)/shard_map/ppermute | solution.py:291
  77.2 3.7 %collective-permute-start.14 = (bf16[1,2,2,3,32,256]{5,4,3,2,1,0:T(8,128)(2,1)S(1)}, bf16[1,2,2,3,32,256]{5,4,3,2,1,0:T(8,128)(2,1)S(1)}, u32[]{:S(2)}, u32[]{:S(2)}) collective-permute-start(bf16[1,2,2,3,32,256]{5,4,3,2,1,0:T(8,128)(2,1)S(1)} %get-tuple-element.85), channel_id=1, source_target_pairs={{0,4},{1,5},{2,6},{3,7},{4,0},{5,1},{6,2},{7,3},{8,12},{9,13},{10,... | collective-permute-start | bytes 589832 | tf_op jit(solution)/shard_map/ppermute | solution.py:291
  81.0 2.2 %late_3.1 = bf16[2,512,256]{2,1,0:T(8,128)(2,1)} custom-call(bf16[36,256,256]{2,1,0:T(8,128)(2,1)S(1)} %bitcast.28, bf16[512,256]{1,0:T(8,128)(2,1)S(1)} %early_0_3.1.g1_zero.refs_2_, bf16[512,256]{1,0:T(8,128)(2,1)S(1)} %early_1_3.1.g1_one.refs_3_), custom_call_target="tpu_custom_call" | custom-call | flops 1207959552 | bytes 1024 | tf_op jit(solution)/shard_map/late_3/pallas_call | solution.py:51
  83.7 0.9 %collective-permute-done.14.refs_1_ = bf16[1,2,2,3,32,256]{5,4,3,2,1,0:T(8,128)(2,1)S(1)} collective-permute-done((bf16[1,2,2,3,32,256]{5,4,3,2,1,0:T(8,128)(2,1)S(1)}, bf16[1,2,2,3,32,256]{5,4,3,2,1,0:T(8,128)(2,1)S(1)}, u32[]{:S(2)}, u32[]{:S(2)}) %collective-permute-start.14) | collective-permute-done | bytes 196640 | tf_op jit(solution)/shard_map/ppermute | solution.py:291
  84.6 1.2 %finish.1 = f32[2,2,9,32,256]{4,3,2,1,0:T(8,128)} custom-call(bf16[1,2,2,3,32,256]{5,4,3,2,1,0:T(8,128)(2,1)S(1)} %get-tuple-element.84.refs_0_, bf16[1,2,2,3,32,256]{5,4,3,2,1,0:T(8,128)(2,1)S(1)} %collective-permute-done.14.refs_1_, bf16[1,2,2,3,32,256]{5,4,3,2,1,0:T(8,128)(2,1)S(1)} %get-tuple-element.92.refs_2_, ...), custom_call_target="tpu_custom_call" | custom-call | flops 603979776 | bytes 1024 | tf_op jit(solution)/shard_map/finish/pallas_call | solution.py:51
  (40 shorter events, 2.9 us)
Async XLA Ops:
  0.6 2.9 %slice-start = ((s8[4718592]{0:T(1024)(128)(4,1)}), s8[4194304]{0:T(1024)(128)(4,1)S(1)}, s32[]{:S(2)}) async-start(s8[4718592]{0:T(1024)(128)(4,1)} %bitcast.12), calls=%async_computation | async-start | bytes 8388608
  0.6 0.8 copy-start.4
  1.5 2.1 %slice-start.1 = ((s8[4718592]{0:T(1024)(128)(4,1)}), s8[524288]{0:T(1024)(128)(4,1)S(1)}, s32[]{:S(2)}) async-start(s8[4718592]{0:T(1024)(128)(4,1)} %bitcast.12), calls=%async_computation.1 | async-start | bytes 1048576
  5.2 6.6 %collective-permute-start = (bf16[512,256]{1,0:T(8,128)(2,1)S(1)}, bf16[512,256]{1,0:T(8,128)(2,1)S(1)}, u32[]{:S(2)}, u32[]{:S(2)}) collective-permute-start(bf16[512,256]{1,0:T(8,128)(2,1)S(1)} %late_1_0.1.refs_1_), channel_id=1, source_target_pairs={{0,8},{16,24},{32,40},{48,56},{64,72},{80,88},{96,104},{112,120},{... | collective-permute-start | bytes 786440 | tf_op jit(solution)/shard_map/ppermute | solution.py:287
  6.1 5.7 %copy-start = (bf16[2,1,4,1,16,32,256]{6,5,4,3,2,1,0:T(8,128)(2,1)S(1)}, bf16[2,1,4,1,16,32,256]{6,5,4,3,2,1,0:T(8,128)(2,1)}, u32[]{:S(2)}) copy-start(bf16[2,1,4,1,16,32,256]{6,5,4,3,2,1,0:T(8,128)(2,1)} %param.10) | copy-start | bytes 6291460
  6.2 5.7 %copy-start.1 = (bf16[2,1,4,1,16,32,256]{6,5,4,3,2,1,0:T(8,128)(2,1)S(1)}, bf16[2,1,4,1,16,32,256]{6,5,4,3,2,1,0:T(8,128)(2,1)}, u32[]{:S(2)}) copy-start(bf16[2,1,4,1,16,32,256]{6,5,4,3,2,1,0:T(8,128)(2,1)} %param.11) | copy-start | bytes 6291460
  7.0 9.9 %collective-permute-start.2 = (bf16[512,256]{1,0:T(8,128)(2,1)S(1)}, bf16[512,256]{1,0:T(8,128)(2,1)S(1)}, u32[]{:S(2)}, u32[]{:S(2)}) collective-permute-start(bf16[512,256]{1,0:T(8,128)(2,1)S(1)} %late_0_0.1.refs_1_), channel_id=1, source_target_pairs={{8,16},{24,32},{40,48},{56,64},{72,80},{88,96},{104,112},{16,8},{3... | collective-permute-start | bytes 786440 | tf_op jit(solution)/shard_map/ppermute | solution.py:287
  12.8 4.1 %copy-start.3 = (bf16[3,1,16,32,256]{4,3,2,1,0:T(8,128)(2,1)S(1)}, bf16[3,1,16,32,256]{4,3,2,1,0:T(8,128)(2,1)}, u32[]{:S(2)}) copy-start(bf16[3,1,16,32,256]{4,3,2,1,0:T(8,128)(2,1)} %param.8) | copy-start | bytes 2359300
  13.7 9.8 %collective-permute-start.1 = (bf16[512,256]{1,0:T(8,128)(2,1)S(1)}, bf16[512,256]{1,0:T(8,128)(2,1)S(1)}, u32[]{:S(2)}, u32[]{:S(2)}) collective-permute-start(bf16[512,256]{1,0:T(8,128)(2,1)S(1)} %late_0_1.1.refs_5_), channel_id=1, source_target_pairs={{8,16},{24,32},{40,48},{56,64},{72,80},{88,96},{104,112},{16,8},{3... | collective-permute-start | bytes 786440 | tf_op jit(solution)/shard_map/ppermute | solution.py:287
  18.0 1.6 %copy-start.2 = (bf16[2,1,4,1,16,32,256]{6,5,4,3,2,1,0:T(8,128)(2,1)S(1)}, bf16[2,1,4,1,16,32,256]{6,5,4,3,2,1,0:T(8,128)(2,1)}, u32[]{:S(2)}) copy-start(bf16[2,1,4,1,16,32,256]{6,5,4,3,2,1,0:T(8,128)(2,1)} %param.9) | copy-start | bytes 6291460
  18.8 6.5 %collective-permute-start.4 = (bf16[512,256]{1,0:T(8,128)(2,1)S(1)}, bf16[512,256]{1,0:T(8,128)(2,1)S(1)}, u32[]{:S(2)}, u32[]{:S(2)}) collective-permute-start(bf16[512,256]{1,0:T(8,128)(2,1)S(1)} %late_1_1.1.refs_5_), channel_id=1, source_target_pairs={{0,8},{16,24},{32,40},{48,56},{64,72},{80,88},{96,104},{112,120},{... | collective-permute-start | bytes 786440 | tf_op jit(solution)/shard_map/ppermute | solution.py:287
  27.2 9.8 %collective-permute-start.5 = (bf16[512,256]{1,0:T(8,128)(2,1)S(1)}, bf16[512,256]{1,0:T(8,128)(2,1)S(1)}, u32[]{:S(2)}, u32[]{:S(2)}) collective-permute-start(bf16[512,256]{1,0:T(8,128)(2,1)S(1)} %late_0_2.1.refs_2_), channel_id=1, source_target_pairs={{8,16},{24,32},{40,48},{56,64},{72,80},{88,96},{104,112},{16,8},{3... | collective-permute-start | bytes 786440 | tf_op jit(solution)/shard_map/ppermute | solution.py:287
  31.1 5.9 %collective-permute-start.3 = (bf16[512,256]{1,0:T(8,128)(2,1)S(1)}, bf16[512,256]{1,0:T(8,128)(2,1)S(1)}, u32[]{:S(2)}, u32[]{:S(2)}) collective-permute-start(bf16[512,256]{1,0:T(8,128)(2,1)S(1)} %late_1_2.1.refs_3_), channel_id=1, source_target_pairs={{0,8},{16,24},{32,40},{48,56},{64,72},{80,88},{96,104},{112,120},{... | collective-permute-start | bytes 786440 | tf_op jit(solution)/shard_map/ppermute | solution.py:287
  39.3 13.9 %collective-permute-start.8 = (bf16[4,2,3,32,256]{4,3,2,1,0:T(8,128)(2,1)S(1)}, bf16[4,2,3,32,256]{4,3,2,1,0:T(8,128)(2,1)S(1)}, u32[]{:S(2)}, u32[]{:S(2)}) collective-permute-start(bf16[4,2,3,32,256]{4,3,2,1,0:T(8,128)(2,1)S(1)} %get-tuple-element.73), channel_id=1, source_target_pairs={{0,1},{1,0},{2,3},{3,2},{4,5},{5,4},{6,7},{7,6},{8,9},{9,8},{10,11... | collective-permute-start | bytes 1179656 | tf_op jit(solution)/shard_map/ppermute | solution.py:291
  41.3 12.8 %collective-permute-start.9 = (bf16[4,2,3,32,256]{4,3,2,1,0:T(8,128)(2,1)S(1)}, bf16[4,2,3,32,256]{4,3,2,1,0:T(8,128)(2,1)S(1)}, u32[]{:S(2)}, u32[]{:S(2)}) collective-permute-start(bf16[4,2,3,32,256]{4,3,2,1,0:T(8,128)(2,1)S(1)} %get-tuple-element.74), channel_id=1, source_target_pairs={{0,3},{1,2},{2,1},{3,0},{4,7},{5,6},{6,5},{7,4},{8,11},{9,10},{10,... | collective-permute-start | bytes 1179656 | tf_op jit(solution)/shard_map/ppermute | solution.py:291
  43.9 11.5 %collective-permute-start.10 = (bf16[4,2,3,32,256]{4,3,2,1,0:T(8,128)(2,1)S(1)}, bf16[4,2,3,32,256]{4,3,2,1,0:T(8,128)(2,1)S(1)}, u32[]{:S(2)}, u32[]{:S(2)}) collective-permute-start(bf16[4,2,3,32,256]{4,3,2,1,0:T(8,128)(2,1)S(1)} %get-tuple-element.75), channel_id=1, source_target_pairs={{0,4},{1,5},{2,6},{3,7},{4,0},{5,1},{6,2},{7,3},{8,12},{9,13},{10,... | collective-permute-start | bytes 1179656 | tf_op jit(solution)/shard_map/ppermute | solution.py:291
  51.5 9.8 %collective-permute-start.6 = (bf16[4,2,3,32,256]{4,3,2,1,0:T(8,128)(2,1)S(1)}, bf16[4,2,3,32,256]{4,3,2,1,0:T(8,128)(2,1)S(1)}, u32[]{:S(2)}, u32[]{:S(2)}) collective-permute-start(bf16[4,2,3,32,256]{4,3,2,1,0:T(8,128)(2,1)S(1)} %get-tuple-element.67), channel_id=1, source_target_pairs={{0,1},{1,0},{2,3},{3,2},{4,5},{5,4},{6,7},{7,6},{8,9},{9,8},{10,11... | collective-permute-start | bytes 1179656 | tf_op jit(solution)/shard_map/ppermute | solution.py:291
  52.6 13.3 %collective-permute-start.15 = (bf16[4,2,3,32,256]{4,3,2,1,0:T(8,128)(2,1)S(1)}, bf16[4,2,3,32,256]{4,3,2,1,0:T(8,128)(2,1)S(1)}, u32[]{:S(2)}, u32[]{:S(2)}) collective-permute-start(bf16[4,2,3,32,256]{4,3,2,1,0:T(8,128)(2,1)S(1)} %get-tuple-element.87), channel_id=1, source_target_pairs={{0,3},{1,2},{2,1},{3,0},{4,7},{5,6},{6,5},{7,4},{8,11},{9,10},{10,... | collective-permute-start | bytes 1179656 | tf_op jit(solution)/shard_map/ppermute | solution.py:291
  53.2 13.4 %collective-permute-start.18 = (bf16[4,2,3,32,256]{4,3,2,1,0:T(8,128)(2,1)S(1)}, bf16[4,2,3,32,256]{4,3,2,1,0:T(8,128)(2,1)S(1)}, u32[]{:S(2)}, u32[]{:S(2)}) collective-permute-start(bf16[4,2,3,32,256]{4,3,2,1,0:T(8,128)(2,1)S(1)} %get-tuple-element.95), channel_id=1, source_target_pairs={{0,4},{1,5},{2,6},{3,7},{4,0},{5,1},{6,2},{7,3},{8,12},{9,13},{10,... | collective-permute-start | bytes 1179656 | tf_op jit(solution)/shard_map/ppermute | solution.py:291
  55.6 13.7 %collective-permute-start.11 = (bf16[2,2,3,32,256]{4,3,2,1,0:T(8,128)(2,1)S(1)}, bf16[2,2,3,32,256]{4,3,2,1,0:T(8,128)(2,1)S(1)}, u32[]{:S(2)}, u32[]{:S(2)}) collective-permute-start(bf16[2,2,3,32,256]{4,3,2,1,0:T(8,128)(2,1)S(1)} %get-tuple-element.79), channel_id=1, source_target_pairs={{0,3},{1,2},{2,1},{3,0},{4,7},{5,6},{6,5},{7,4},{8,11},{9,10},{10,... | collective-permute-start | bytes 589832 | tf_op jit(solution)/shard_map/ppermute | solution.py:291
  58.5 11.7 %collective-permute-start.12 = (bf16[2,2,3,32,256]{4,3,2,1,0:T(8,128)(2,1)S(1)}, bf16[2,2,3,32,256]{4,3,2,1,0:T(8,128)(2,1)S(1)}, u32[]{:S(2)}, u32[]{:S(2)}) collective-permute-start(bf16[2,2,3,32,256]{4,3,2,1,0:T(8,128)(2,1)S(1)} %get-tuple-element.80), channel_id=1, source_target_pairs={{0,4},{1,5},{2,6},{3,7},{4,0},{5,1},{6,2},{7,3},{8,12},{9,13},{10,... | collective-permute-start | bytes 589832 | tf_op jit(solution)/shard_map/ppermute | solution.py:291
  61.2 9.0 %collective-permute-start.13 = (bf16[2,2,3,32,256]{4,3,2,1,0:T(8,128)(2,1)S(1)}, bf16[2,2,3,32,256]{4,3,2,1,0:T(8,128)(2,1)S(1)}, u32[]{:S(2)}, u32[]{:S(2)}) collective-permute-start(bf16[2,2,3,32,256]{4,3,2,1,0:T(8,128)(2,1)S(1)} %get-tuple-element.81), channel_id=1, source_target_pairs={{0,1},{1,0},{2,3},{3,2},{4,5},{5,4},{6,7},{7,6},{8,9},{9,8},{10,11... | collective-permute-start | bytes 589832 | tf_op jit(solution)/shard_map/ppermute | solution.py:291
  65.9 11.3 %collective-permute-start.7 = (bf16[2,2,3,32,256]{4,3,2,1,0:T(8,128)(2,1)S(1)}, bf16[2,2,3,32,256]{4,3,2,1,0:T(8,128)(2,1)S(1)}, u32[]{:S(2)}, u32[]{:S(2)}) collective-permute-start(bf16[2,2,3,32,256]{4,3,2,1,0:T(8,128)(2,1)S(1)} %get-tuple-element.69), channel_id=1, source_target_pairs={{0,3},{1,2},{2,1},{3,0},{4,7},{5,6},{6,5},{7,4},{8,11},{9,10},{10,... | collective-permute-start | bytes 589832 | tf_op jit(solution)/shard_map/ppermute | solution.py:291
  66.6 10.2 %collective-permute-start.16 = (bf16[2,2,3,32,256]{4,3,2,1,0:T(8,128)(2,1)S(1)}, bf16[2,2,3,32,256]{4,3,2,1,0:T(8,128)(2,1)S(1)}, u32[]{:S(2)}, u32[]{:S(2)}) collective-permute-start(bf16[2,2,3,32,256]{4,3,2,1,0:T(8,128)(2,1)S(1)} %get-tuple-element.89), channel_id=1, source_target_pairs={{0,4},{1,5},{2,6},{3,7},{4,0},{5,1},{6,2},{7,3},{8,12},{9,13},{10,... | collective-permute-start | bytes 589832 | tf_op jit(solution)/shard_map/ppermute | solution.py:291
  69.3 7.3 %collective-permute-start.19 = (bf16[2,2,3,32,256]{4,3,2,1,0:T(8,128)(2,1)S(1)}, bf16[2,2,3,32,256]{4,3,2,1,0:T(8,128)(2,1)S(1)}, u32[]{:S(2)}, u32[]{:S(2)}) collective-permute-start(bf16[2,2,3,32,256]{4,3,2,1,0:T(8,128)(2,1)S(1)} %get-tuple-element.97), channel_id=1, source_target_pairs={{0,1},{1,0},{2,3},{3,2},{4,5},{5,4},{6,7},{7,6},{8,9},{9,8},{10,11... | collective-permute-start | bytes 589832 | tf_op jit(solution)/shard_map/ppermute | solution.py:291
  76.7 7.0 %collective-permute-start.20 = (bf16[1,2,2,3,32,256]{5,4,3,2,1,0:T(8,128)(2,1)S(1)}, bf16[1,2,2,3,32,256]{5,4,3,2,1,0:T(8,128)(2,1)S(1)}, u32[]{:S(2)}, u32[]{:S(2)}) collective-permute-start(bf16[1,2,2,3,32,256]{5,4,3,2,1,0:T(8,128)(2,1)S(1)} %get-tuple-element.101), channel_id=1, source_target_pairs={{0,3},{1,2},{2,1},{3,0},{4,7},{5,6},{6,5},{7,4},{8,11},{9,10},{10,... | collective-permute-start | bytes 589832 | tf_op jit(solution)/shard_map/ppermute | solution.py:291
  76.9 6.8 %collective-permute-start.17 = (bf16[1,2,2,3,32,256]{5,4,3,2,1,0:T(8,128)(2,1)S(1)}, bf16[1,2,2,3,32,256]{5,4,3,2,1,0:T(8,128)(2,1)S(1)}, u32[]{:S(2)}, u32[]{:S(2)}) collective-permute-start(bf16[1,2,2,3,32,256]{5,4,3,2,1,0:T(8,128)(2,1)S(1)} %get-tuple-element.93), channel_id=1, source_target_pairs={{0,1},{1,0},{2,3},{3,2},{4,5},{5,4},{6,7},{7,6},{8,9},{9,8},{10,11... | collective-permute-start | bytes 589832 | tf_op jit(solution)/shard_map/ppermute | solution.py:291
  77.2 7.4 %collective-permute-start.14 = (bf16[1,2,2,3,32,256]{5,4,3,2,1,0:T(8,128)(2,1)S(1)}, bf16[1,2,2,3,32,256]{5,4,3,2,1,0:T(8,128)(2,1)S(1)}, u32[]{:S(2)}, u32[]{:S(2)}) collective-permute-start(bf16[1,2,2,3,32,256]{5,4,3,2,1,0:T(8,128)(2,1)S(1)} %get-tuple-element.85), channel_id=1, source_target_pairs={{0,4},{1,5},{2,6},{3,7},{4,0},{5,1},{6,2},{7,3},{8,12},{9,13},{10,... | collective-permute-start | bytes 589832 | tf_op jit(solution)/shard_map/ppermute | solution.py:291

commit v3 on v2

--- a/solution.py
+++ b/solution.py
@@ -270,15 +270,22 @@
     fold_in(keep, got, send.at[:, 0], left.at[:, 0])
 
 
-def finish_kernel(scale, *refs):
+def finish_some_kernel(scale, *refs):
     out = refs[-1]
-    for o in range(3):
+    for o in range(2):
         keep, got = refs[2 * o : 2 * o + 2]
         total = keep[0].astype(F32) + got[0].astype(F32)
         for role in range(2):
-            half = half_of(role)
             for piece in range(2):
-                out[half, piece, 3 * o : 3 * o + 3] = total[piece, role] * scale
+                out[half_of(role), piece, 3 * o : 3 * o + 3] = total[piece, role] * scale
+
+
+def finish_kernel(scale, some, keep, got, out):
+    out[:, :, 0:6] = some[...]
+    total = keep[0].astype(F32) + got[0].astype(F32)
+    for role in range(2):
+        for piece in range(2):
+            out[half_of(role), piece, 6:9] = total[piece, role] * scale
 
 
 def relay(block, role):
@@ -410,22 +417,35 @@
     res = call(fold_kernel, "fold_two", (*keeps2, *gots2), (part2,) * 6, ops=FOLD_COST)
     gots2 = [exchange(res[o], ORDERS[o][1]) for o in range(3)]
     begun = call(fold_two_last_kernel, "fold_two_last", (*res[3:6], *gots2), (part3,) * 6, ops=FOLD_COST)
+    firsts = []
     for o in range(3):
-        send, keep = call(fold_in, f"fold_one_{o}", (keeps1[o], gots1[o]), (part2, part2))
-        got = exchange(send, ORDERS[o][1])
+        send, keep = call(fold_in, f"fold_one_{o}", (keeps1[o], gots1[o]), (part2, part2), after=firsts[-1:])
+        firsts.append(keep)
+        gots1[o] = exchange(send, ORDERS[o][1])
+    lasts = []
+    for o in range(3):
         send, keep = call(
             fold_one_last_kernel,
             f"fold_one_last_{o}",
-            (keep, got, begun[o], begun[3 + o]),
+            (firsts[o], gots1[o], begun[o], begun[3 + o]),
             (part3, part3),
             aliases={2: 0, 3: 1},
+            after=lasts[-1:],
         )
+        lasts.append(keep)
         parts += [keep, exchange(send, ORDERS[o][2])]
     scale = 1.0 / math.sqrt(TICKS * DP * PIX)
+    some = call(
+        functools.partial(finish_some_kernel, scale),
+        "finish_some",
+        tuple(parts[:4]),
+        jax.ShapeDtypeStruct((2, 2, 6, SHARE, CH), F32),
+        ops=FOLD_COST,
+    )
     grads = call(
         functools.partial(finish_kernel, scale),
         "finish",
-        tuple(parts),
+        (some, *parts[4:]),
         jax.ShapeDtypeStruct((2, 2, 9, SHARE, CH), F32),
     )
     return (

time: 87.3 us -> 87.4 us (level)
    pallas_call x30 -> x31, Pallas kernels: 29.9 us -> 30 us  [call(): pl.pallas_call(body if after else kernel, out_shape=outs, in_specs=[VM] *...]
  transfers between devices with their start and end apart: 21 -> 21, of which waited for: 11 -> 12; matrix products, arithmetic and copies ran while one was open for 0% -> 0% of each run, Pallas kernels for 27% -> 27%
where the time goes in v3:
time: 87.4 us; the launch traced here: 86.5 us
  starting transfers between devices  33.2 us (38%)
  Pallas kernels  32 us (37%)
  waiting for transfers between devices  19 us (22%)
  local copies, waits for them, and re-layouts  1.33 us (2%)
  between operations  0.97 us (1%)
    pallas_call x31, Pallas kernels, call(): pl.pallas_call(body if after else kernel, out_shape=outs, in_specs=[VM] *...  30 us
    ppermute x15, starting transfers between devices, exchange(): return lax.ppermute(block, 'dp', PAIRS[step])  21.1 us
    ppermute x15, waiting for transfers between devices, exchange(): return lax.ppermute(block, 'dp', PAIRS[step])  16.7 us
    ppermute x6, starting transfers between devices, relay(): return lax.ppermute(block, 'section', pairs + [(b, a) for a, b in pairs])  12.2 us
    ppermute x6, waiting for transfers between devices, relay(): return lax.ppermute(block, 'section', pairs + [(b, a) for a, b in pairs])  2.22 us
    pallas_call x1, Pallas kernels, prepare(): pl.pallas_call(prepare_kernel, grid_spec=pltpu.PrefetchScalarGridSpec(num...  2.04 us
  transfers between devices with their start and end apart: 21, of which 12 were waited for; matrix products, arithmetic and copies ran while one was open for 0% of the time, Pallas kernels for 27%

profile of v3, /device:TPU:8, one launch (start us, length us, event | category | flops | bytes accessed | tf_op | source)
XLA Modules:
  0.0 86.5 jit_solution(12481636309571658033)
XLA Ops:
  0.7 0.8 copy-done.4
  1.5 2.0 %prepare.1 = (bf16[512,256]{1,0:T(8,128)(2,1)S(1)}, bf16[512,256]{1,0:T(8,128)(2,1)S(1)}, bf16[512,256]{1,0:T(8,128)(2,1)S(1)}, bf16[512,256]{1,0:T(8,128)(2,1)S(1)}) custom-call(s32[4,32]{1,0:T(4,128)S(1)} %copy-done.4, bf16[2,512,256]{2,1,0:T(8,128)(2,1)} %bitcast.53, bf16[2,512,256]{2,1,0:T(8,128)(2,1)} %bitcast.54, bf16[8,512,256]{2,1,0:T(8,128)(2,1)} %bitcast.40, ...), custom_call_target="tpu_custom_call" | custom-call | flops 1 | bytes 1024 | tf_op jit(solution)/shard_map/prepare/pallas_call | solution.py:129
  3.5 0.8 early_1_0.1.g1.refs_0_
  4.4 0.8 late_1_0.1.refs_1_
  5.3 0.8 early_0_0.1.refs_0_.g1
  6.2 0.8 late_0_0.1.refs_1_
  7.0 4.8 %collective-permute-start.2 = (bf16[512,256]{1,0:T(8,128)(2,1)S(1)}, bf16[512,256]{1,0:T(8,128)(2,1)S(1)}, u32[]{:S(2)}, u32[]{:S(2)}) collective-permute-start(bf16[512,256]{1,0:T(8,128)(2,1)S(1)} %late_0_0.1.refs_1_), channel_id=1, source_target_pairs={{8,16},{24,32},{40,48},{56,64},{72,80},{88,96},{104,112},{16,8},{3... | collective-permute-start | bytes 786440 | tf_op jit(solution)/shard_map/ppermute | solution.py:294
  11.8 1.0 %early_0_1.1 = (bf16[512,256]{1,0:T(8,128)(2,1)S(1)}, bf16[512,256]{1,0:T(8,128)(2,1)S(1)}) custom-call(s32[4,32]{1,0:T(4,128)S(1)} %copy-done.4, bf16[8,512,256]{2,1,0:T(8,128)(2,1)S(1)} %bitcast.31, bf16[8,512,256]{2,1,0:T(8,128)(2,1)S(1)} %bitcast.42, bf16[36,256,256]{2,1,0:T(8,128)(2,1)S(1)} %bitcast.18, ...), custom_call_target="tpu_custom_call" | custom-call | flops 603979776 | bytes 1024 | tf_op jit(solution)/shard_map/early_0_1/pallas_call | solution.py:51
  12.8 0.8 late_0_1.1.refs_5_
  13.7 3.0 %collective-permute-start.1 = (bf16[512,256]{1,0:T(8,128)(2,1)S(1)}, bf16[512,256]{1,0:T(8,128)(2,1)S(1)}, u32[]{:S(2)}, u32[]{:S(2)}) collective-permute-start(bf16[512,256]{1,0:T(8,128)(2,1)S(1)} %late_0_1.1.refs_5_), channel_id=1, source_target_pairs={{8,16},{24,32},{40,48},{56,64},{72,80},{88,96},{104,112},{16,8},{3... | collective-permute-start | bytes 786440 | tf_op jit(solution)/shard_map/ppermute | solution.py:294
  16.9 1.0 %early_1_1.1 = (bf16[512,256]{1,0:T(8,128)(2,1)S(1)}, bf16[512,256]{1,0:T(8,128)(2,1)S(1)}) custom-call(s32[4,32]{1,0:T(4,128)S(1)} %copy-done.4, bf16[8,512,256]{2,1,0:T(8,128)(2,1)S(1)} %bitcast.32, bf16[8,512,256]{2,1,0:T(8,128)(2,1)S(1)} %bitcast.43, bf16[36,256,256]{2,1,0:T(8,128)(2,1)S(1)} %bitcast.20, ...), custom_call_target="tpu_custom_call" | custom-call | flops 603979776 | bytes 1024 | tf_op jit(solution)/shard_map/early_1_1/pallas_call | solution.py:51
  18.0 0.8 late_1_1.1.refs_5_
  19.6 1.6 %wgrad1_1.1.refs_8_.refs_7_.refs_5_ = f32[9,256,256]{2,1,0:T(8,128)S(1)} custom-call(s32[4,32]{1,0:T(4,128)S(1)} %copy-done.4, bf16[8,512,256]{2,1,0:T(8,128)(2,1)S(1)} %bitcast.47, bf16[512,256]{1,0:T(8,128)(2,1)S(1)} %early_1_0.1.g1.refs_0_, bf16[512,256]{1,0:T(8,128)(2,1)S(1)} %get-tuple-element.57.refs_1_.g1), custom_call_target="tpu_custom_call" | custom-call | flops 1207959552 | bytes 1024 | tf_op jit(solution)/shard_map/wgrad1_1/pallas_call | solution.py:51
  21.1 1.6 %wgrad1_0.1.refs_7_.refs_6_.refs_4_ = f32[9,256,256]{2,1,0:T(8,128)S(1)} custom-call(s32[4,32]{1,0:T(4,128)S(1)} %copy-done.4, bf16[8,512,256]{2,1,0:T(8,128)(2,1)S(1)} %bitcast.48, bf16[512,256]{1,0:T(8,128)(2,1)S(1)} %early_0_0.1.refs_0_.g1, bf16[512,256]{1,0:T(8,128)(2,1)S(1)} %get-tuple-element.54.g1.refs_1_), custom_call_target="tpu_custom_call" | custom-call | flops 1207959552 | bytes 1024 | tf_op jit(solution)/shard_map/wgrad1_0/pallas_call | solution.py:51
  23.5 1.0 %early_1_2.1 = (bf16[512,256]{1,0:T(8,128)(2,1)S(1)}, bf16[512,256]{1,0:T(8,128)(2,1)S(1)}) custom-call(s32[4,32]{1,0:T(4,128)S(1)} %copy-done.4, bf16[8,512,256]{2,1,0:T(8,128)(2,1)S(1)} %bitcast.33, bf16[8,512,256]{2,1,0:T(8,128)(2,1)S(1)} %bitcast.44, bf16[36,256,256]{2,1,0:T(8,128)(2,1)S(1)} %bitcast.22, ...), custom_call_target="tpu_custom_call" | custom-call | flops 603979776 | bytes 1024 | tf_op jit(solution)/shard_map/early_1_2/pallas_call | solution.py:51
  24.5 0.8 late_1_2.1.refs_3_
  25.3 1.0 %early_0_2.1 = (bf16[512,256]{1,0:T(8,128)(2,1)S(1)}, bf16[512,256]{1,0:T(8,128)(2,1)S(1)}) custom-call(s32[4,32]{1,0:T(4,128)S(1)} %copy-done.4, bf16[8,512,256]{2,1,0:T(8,128)(2,1)S(1)} %bitcast.34, bf16[8,512,256]{2,1,0:T(8,128)(2,1)S(1)} %bitcast.45, bf16[36,256,256]{2,1,0:T(8,128)(2,1)S(1)} %bitcast.24, ...), custom_call_target="tpu_custom_call" | custom-call | flops 603979776 | bytes 1024 | tf_op jit(solution)/shard_map/early_0_2/pallas_call | solution.py:51
  26.3 0.8 late_0_2.1.refs_2_
  27.2 3.9 %collective-permute-start.5 = (bf16[512,256]{1,0:T(8,128)(2,1)S(1)}, bf16[512,256]{1,0:T(8,128)(2,1)S(1)}, u32[]{:S(2)}, u32[]{:S(2)}) collective-permute-start(bf16[512,256]{1,0:T(8,128)(2,1)S(1)} %late_0_2.1.refs_2_), channel_id=1, source_target_pairs={{8,16},{24,32},{40,48},{56,64},{72,80},{88,96},{104,112},{16,8},{3... | collective-permute-start | bytes 786440 | tf_op jit(solution)/shard_map/ppermute | solution.py:294
  31.2 2.3 %wgrad2_1.1.refs_5_ = f32[9,256,256]{2,1,0:T(8,128)S(1)} custom-call(s32[4,32]{1,0:T(4,128)S(1)} %copy-done.4, bf16[8,512,256]{2,1,0:T(8,128)(2,1)S(1)} %bitcast.35, bf16[512,256]{1,0:T(8,128)(2,1)S(1)} %get-tuple-element.53.g2.refs_0_, bf16[512,256]{1,0:T(8,128)(2,1)S(1)} %get-tuple-element.62.refs_1_, bf16[512,256]{1,0:T(8,128)(2,1)S(1)} %get-tuple-element.63.refs_2_), custom_call_target="tpu_custom_call" | custom-call | flops 1811939328 | bytes 1024 | tf_op jit(solution)/shard_map/wgrad2_1/pallas_call | solution.py:51
  33.5 2.3 %wgrad2_0.1.refs_4_ = f32[9,256,256]{2,1,0:T(8,128)S(1)} custom-call(s32[4,32]{1,0:T(4,128)S(1)} %copy-done.4, bf16[8,512,256]{2,1,0:T(8,128)(2,1)S(1)} %bitcast.36, bf16[512,256]{1,0:T(8,128)(2,1)S(1)} %get-tuple-element.56.g2.refs_0_, bf16[512,256]{1,0:T(8,128)(2,1)S(1)} %get-tuple-element.60.refs_1_, bf16[512,256]{1,0:T(8,128)(2,1)S(1)} %get-tuple-element.61.refs_2_), custom_call_target="tpu_custom_call" | custom-call | flops 1811939328 | bytes 1024 | tf_op jit(solution)/shard_map/wgrad2_0/pallas_call | solution.py:51
  35.7 1.2 %collective-permute-done.5.refs_1_ = bf16[512,256]{1,0:T(8,128)(2,1)S(1)} collective-permute-done((bf16[512,256]{1,0:T(8,128)(2,1)S(1)}, bf16[512,256]{1,0:T(8,128)(2,1)S(1)}, u32[]{:S(2)}, u32[]{:S(2)}) %collective-permute-start.5) | collective-permute-done | bytes 262176 | tf_op jit(solution)/shard_map/ppermute | solution.py:294
  37.0 2.3 %last_two.1 = (bf16[4,2,3,32,256]{4,3,2,1,0:T(8,128)(2,1)S(1)}, bf16[4,2,3,32,256]{4,3,2,1,0:T(8,128)(2,1)S(1)}, bf16[4,2,3,32,256]{4,3,2,1,0:T(8,128)(2,1)S(1)}...) custom-call(s32[4,32]{1,0:T(4,128)S(1)} %copy-done.4, ...), custom_call_target="tpu_custom_call" | custom-call | flops 1207959552 | bytes 1024 | tf_op jit(solution)/shard_map/last_two/pallas_call | solution.py:51
  39.3 2.0 %collective-permute-start.8 = (bf16[4,2,3,32,256]{4,3,2,1,0:T(8,128)(2,1)S(1)}, bf16[4,2,3,32,256]{4,3,2,1,0:T(8,128)(2,1)S(1)}, u32[]{:S(2)}, u32[]{:S(2)}) collective-permute-start(bf16[4,2,3,32,256]{4,3,2,1,0:T(8,128)(2,1)S(1)} %get-tuple-element.73), channel_id=1, source_target_pairs={{0,1},{1,0},{2,3},{3,2},{4,5},{5,4},{6,7},{7,6},{8,9},{9,8},{10,11... | collective-permute-start | bytes 1179656 | tf_op jit(solution)/shard_map/ppermute | solution.py:298
  41.3 2.5 %collective-permute-start.9 = (bf16[4,2,3,32,256]{4,3,2,1,0:T(8,128)(2,1)S(1)}, bf16[4,2,3,32,256]{4,3,2,1,0:T(8,128)(2,1)S(1)}, u32[]{:S(2)}, u32[]{:S(2)}) collective-permute-start(bf16[4,2,3,32,256]{4,3,2,1,0:T(8,128)(2,1)S(1)} %get-tuple-element.74), channel_id=1, source_target_pairs={{0,3},{1,2},{2,1},{3,0},{4,7},{5,6},{6,5},{7,4},{8,11},{9,10},{10,... | collective-permute-start | bytes 1179656 | tf_op jit(solution)/shard_map/ppermute | solution.py:298
  43.9 2.6 %collective-permute-start.10 = (bf16[4,2,3,32,256]{4,3,2,1,0:T(8,128)(2,1)S(1)}, bf16[4,2,3,32,256]{4,3,2,1,0:T(8,128)(2,1)S(1)}, u32[]{:S(2)}, u32[]{:S(2)}) collective-permute-start(bf16[4,2,3,32,256]{4,3,2,1,0:T(8,128)(2,1)S(1)} %get-tuple-element.75), channel_id=1, source_target_pairs={{0,4},{1,5},{2,6},{3,7},{4,0},{5,1},{6,2},{7,3},{8,12},{9,13},{10,... | collective-permute-start | bytes 1179656 | tf_op jit(solution)/shard_map/ppermute | solution.py:298
  46.4 0.8 early_0_3.1.g1_zero.refs_2_
  47.3 0.8 early_1_3.1.g1_one.refs_3_
  48.1 3.4 %last_one.1 = (bf16[4,2,3,32,256]{4,3,2,1,0:T(8,128)(2,1)S(1)}, bf16[4,2,3,32,256]{4,3,2,1,0:T(8,128)(2,1)S(1)}, bf16[4,2,3,32,256]{4,3,2,1,0:T(8,128)(2,1)S(1)}...) custom-call(s32[4,32]{1,0:T(4,128)S(1)} %copy-done.4, ...), custom_call_target="tpu_custom_call" | custom-call | flops 2415919104 | bytes 1024 | tf_op jit(solution)/shard_map/last_one/pallas_call | solution.py:51
  51.5 1.1 %collective-permute-start.6 = (bf16[4,2,3,32,256]{4,3,2,1,0:T(8,128)(2,1)S(1)}, bf16[4,2,3,32,256]{4,3,2,1,0:T(8,128)(2,1)S(1)}, u32[]{:S(2)}, u32[]{:S(2)}) collective-permute-start(bf16[4,2,3,32,256]{4,3,2,1,0:T(8,128)(2,1)S(1)} %get-tuple-element.67), channel_id=1, source_target_pairs={{0,1},{1,0},{2,3},{3,2},{4,5},{5,4},{6,7},{7,6},{8,9},{9,8},{10,11... | collective-permute-start | bytes 1179656 | tf_op jit(solution)/shard_map/ppermute | solution.py:298
  53.2 0.9 %collective-permute-start.18 = (bf16[4,2,3,32,256]{4,3,2,1,0:T(8,128)(2,1)S(1)}, bf16[4,2,3,32,256]{4,3,2,1,0:T(8,128)(2,1)S(1)}, u32[]{:S(2)}, u32[]{:S(2)}) collective-permute-start(bf16[4,2,3,32,256]{4,3,2,1,0:T(8,128)(2,1)S(1)} %get-tuple-element.95), channel_id=1, source_target_pairs={{0,4},{1,5},{2,6},{3,7},{4,0},{5,1},{6,2},{7,3},{8,12},{9,13},{10,... | collective-permute-start | bytes 1179656 | tf_op jit(solution)/shard_map/ppermute | solution.py:298
  54.2 1.2 %collective-permute-done.10.refs_5_ = bf16[4,2,3,32,256]{4,3,2,1,0:T(8,128)(2,1)S(1)} collective-permute-done((bf16[4,2,3,32,256]{4,3,2,1,0:T(8,128)(2,1)S(1)}, bf16[4,2,3,32,256]{4,3,2,1,0:T(8,128)(2,1)S(1)}, u32[]{:S(2)}, u32[]{:S(2)}) %collective-permute-start.10) | collective-permute-done | bytes 393248 | tf_op jit(solution)/shard_map/ppermute | solution.py:298
  55.6 2.9 %collective-permute-start.11 = (bf16[2,2,3,32,256]{4,3,2,1,0:T(8,128)(2,1)S(1)}, bf16[2,2,3,32,256]{4,3,2,1,0:T(8,128)(2,1)S(1)}, u32[]{:S(2)}, u32[]{:S(2)}) collective-permute-start(bf16[2,2,3,32,256]{4,3,2,1,0:T(8,128)(2,1)S(1)} %get-tuple-element.79), channel_id=1, source_target_pairs={{0,3},{1,2},{2,1},{3,0},{4,7},{5,6},{6,5},{7,4},{8,11},{9,10},{10,... | collective-permute-start | bytes 589832 | tf_op jit(solution)/shard_map/ppermute | solution.py:298
  58.5 1.3 %collective-permute-start.12 = (bf16[2,2,3,32,256]{4,3,2,1,0:T(8,128)(2,1)S(1)}, bf16[2,2,3,32,256]{4,3,2,1,0:T(8,128)(2,1)S(1)}, u32[]{:S(2)}, u32[]{:S(2)}) collective-permute-start(bf16[2,2,3,32,256]{4,3,2,1,0:T(8,128)(2,1)S(1)} %get-tuple-element.80), channel_id=1, source_target_pairs={{0,4},{1,5},{2,6},{3,7},{4,0},{5,1},{6,2},{7,3},{8,12},{9,13},{10,... | collective-permute-start | bytes 589832 | tf_op jit(solution)/shard_map/ppermute | solution.py:298
  59.8 1.5 %collective-permute-done.6.got = bf16[4,2,3,32,256]{4,3,2,1,0:T(8,128)(2,1)S(1)} collective-permute-done((bf16[4,2,3,32,256]{4,3,2,1,0:T(8,128)(2,1)S(1)}, bf16[4,2,3,32,256]{4,3,2,1,0:T(8,128)(2,1)S(1)}, u32[]{:S(2)}, u32[]{:S(2)}) %collective-permute-start.6) | collective-permute-done | bytes 393248 | tf_op jit(solution)/shard_map/ppermute | solution.py:298
  61.2 0.8 collective-permute-start.13
  62.2 3.7 %collective-permute-done.15.refs_1_ = bf16[4,2,3,32,256]{4,3,2,1,0:T(8,128)(2,1)S(1)} collective-permute-done((bf16[4,2,3,32,256]{4,3,2,1,0:T(8,128)(2,1)S(1)}, bf16[4,2,3,32,256]{4,3,2,1,0:T(8,128)(2,1)S(1)}, u32[]{:S(2)}, u32[]{:S(2)}) %collective-permute-start.15) | collective-permute-done | bytes 393248 | tf_op jit(solution)/shard_map/ppermute | solution.py:298
  66.6 1.3 %collective-permute-start.16 = (bf16[2,2,3,32,256]{4,3,2,1,0:T(8,128)(2,1)S(1)}, bf16[2,2,3,32,256]{4,3,2,1,0:T(8,128)(2,1)S(1)}, u32[]{:S(2)}, u32[]{:S(2)}) collective-permute-start(bf16[2,2,3,32,256]{4,3,2,1,0:T(8,128)(2,1)S(1)} %get-tuple-element.89), channel_id=1, source_target_pairs={{0,4},{1,5},{2,6},{3,7},{4,0},{5,1},{6,2},{7,3},{8,12},{9,13},{10,... | collective-permute-start | bytes 589832 | tf_op jit(solution)/shard_map/ppermute | solution.py:298
  68.0 1.3 %collective-permute-done.11.refs_3_ = bf16[2,2,3,32,256]{4,3,2,1,0:T(8,128)(2,1)S(1)} collective-permute-done((bf16[2,2,3,32,256]{4,3,2,1,0:T(8,128)(2,1)S(1)}, bf16[2,2,3,32,256]{4,3,2,1,0:T(8,128)(2,1)S(1)}, u32[]{:S(2)}, u32[]{:S(2)}) %collective-permute-start.11) | collective-permute-done | bytes 196640 | tf_op jit(solution)/shard_map/ppermute | solution.py:298
  69.3 0.9 %collective-permute-done.12.refs_4_ = bf16[2,2,3,32,256]{4,3,2,1,0:T(8,128)(2,1)S(1)} collective-permute-done((bf16[2,2,3,32,256]{4,3,2,1,0:T(8,128)(2,1)S(1)}, bf16[2,2,3,32,256]{4,3,2,1,0:T(8,128)(2,1)S(1)}, u32[]{:S(2)}, u32[]{:S(2)}) %collective-permute-start.12) | collective-permute-done | bytes 196640 | tf_op jit(solution)/shard_map/ppermute | solution.py:298
  70.4 2.4 %collective-permute-done.7.got = bf16[2,2,3,32,256]{4,3,2,1,0:T(8,128)(2,1)S(1)} collective-permute-done((bf16[2,2,3,32,256]{4,3,2,1,0:T(8,128)(2,1)S(1)}, bf16[2,2,3,32,256]{4,3,2,1,0:T(8,128)(2,1)S(1)}, u32[]{:S(2)}, u32[]{:S(2)}) %collective-permute-start.7) | collective-permute-done | bytes 196640 | tf_op jit(solution)/shard_map/ppermute | solution.py:298
  72.8 1.0 %collective-permute-done.16.refs_1_ = bf16[2,2,3,32,256]{4,3,2,1,0:T(8,128)(2,1)S(1)} collective-permute-done((bf16[2,2,3,32,256]{4,3,2,1,0:T(8,128)(2,1)S(1)}, bf16[2,2,3,32,256]{4,3,2,1,0:T(8,128)(2,1)S(1)}, u32[]{:S(2)}, u32[]{:S(2)}) %collective-permute-start.16) | collective-permute-done | bytes 196640 | tf_op jit(solution)/shard_map/ppermute | solution.py:298
  74.1 2.0 %collective-permute-start.14 = (bf16[1,2,2,3,32,256]{5,4,3,2,1,0:T(8,128)(2,1)S(1)}, bf16[1,2,2,3,32,256]{5,4,3,2,1,0:T(8,128)(2,1)S(1)}, u32[]{:S(2)}, u32[]{:S(2)}) collective-permute-start(bf16[1,2,2,3,32,256]{5,4,3,2,1,0:T(8,128)(2,1)S(1)} %get-tuple-element.85), channel_id=1, source_target_pairs={{0,4},{1,5},{2,6},{3,7},{4,0},{5,1},{6,2},{7,3},{8,12},{9,13},{10,... | collective-permute-start | bytes 589832 | tf_op jit(solution)/shard_map/ppermute | solution.py:298
  76.1 2.2 %late_3.1 = bf16[2,512,256]{2,1,0:T(8,128)(2,1)} custom-call(bf16[36,256,256]{2,1,0:T(8,128)(2,1)S(1)} %bitcast.28, bf16[512,256]{1,0:T(8,128)(2,1)S(1)} %early_0_3.1.g1_zero.refs_2_, bf16[512,256]{1,0:T(8,128)(2,1)S(1)} %early_1_3.1.g1_one.refs_3_), custom_call_target="tpu_custom_call" | custom-call | flops 1207959552 | bytes 1024 | tf_op jit(solution)/shard_map/late_3/pallas_call | solution.py:51
  78.4 2.1 %collective-permute-start.20 = (bf16[1,2,2,3,32,256]{5,4,3,2,1,0:T(8,128)(2,1)S(1)}, bf16[1,2,2,3,32,256]{5,4,3,2,1,0:T(8,128)(2,1)S(1)}, u32[]{:S(2)}, u32[]{:S(2)}) collective-permute-start(bf16[1,2,2,3,32,256]{5,4,3,2,1,0:T(8,128)(2,1)S(1)} %get-tuple-element.101), channel_id=1, source_target_pairs={{0,3},{1,2},{2,1},{3,0},{4,7},{5,6},{6,5},{7,4},{8,11},{9,10},{10,... | collective-permute-start | bytes 589832 | tf_op jit(solution)/shard_map/ppermute | solution.py:298
  80.5 0.8 collective-permute-done.14.refs_1_
  81.4 4.0 %collective-permute-done.20.got = bf16[1,2,2,3,32,256]{5,4,3,2,1,0:T(8,128)(2,1)S(1)} collective-permute-done((bf16[1,2,2,3,32,256]{5,4,3,2,1,0:T(8,128)(2,1)S(1)}, bf16[1,2,2,3,32,256]{5,4,3,2,1,0:T(8,128)(2,1)S(1)}, u32[]{:S(2)}, u32[]{:S(2)}) %collective-permute-start.20) | collective-permute-done | bytes 196640 | tf_op jit(solution)/shard_map/ppermute | solution.py:298
  85.4 1.1 %finish.1 = f32[2,2,9,32,256]{4,3,2,1,0:T(8,128)} custom-call(f32[2,2,6,32,256]{4,3,2,1,0:T(8,128)S(1)} %finish_some.1.some, bf16[1,2,2,3,32,256]{5,4,3,2,1,0:T(8,128)(2,1)S(1)} %get-tuple-element.100.keep, bf16[1,2,2,3,32,256]{5,4,3,2,1,0:T(8,128)(2,1)S(1)} %collective-permute-done.20.got), custom_call_target="tpu_custom_call" | custom-call | flops 603979776 | bytes 1024 | tf_op jit(solution)/shard_map/finish/pallas_call | solution.py:51
  (41 shorter events, 4.3 us)
Async XLA Ops:
  0.6 2.9 %slice-start = ((s8[4718592]{0:T(1024)(128)(4,1)}), s8[4194304]{0:T(1024)(128)(4,1)S(1)}, s32[]{:S(2)}) async-start(s8[4718592]{0:T(1024)(128)(4,1)} %bitcast.12), calls=%async_computation | async-start | bytes 8388608
  0.6 0.8 copy-start.4
  1.5 2.1 %slice-start.1 = ((s8[4718592]{0:T(1024)(128)(4,1)}), s8[524288]{0:T(1024)(128)(4,1)S(1)}, s32[]{:S(2)}) async-start(s8[4718592]{0:T(1024)(128)(4,1)} %bitcast.12), calls=%async_computation.1 | async-start | bytes 1048576
  5.2 6.6 %collective-permute-start = (bf16[512,256]{1,0:T(8,128)(2,1)S(1)}, bf16[512,256]{1,0:T(8,128)(2,1)S(1)}, u32[]{:S(2)}, u32[]{:S(2)}) collective-permute-start(bf16[512,256]{1,0:T(8,128)(2,1)S(1)} %late_1_0.1.refs_1_), channel_id=1, source_target_pairs={{0,8},{16,24},{32,40},{48,56},{64,72},{80,88},{96,104},{112,120},{... | collective-permute-start | bytes 786440 | tf_op jit(solution)/shard_map/ppermute | solution.py:294
  6.1 5.7 %copy-start = (bf16[2,1,4,1,16,32,256]{6,5,4,3,2,1,0:T(8,128)(2,1)S(1)}, bf16[2,1,4,1,16,32,256]{6,5,4,3,2,1,0:T(8,128)(2,1)}, u32[]{:S(2)}) copy-start(bf16[2,1,4,1,16,32,256]{6,5,4,3,2,1,0:T(8,128)(2,1)} %param.10) | copy-start | bytes 6291460
  6.2 5.7 %copy-start.1 = (bf16[2,1,4,1,16,32,256]{6,5,4,3,2,1,0:T(8,128)(2,1)S(1)}, bf16[2,1,4,1,16,32,256]{6,5,4,3,2,1,0:T(8,128)(2,1)}, u32[]{:S(2)}) copy-start(bf16[2,1,4,1,16,32,256]{6,5,4,3,2,1,0:T(8,128)(2,1)} %param.11) | copy-start | bytes 6291460
  7.0 9.9 %collective-permute-start.2 = (bf16[512,256]{1,0:T(8,128)(2,1)S(1)}, bf16[512,256]{1,0:T(8,128)(2,1)S(1)}, u32[]{:S(2)}, u32[]{:S(2)}) collective-permute-start(bf16[512,256]{1,0:T(8,128)(2,1)S(1)} %late_0_0.1.refs_1_), channel_id=1, source_target_pairs={{8,16},{24,32},{40,48},{56,64},{72,80},{88,96},{104,112},{16,8},{3... | collective-permute-start | bytes 786440 | tf_op jit(solution)/shard_map/ppermute | solution.py:294
  12.8 4.1 %copy-start.3 = (bf16[3,1,16,32,256]{4,3,2,1,0:T(8,128)(2,1)S(1)}, bf16[3,1,16,32,256]{4,3,2,1,0:T(8,128)(2,1)}, u32[]{:S(2)}) copy-start(bf16[3,1,16,32,256]{4,3,2,1,0:T(8,128)(2,1)} %param.8) | copy-start | bytes 2359300
  13.7 9.8 %collective-permute-start.1 = (bf16[512,256]{1,0:T(8,128)(2,1)S(1)}, bf16[512,256]{1,0:T(8,128)(2,1)S(1)}, u32[]{:S(2)}, u32[]{:S(2)}) collective-permute-start(bf16[512,256]{1,0:T(8,128)(2,1)S(1)} %late_0_1.1.refs_5_), channel_id=1, source_target_pairs={{8,16},{24,32},{40,48},{56,64},{72,80},{88,96},{104,112},{16,8},{3... | collective-permute-start | bytes 786440 | tf_op jit(solution)/shard_map/ppermute | solution.py:294
  18.0 1.6 %copy-start.2 = (bf16[2,1,4,1,16,32,256]{6,5,4,3,2,1,0:T(8,128)(2,1)S(1)}, bf16[2,1,4,1,16,32,256]{6,5,4,3,2,1,0:T(8,128)(2,1)}, u32[]{:S(2)}) copy-start(bf16[2,1,4,1,16,32,256]{6,5,4,3,2,1,0:T(8,128)(2,1)} %param.9) | copy-start | bytes 6291460
  18.8 6.5 %collective-permute-start.4 = (bf16[512,256]{1,0:T(8,128)(2,1)S(1)}, bf16[512,256]{1,0:T(8,128)(2,1)S(1)}, u32[]{:S(2)}, u32[]{:S(2)}) collective-permute-start(bf16[512,256]{1,0:T(8,128)(2,1)S(1)} %late_1_1.1.refs_5_), channel_id=1, source_target_pairs={{0,8},{16,24},{32,40},{48,56},{64,72},{80,88},{96,104},{112,120},{... | collective-permute-start | bytes 786440 | tf_op jit(solution)/shard_map/ppermute | solution.py:294
  27.2 9.8 %collective-permute-start.5 = (bf16[512,256]{1,0:T(8,128)(2,1)S(1)}, bf16[512,256]{1,0:T(8,128)(2,1)S(1)}, u32[]{:S(2)}, u32[]{:S(2)}) collective-permute-start(bf16[512,256]{1,0:T(8,128)(2,1)S(1)} %late_0_2.1.refs_2_), channel_id=1, source_target_pairs={{8,16},{24,32},{40,48},{56,64},{72,80},{88,96},{104,112},{16,8},{3... | collective-permute-start | bytes 786440 | tf_op jit(solution)/shard_map/ppermute | solution.py:294
  31.1 5.9 %collective-permute-start.3 = (bf16[512,256]{1,0:T(8,128)(2,1)S(1)}, bf16[512,256]{1,0:T(8,128)(2,1)S(1)}, u32[]{:S(2)}, u32[]{:S(2)}) collective-permute-start(bf16[512,256]{1,0:T(8,128)(2,1)S(1)} %late_1_2.1.refs_3_), channel_id=1, source_target_pairs={{0,8},{16,24},{32,40},{48,56},{64,72},{80,88},{96,104},{112,120},{... | collective-permute-start | bytes 786440 | tf_op jit(solution)/shard_map/ppermute | solution.py:294
  39.3 13.9 %collective-permute-start.8 = (bf16[4,2,3,32,256]{4,3,2,1,0:T(8,128)(2,1)S(1)}, bf16[4,2,3,32,256]{4,3,2,1,0:T(8,128)(2,1)S(1)}, u32[]{:S(2)}, u32[]{:S(2)}) collective-permute-start(bf16[4,2,3,32,256]{4,3,2,1,0:T(8,128)(2,1)S(1)} %get-tuple-element.73), channel_id=1, source_target_pairs={{0,1},{1,0},{2,3},{3,2},{4,5},{5,4},{6,7},{7,6},{8,9},{9,8},{10,11... | collective-permute-start | bytes 1179656 | tf_op jit(solution)/shard_map/ppermute | solution.py:298
  41.3 12.8 %collective-permute-start.9 = (bf16[4,2,3,32,256]{4,3,2,1,0:T(8,128)(2,1)S(1)}, bf16[4,2,3,32,256]{4,3,2,1,0:T(8,128)(2,1)S(1)}, u32[]{:S(2)}, u32[]{:S(2)}) collective-permute-start(bf16[4,2,3,32,256]{4,3,2,1,0:T(8,128)(2,1)S(1)} %get-tuple-element.74), channel_id=1, source_target_pairs={{0,3},{1,2},{2,1},{3,0},{4,7},{5,6},{6,5},{7,4},{8,11},{9,10},{10,... | collective-permute-start | bytes 1179656 | tf_op jit(solution)/shard_map/ppermute | solution.py:298
  43.9 11.5 %collective-permute-start.10 = (bf16[4,2,3,32,256]{4,3,2,1,0:T(8,128)(2,1)S(1)}, bf16[4,2,3,32,256]{4,3,2,1,0:T(8,128)(2,1)S(1)}, u32[]{:S(2)}, u32[]{:S(2)}) collective-permute-start(bf16[4,2,3,32,256]{4,3,2,1,0:T(8,128)(2,1)S(1)} %get-tuple-element.75), channel_id=1, source_target_pairs={{0,4},{1,5},{2,6},{3,7},{4,0},{5,1},{6,2},{7,3},{8,12},{9,13},{10,... | collective-permute-start | bytes 1179656 | tf_op jit(solution)/shard_map/ppermute | solution.py:298
  51.5 9.8 %collective-permute-start.6 = (bf16[4,2,3,32,256]{4,3,2,1,0:T(8,128)(2,1)S(1)}, bf16[4,2,3,32,256]{4,3,2,1,0:T(8,128)(2,1)S(1)}, u32[]{:S(2)}, u32[]{:S(2)}) collective-permute-start(bf16[4,2,3,32,256]{4,3,2,1,0:T(8,128)(2,1)S(1)} %get-tuple-element.67), channel_id=1, source_target_pairs={{0,1},{1,0},{2,3},{3,2},{4,5},{5,4},{6,7},{7,6},{8,9},{9,8},{10,11... | collective-permute-start | bytes 1179656 | tf_op jit(solution)/shard_map/ppermute | solution.py:298
  52.6 13.3 %collective-permute-start.15 = (bf16[4,2,3,32,256]{4,3,2,1,0:T(8,128)(2,1)S(1)}, bf16[4,2,3,32,256]{4,3,2,1,0:T(8,128)(2,1)S(1)}, u32[]{:S(2)}, u32[]{:S(2)}) collective-permute-start(bf16[4,2,3,32,256]{4,3,2,1,0:T(8,128)(2,1)S(1)} %get-tuple-element.87), channel_id=1, source_target_pairs={{0,3},{1,2},{2,1},{3,0},{4,7},{5,6},{6,5},{7,4},{8,11},{9,10},{10,... | collective-permute-start | bytes 1179656 | tf_op jit(solution)/shard_map/ppermute | solution.py:298
  53.2 13.4 %collective-permute-start.18 = (bf16[4,2,3,32,256]{4,3,2,1,0:T(8,128)(2,1)S(1)}, bf16[4,2,3,32,256]{4,3,2,1,0:T(8,128)(2,1)S(1)}, u32[]{:S(2)}, u32[]{:S(2)}) collective-permute-start(bf16[4,2,3,32,256]{4,3,2,1,0:T(8,128)(2,1)S(1)} %get-tuple-element.95), channel_id=1, source_target_pairs={{0,4},{1,5},{2,6},{3,7},{4,0},{5,1},{6,2},{7,3},{8,12},{9,13},{10,... | collective-permute-start | bytes 1179656 | tf_op jit(solution)/shard_map/ppermute | solution.py:298
  55.6 13.7 %collective-permute-start.11 = (bf16[2,2,3,32,256]{4,3,2,1,0:T(8,128)(2,1)S(1)}, bf16[2,2,3,32,256]{4,3,2,1,0:T(8,128)(2,1)S(1)}, u32[]{:S(2)}, u32[]{:S(2)}) collective-permute-start(bf16[2,2,3,32,256]{4,3,2,1,0:T(8,128)(2,1)S(1)} %get-tuple-element.79), channel_id=1, source_target_pairs={{0,3},{1,2},{2,1},{3,0},{4,7},{5,6},{6,5},{7,4},{8,11},{9,10},{10,... | collective-permute-start | bytes 589832 | tf_op jit(solution)/shard_map/ppermute | solution.py:298
  58.5 11.7 %collective-permute-start.12 = (bf16[2,2,3,32,256]{4,3,2,1,0:T(8,128)(2,1)S(1)}, bf16[2,2,3,32,256]{4,3,2,1,0:T(8,128)(2,1)S(1)}, u32[]{:S(2)}, u32[]{:S(2)}) collective-permute-start(bf16[2,2,3,32,256]{4,3,2,1,0:T(8,128)(2,1)S(1)} %get-tuple-element.80), channel_id=1, source_target_pairs={{0,4},{1,5},{2,6},{3,7},{4,0},{5,1},{6,2},{7,3},{8,12},{9,13},{10,... | collective-permute-start | bytes 589832 | tf_op jit(solution)/shard_map/ppermute | solution.py:298
  61.2 9.0 %collective-permute-start.13 = (bf16[2,2,3,32,256]{4,3,2,1,0:T(8,128)(2,1)S(1)}, bf16[2,2,3,32,256]{4,3,2,1,0:T(8,128)(2,1)S(1)}, u32[]{:S(2)}, u32[]{:S(2)}) collective-permute-start(bf16[2,2,3,32,256]{4,3,2,1,0:T(8,128)(2,1)S(1)} %get-tuple-element.81), channel_id=1, source_target_pairs={{0,1},{1,0},{2,3},{3,2},{4,5},{5,4},{6,7},{7,6},{8,9},{9,8},{10,11... | collective-permute-start | bytes 589832 | tf_op jit(solution)/shard_map/ppermute | solution.py:298
  65.9 6.9 %collective-permute-start.7 = (bf16[2,2,3,32,256]{4,3,2,1,0:T(8,128)(2,1)S(1)}, bf16[2,2,3,32,256]{4,3,2,1,0:T(8,128)(2,1)S(1)}, u32[]{:S(2)}, u32[]{:S(2)}) collective-permute-start(bf16[2,2,3,32,256]{4,3,2,1,0:T(8,128)(2,1)S(1)} %get-tuple-element.69), channel_id=1, source_target_pairs={{0,3},{1,2},{2,1},{3,0},{4,7},{5,6},{6,5},{7,4},{8,11},{9,10},{10,... | collective-permute-start | bytes 589832 | tf_op jit(solution)/shard_map/ppermute | solution.py:298
  66.6 7.3 %collective-permute-start.16 = (bf16[2,2,3,32,256]{4,3,2,1,0:T(8,128)(2,1)S(1)}, bf16[2,2,3,32,256]{4,3,2,1,0:T(8,128)(2,1)S(1)}, u32[]{:S(2)}, u32[]{:S(2)}) collective-permute-start(bf16[2,2,3,32,256]{4,3,2,1,0:T(8,128)(2,1)S(1)} %get-tuple-element.89), channel_id=1, source_target_pairs={{0,4},{1,5},{2,6},{3,7},{4,0},{5,1},{6,2},{7,3},{8,12},{9,13},{10,... | collective-permute-start | bytes 589832 | tf_op jit(solution)/shard_map/ppermute | solution.py:298
  69.3 9.0 %collective-permute-start.19 = (bf16[2,2,3,32,256]{4,3,2,1,0:T(8,128)(2,1)S(1)}, bf16[2,2,3,32,256]{4,3,2,1,0:T(8,128)(2,1)S(1)}, u32[]{:S(2)}, u32[]{:S(2)}) collective-permute-start(bf16[2,2,3,32,256]{4,3,2,1,0:T(8,128)(2,1)S(1)} %get-tuple-element.97), channel_id=1, source_target_pairs={{0,1},{1,0},{2,3},{3,2},{4,5},{5,4},{6,7},{7,6},{8,9},{9,8},{10,11... | collective-permute-start | bytes 589832 | tf_op jit(solution)/shard_map/ppermute | solution.py:298
  73.9 6.6 %collective-permute-start.17 = (bf16[1,2,2,3,32,256]{5,4,3,2,1,0:T(8,128)(2,1)S(1)}, bf16[1,2,2,3,32,256]{5,4,3,2,1,0:T(8,128)(2,1)S(1)}, u32[]{:S(2)}, u32[]{:S(2)}) collective-permute-start(bf16[1,2,2,3,32,256]{5,4,3,2,1,0:T(8,128)(2,1)S(1)} %get-tuple-element.93), channel_id=1, source_target_pairs={{0,1},{1,0},{2,3},{3,2},{4,5},{5,4},{6,7},{7,6},{8,9},{9,8},{10,11... | collective-permute-start | bytes 589832 | tf_op jit(solution)/shard_map/ppermute | solution.py:298
  74.1 7.2 %collective-permute-start.14 = (bf16[1,2,2,3,32,256]{5,4,3,2,1,0:T(8,128)(2,1)S(1)}, bf16[1,2,2,3,32,256]{5,4,3,2,1,0:T(8,128)(2,1)S(1)}, u32[]{:S(2)}, u32[]{:S(2)}) collective-permute-start(bf16[1,2,2,3,32,256]{5,4,3,2,1,0:T(8,128)(2,1)S(1)} %get-tuple-element.85), channel_id=1, source_target_pairs={{0,4},{1,5},{2,6},{3,7},{4,0},{5,1},{6,2},{7,3},{8,12},{9,13},{10,... | collective-permute-start | bytes 589832 | tf_op jit(solution)/shard_map/ppermute | solution.py:298
  78.4 7.0 %collective-permute-start.20 = (bf16[1,2,2,3,32,256]{5,4,3,2,1,0:T(8,128)(2,1)S(1)}, bf16[1,2,2,3,32,256]{5,4,3,2,1,0:T(8,128)(2,1)S(1)}, u32[]{:S(2)}, u32[]{:S(2)}) collective-permute-start(bf16[1,2,2,3,32,256]{5,4,3,2,1,0:T(8,128)(2,1)S(1)} %get-tuple-element.101), channel_id=1, source_target_pairs={{0,3},{1,2},{2,1},{3,0},{4,7},{5,6},{6,5},{7,4},{8,11},{9,10},{10,... | collective-permute-start | bytes 589832 | tf_op jit(solution)/shard_map/ppermute | solution.py:298

commit v4 on v3

--- a/solution.py
+++ b/solution.py
@@ -33,6 +33,7 @@
 SM = pl.BlockSpec(memory_space=pltpu.SMEM)
 HB = pl.BlockSpec(memory_space=pltpu.HBM)
 FIELD = jax.ShapeDtypeStruct((PIX, CH), BF)
+MARK = jax.ShapeDtypeStruct((8, 128), F32)
 SUMS = jax.ShapeDtypeStruct((9, CH, CH), F32)
 WINDOWS = pltpu.VMEM((3, PIX + 2 * COLS, CH), BF)
 
@@ -240,7 +241,8 @@
             put_shares(staged[role], k, sends, keeps, role)
 
 
-def last_late_kernel(taps, g1_zero, g1_one, out, *wins):
+def last_late_kernel(taps, g1_zero, g1_one, out, mark, *wins):
+    mark[...] = jnp.zeros(MARK.shape, F32)
     for role in range(2):
         half = half_of(role)
         fill_windows(wins[role], (g1_zero, g1_one)[role][...].astype(F32))
@@ -402,11 +404,11 @@
     )
     keeps1 = res[3:6]
     gots1 = [exchange(res[o], ORDERS[o][0]) for o in range(3)]
-    final = call(
+    final, mark = call(
         last_late_kernel,
         f"late_{TICKS - 1}",
         (taps, *g1s),
-        jax.ShapeDtypeStruct((2, PIX, CH), BF),
+        (jax.ShapeDtypeStruct((2, PIX, CH), BF), MARK),
         scratch=windows * 2,
         ops=2,
     )
@@ -418,9 +420,11 @@
     gots2 = [exchange(res[o], ORDERS[o][1]) for o in range(3)]
     begun = call(fold_two_last_kernel, "fold_two_last", (*res[3:6], *gots2), (part3,) * 6, ops=FOLD_COST)
     firsts = []
+    order = [mark]
     for o in range(3):
-        send, keep = call(fold_in, f"fold_one_{o}", (keeps1[o], gots1[o]), (part2, part2), after=firsts[-1:])
+        send, keep = call(fold_in, f"fold_one_{o}", (keeps1[o], gots1[o]), (part2, part2), after=order[-1:])
         firsts.append(keep)
+        order.append(keep)
         gots1[o] = exchange(send, ORDERS[o][1])
     lasts = []
     for o in range(3):

time: 87.4 us -> 85.8 us (0.982)
  waiting for transfers between devices: 19 us -> 16 us
    ppermute x15, waiting for transfers between devices: 16.7 us -> 13.8 us  [exchange(): return lax.ppermute(block, 'dp', PAIRS[step])]
  transfers between devices with their start and end apart: 21 -> 21, of which waited for: 12 -> 13; matrix products, arithmetic and copies ran while one was open for 0% -> 0% of each run, Pallas kernels for 27% -> 27%
where the time goes in v4:
time: 85.8 us; the launch traced here: 84.3 us
  starting transfers between devices  33.9 us (40%)
  Pallas kernels  32 us (37%)
  waiting for transfers between devices  16 us (19%)
  local copies, waits for them, and re-layouts  1.33 us (2%)
  between operations  0.97 us (1%)
    pallas_call x31, Pallas kernels, call(): pl.pallas_call(body if after else kernel, out_shape=outs, in_specs=[VM] *...  30 us
    ppermute x15, starting transfers between devices, exchange(): return lax.ppermute(block, 'dp', PAIRS[step])  21.8 us
    ppermute x15, waiting for transfers between devices, exchange(): return lax.ppermute(block, 'dp', PAIRS[step])  13.8 us
    ppermute x6, starting transfers between devices, relay(): return lax.ppermute(block, 'section', pairs + [(b, a) for a, b in pairs])  12.2 us
    ppermute x6, waiting for transfers between devices, relay(): return lax.ppermute(block, 'section', pairs + [(b, a) for a, b in pairs])  2.22 us
    pallas_call x1, Pallas kernels, prepare(): pl.pallas_call(prepare_kernel, grid_spec=pltpu.PrefetchScalarGridSpec(num...  2.04 us
  transfers between devices with their start and end apart: 21, of which 13 were waited for; matrix products, arithmetic and copies ran while one was open for 0% of the time, Pallas kernels for 27%

profile of v4, /device:TPU:8, one launch (start us, length us, event | category | flops | bytes accessed | tf_op | source)
XLA Modules:
  0.0 84.3 jit_solution(8701748265381363305)
XLA Ops:
  0.7 0.8 copy-done.4
  1.5 2.0 %prepare.1 = (bf16[512,256]{1,0:T(8,128)(2,1)S(1)}, bf16[512,256]{1,0:T(8,128)(2,1)S(1)}, bf16[512,256]{1,0:T(8,128)(2,1)S(1)}, bf16[512,256]{1,0:T(8,128)(2,1)S(1)}) custom-call(s32[4,32]{1,0:T(4,128)S(1)} %copy-done.4, bf16[2,512,256]{2,1,0:T(8,128)(2,1)} %bitcast.53, bf16[2,512,256]{2,1,0:T(8,128)(2,1)} %bitcast.54, bf16[8,512,256]{2,1,0:T(8,128)(2,1)} %bitcast.40, ...), custom_call_target="tpu_custom_call" | custom-call | flops 1 | bytes 1024 | tf_op jit(solution)/shard_map/prepare/pallas_call | solution.py:130
  3.5 0.8 early_1_0.1.g1.refs_0_
  4.4 0.8 late_1_0.1.refs_1_
  5.3 0.8 early_0_0.1.refs_0_.g1
  6.2 0.8 late_0_0.1.refs_1_
  7.0 4.8 %collective-permute-start.2 = (bf16[512,256]{1,0:T(8,128)(2,1)S(1)}, bf16[512,256]{1,0:T(8,128)(2,1)S(1)}, u32[]{:S(2)}, u32[]{:S(2)}) collective-permute-start(bf16[512,256]{1,0:T(8,128)(2,1)S(1)} %late_0_0.1.refs_1_), channel_id=1, source_target_pairs={{8,16},{24,32},{40,48},{56,64},{72,80},{88,96},{104,112},{16,8},{3... | collective-permute-start | bytes 786440 | tf_op jit(solution)/shard_map/ppermute | solution.py:296
  11.8 1.0 %early_0_1.1 = (bf16[512,256]{1,0:T(8,128)(2,1)S(1)}, bf16[512,256]{1,0:T(8,128)(2,1)S(1)}) custom-call(s32[4,32]{1,0:T(4,128)S(1)} %copy-done.4, bf16[8,512,256]{2,1,0:T(8,128)(2,1)S(1)} %bitcast.31, bf16[8,512,256]{2,1,0:T(8,128)(2,1)S(1)} %bitcast.42, bf16[36,256,256]{2,1,0:T(8,128)(2,1)S(1)} %bitcast.18, ...), custom_call_target="tpu_custom_call" | custom-call | flops 603979776 | bytes 1024 | tf_op jit(solution)/shard_map/early_0_1/pallas_call | solution.py:52
  12.8 0.8 late_0_1.1.refs_5_
  13.7 3.0 %collective-permute-start.1 = (bf16[512,256]{1,0:T(8,128)(2,1)S(1)}, bf16[512,256]{1,0:T(8,128)(2,1)S(1)}, u32[]{:S(2)}, u32[]{:S(2)}) collective-permute-start(bf16[512,256]{1,0:T(8,128)(2,1)S(1)} %late_0_1.1.refs_5_), channel_id=1, source_target_pairs={{8,16},{24,32},{40,48},{56,64},{72,80},{88,96},{104,112},{16,8},{3... | collective-permute-start | bytes 786440 | tf_op jit(solution)/shard_map/ppermute | solution.py:296
  16.9 1.0 %early_1_1.1 = (bf16[512,256]{1,0:T(8,128)(2,1)S(1)}, bf16[512,256]{1,0:T(8,128)(2,1)S(1)}) custom-call(s32[4,32]{1,0:T(4,128)S(1)} %copy-done.4, bf16[8,512,256]{2,1,0:T(8,128)(2,1)S(1)} %bitcast.32, bf16[8,512,256]{2,1,0:T(8,128)(2,1)S(1)} %bitcast.43, bf16[36,256,256]{2,1,0:T(8,128)(2,1)S(1)} %bitcast.20, ...), custom_call_target="tpu_custom_call" | custom-call | flops 603979776 | bytes 1024 | tf_op jit(solution)/shard_map/early_1_1/pallas_call | solution.py:52
  18.0 0.8 late_1_1.1.refs_5_
  19.6 1.6 %wgrad1_1.1.refs_8_.refs_7_.refs_5_ = f32[9,256,256]{2,1,0:T(8,128)S(1)} custom-call(s32[4,32]{1,0:T(4,128)S(1)} %copy-done.4, bf16[8,512,256]{2,1,0:T(8,128)(2,1)S(1)} %bitcast.47, bf16[512,256]{1,0:T(8,128)(2,1)S(1)} %early_1_0.1.g1.refs_0_, bf16[512,256]{1,0:T(8,128)(2,1)S(1)} %get-tuple-element.59.refs_1_.g1), custom_call_target="tpu_custom_call" | custom-call | flops 1207959552 | bytes 1024 | tf_op jit(solution)/shard_map/wgrad1_1/pallas_call | solution.py:52
  21.1 1.6 %wgrad1_0.1.refs_7_.refs_6_.refs_4_ = f32[9,256,256]{2,1,0:T(8,128)S(1)} custom-call(s32[4,32]{1,0:T(4,128)S(1)} %copy-done.4, bf16[8,512,256]{2,1,0:T(8,128)(2,1)S(1)} %bitcast.48, bf16[512,256]{1,0:T(8,128)(2,1)S(1)} %early_0_0.1.refs_0_.g1, bf16[512,256]{1,0:T(8,128)(2,1)S(1)} %get-tuple-element.56.g1.refs_1_), custom_call_target="tpu_custom_call" | custom-call | flops 1207959552 | bytes 1024 | tf_op jit(solution)/shard_map/wgrad1_0/pallas_call | solution.py:52
  23.5 1.0 %early_1_2.1 = (bf16[512,256]{1,0:T(8,128)(2,1)S(1)}, bf16[512,256]{1,0:T(8,128)(2,1)S(1)}) custom-call(s32[4,32]{1,0:T(4,128)S(1)} %copy-done.4, bf16[8,512,256]{2,1,0:T(8,128)(2,1)S(1)} %bitcast.33, bf16[8,512,256]{2,1,0:T(8,128)(2,1)S(1)} %bitcast.44, bf16[36,256,256]{2,1,0:T(8,128)(2,1)S(1)} %bitcast.22, ...), custom_call_target="tpu_custom_call" | custom-call | flops 603979776 | bytes 1024 | tf_op jit(solution)/shard_map/early_1_2/pallas_call | solution.py:52
  24.5 0.8 late_1_2.1.refs_3_
  25.3 1.0 %early_0_2.1 = (bf16[512,256]{1,0:T(8,128)(2,1)S(1)}, bf16[512,256]{1,0:T(8,128)(2,1)S(1)}) custom-call(s32[4,32]{1,0:T(4,128)S(1)} %copy-done.4, bf16[8,512,256]{2,1,0:T(8,128)(2,1)S(1)} %bitcast.34, bf16[8,512,256]{2,1,0:T(8,128)(2,1)S(1)} %bitcast.45, bf16[36,256,256]{2,1,0:T(8,128)(2,1)S(1)} %bitcast.24, ...), custom_call_target="tpu_custom_call" | custom-call | flops 603979776 | bytes 1024 | tf_op jit(solution)/shard_map/early_0_2/pallas_call | solution.py:52
  26.3 0.8 late_0_2.1.refs_2_
  27.2 3.9 %collective-permute-start.5 = (bf16[512,256]{1,0:T(8,128)(2,1)S(1)}, bf16[512,256]{1,0:T(8,128)(2,1)S(1)}, u32[]{:S(2)}, u32[]{:S(2)}) collective-permute-start(bf16[512,256]{1,0:T(8,128)(2,1)S(1)} %late_0_2.1.refs_2_), channel_id=1, source_target_pairs={{8,16},{24,32},{40,48},{56,64},{72,80},{88,96},{104,112},{16,8},{3... | collective-permute-start | bytes 786440 | tf_op jit(solution)/shard_map/ppermute | solution.py:296
  31.2 2.3 %wgrad2_1.1.refs_5_ = f32[9,256,256]{2,1,0:T(8,128)S(1)} custom-call(s32[4,32]{1,0:T(4,128)S(1)} %copy-done.4, bf16[8,512,256]{2,1,0:T(8,128)(2,1)S(1)} %bitcast.35, bf16[512,256]{1,0:T(8,128)(2,1)S(1)} %get-tuple-element.55.g2.refs_0_, bf16[512,256]{1,0:T(8,128)(2,1)S(1)} %get-tuple-element.64.refs_1_, bf16[512,256]{1,0:T(8,128)(2,1)S(1)} %get-tuple-element.65.refs_2_), custom_call_target="tpu_custom_call" | custom-call | flops 1811939328 | bytes 1024 | tf_op jit(solution)/shard_map/wgrad2_1/pallas_call | solution.py:52
  33.5 2.3 %wgrad2_0.1.refs_4_ = f32[9,256,256]{2,1,0:T(8,128)S(1)} custom-call(s32[4,32]{1,0:T(4,128)S(1)} %copy-done.4, bf16[8,512,256]{2,1,0:T(8,128)(2,1)S(1)} %bitcast.36, bf16[512,256]{1,0:T(8,128)(2,1)S(1)} %get-tuple-element.58.g2.refs_0_, bf16[512,256]{1,0:T(8,128)(2,1)S(1)} %get-tuple-element.62.refs_1_, bf16[512,256]{1,0:T(8,128)(2,1)S(1)} %get-tuple-element.63.refs_2_), custom_call_target="tpu_custom_call" | custom-call | flops 1811939328 | bytes 1024 | tf_op jit(solution)/shard_map/wgrad2_0/pallas_call | solution.py:52
  35.7 1.2 %collective-permute-done.5.refs_1_ = bf16[512,256]{1,0:T(8,128)(2,1)S(1)} collective-permute-done((bf16[512,256]{1,0:T(8,128)(2,1)S(1)}, bf16[512,256]{1,0:T(8,128)(2,1)S(1)}, u32[]{:S(2)}, u32[]{:S(2)}) %collective-permute-start.5) | collective-permute-done | bytes 262176 | tf_op jit(solution)/shard_map/ppermute | solution.py:296
  37.0 2.3 %last_two.1 = (bf16[4,2,3,32,256]{4,3,2,1,0:T(8,128)(2,1)S(1)}, bf16[4,2,3,32,256]{4,3,2,1,0:T(8,128)(2,1)S(1)}, bf16[4,2,3,32,256]{4,3,2,1,0:T(8,128)(2,1)S(1)}...) custom-call(s32[4,32]{1,0:T(4,128)S(1)} %copy-done.4, ...), custom_call_target="tpu_custom_call" | custom-call | flops 1207959552 | bytes 1024 | tf_op jit(solution)/shard_map/last_two/pallas_call | solution.py:52
  39.3 2.0 %collective-permute-start.8 = (bf16[4,2,3,32,256]{4,3,2,1,0:T(8,128)(2,1)S(1)}, bf16[4,2,3,32,256]{4,3,2,1,0:T(8,128)(2,1)S(1)}, u32[]{:S(2)}, u32[]{:S(2)}) collective-permute-start(bf16[4,2,3,32,256]{4,3,2,1,0:T(8,128)(2,1)S(1)} %get-tuple-element.77), channel_id=1, source_target_pairs={{0,1},{1,0},{2,3},{3,2},{4,5},{5,4},{6,7},{7,6},{8,9},{9,8},{10,11... | collective-permute-start | bytes 1179656 | tf_op jit(solution)/shard_map/ppermute | solution.py:300
  41.3 2.5 %collective-permute-start.9 = (bf16[4,2,3,32,256]{4,3,2,1,0:T(8,128)(2,1)S(1)}, bf16[4,2,3,32,256]{4,3,2,1,0:T(8,128)(2,1)S(1)}, u32[]{:S(2)}, u32[]{:S(2)}) collective-permute-start(bf16[4,2,3,32,256]{4,3,2,1,0:T(8,128)(2,1)S(1)} %get-tuple-element.78), channel_id=1, source_target_pairs={{0,3},{1,2},{2,1},{3,0},{4,7},{5,6},{6,5},{7,4},{8,11},{9,10},{10,... | collective-permute-start | bytes 1179656 | tf_op jit(solution)/shard_map/ppermute | solution.py:300
  43.9 2.6 %collective-permute-start.10 = (bf16[4,2,3,32,256]{4,3,2,1,0:T(8,128)(2,1)S(1)}, bf16[4,2,3,32,256]{4,3,2,1,0:T(8,128)(2,1)S(1)}, u32[]{:S(2)}, u32[]{:S(2)}) collective-permute-start(bf16[4,2,3,32,256]{4,3,2,1,0:T(8,128)(2,1)S(1)} %get-tuple-element.79), channel_id=1, source_target_pairs={{0,4},{1,5},{2,6},{3,7},{4,0},{5,1},{6,2},{7,3},{8,12},{9,13},{10,... | collective-permute-start | bytes 1179656 | tf_op jit(solution)/shard_map/ppermute | solution.py:300
  47.3 0.8 early_1_3.1.g1_one.refs_3_
  48.1 3.4 %last_one.1 = (bf16[4,2,3,32,256]{4,3,2,1,0:T(8,128)(2,1)S(1)}, bf16[4,2,3,32,256]{4,3,2,1,0:T(8,128)(2,1)S(1)}, bf16[4,2,3,32,256]{4,3,2,1,0:T(8,128)(2,1)S(1)}...) custom-call(s32[4,32]{1,0:T(4,128)S(1)} %copy-done.4, ...), custom_call_target="tpu_custom_call" | custom-call | flops 2415919104 | bytes 1024 | tf_op jit(solution)/shard_map/last_one/pallas_call | solution.py:52
  51.5 1.1 %collective-permute-start.6 = (bf16[4,2,3,32,256]{4,3,2,1,0:T(8,128)(2,1)S(1)}, bf16[4,2,3,32,256]{4,3,2,1,0:T(8,128)(2,1)S(1)}, u32[]{:S(2)}, u32[]{:S(2)}) collective-permute-start(bf16[4,2,3,32,256]{4,3,2,1,0:T(8,128)(2,1)S(1)} %get-tuple-element.70), channel_id=1, source_target_pairs={{0,1},{1,0},{2,3},{3,2},{4,5},{5,4},{6,7},{7,6},{8,9},{9,8},{10,11... | collective-permute-start | bytes 1179656 | tf_op jit(solution)/shard_map/ppermute | solution.py:300
  53.2 0.9 %collective-permute-start.18 = (bf16[4,2,3,32,256]{4,3,2,1,0:T(8,128)(2,1)S(1)}, bf16[4,2,3,32,256]{4,3,2,1,0:T(8,128)(2,1)S(1)}, u32[]{:S(2)}, u32[]{:S(2)}) collective-permute-start(bf16[4,2,3,32,256]{4,3,2,1,0:T(8,128)(2,1)S(1)} %get-tuple-element.99), channel_id=1, source_target_pairs={{0,4},{1,5},{2,6},{3,7},{4,0},{5,1},{6,2},{7,3},{8,12},{9,13},{10,... | collective-permute-start | bytes 1179656 | tf_op jit(solution)/shard_map/ppermute | solution.py:300
  54.2 1.2 %collective-permute-done.10.refs_5_ = bf16[4,2,3,32,256]{4,3,2,1,0:T(8,128)(2,1)S(1)} collective-permute-done((bf16[4,2,3,32,256]{4,3,2,1,0:T(8,128)(2,1)S(1)}, bf16[4,2,3,32,256]{4,3,2,1,0:T(8,128)(2,1)S(1)}, u32[]{:S(2)}, u32[]{:S(2)}) %collective-permute-start.10) | collective-permute-done | bytes 393248 | tf_op jit(solution)/shard_map/ppermute | solution.py:300
  55.6 2.9 %collective-permute-start.11 = (bf16[2,2,3,32,256]{4,3,2,1,0:T(8,128)(2,1)S(1)}, bf16[2,2,3,32,256]{4,3,2,1,0:T(8,128)(2,1)S(1)}, u32[]{:S(2)}, u32[]{:S(2)}) collective-permute-start(bf16[2,2,3,32,256]{4,3,2,1,0:T(8,128)(2,1)S(1)} %get-tuple-element.83), channel_id=1, source_target_pairs={{0,3},{1,2},{2,1},{3,0},{4,7},{5,6},{6,5},{7,4},{8,11},{9,10},{10,... | collective-permute-start | bytes 589832 | tf_op jit(solution)/shard_map/ppermute | solution.py:300
  58.5 1.3 %collective-permute-start.12 = (bf16[2,2,3,32,256]{4,3,2,1,0:T(8,128)(2,1)S(1)}, bf16[2,2,3,32,256]{4,3,2,1,0:T(8,128)(2,1)S(1)}, u32[]{:S(2)}, u32[]{:S(2)}) collective-permute-start(bf16[2,2,3,32,256]{4,3,2,1,0:T(8,128)(2,1)S(1)} %get-tuple-element.84), channel_id=1, source_target_pairs={{0,4},{1,5},{2,6},{3,7},{4,0},{5,1},{6,2},{7,3},{8,12},{9,13},{10,... | collective-permute-start | bytes 589832 | tf_op jit(solution)/shard_map/ppermute | solution.py:300
  59.8 1.5 %collective-permute-done.6.refs_1_ = bf16[4,2,3,32,256]{4,3,2,1,0:T(8,128)(2,1)S(1)} collective-permute-done((bf16[4,2,3,32,256]{4,3,2,1,0:T(8,128)(2,1)S(1)}, bf16[4,2,3,32,256]{4,3,2,1,0:T(8,128)(2,1)S(1)}, u32[]{:S(2)}, u32[]{:S(2)}) %collective-permute-start.6) | collective-permute-done | bytes 393248 | tf_op jit(solution)/shard_map/ppermute | solution.py:300
  61.2 0.8 collective-permute-start.13
  62.1 2.2 %late_3.1 = (bf16[2,512,256]{2,1,0:T(8,128)(2,1)}, f32[8,128]{1,0:T(8,128)S(1)}) custom-call(bf16[36,256,256]{2,1,0:T(8,128)(2,1)S(1)} %bitcast.28, bf16[512,256]{1,0:T(8,128)(2,1)S(1)} %early_0_3.1.g1_zero.refs_2_, bf16[512,256]{1,0:T(8,128)(2,1)S(1)} %early_1_3.1.g1_one.refs_3_), custom_call_target="tpu_custom_call" | custom-call | flops 1207959552 | bytes 1024 | tf_op jit(solution)/shard_map/late_3/pallas_call | solution.py:52
  65.1 0.9 %collective-permute-start.7 = (bf16[2,2,3,32,256]{4,3,2,1,0:T(8,128)(2,1)S(1)}, bf16[2,2,3,32,256]{4,3,2,1,0:T(8,128)(2,1)S(1)}, u32[]{:S(2)}, u32[]{:S(2)}) collective-permute-start(bf16[2,2,3,32,256]{4,3,2,1,0:T(8,128)(2,1)S(1)} %get-tuple-element.73), channel_id=1, source_target_pairs={{0,3},{1,2},{2,1},{3,0},{4,7},{5,6},{6,5},{7,4},{8,11},{9,10},{10,... | collective-permute-start | bytes 589832 | tf_op jit(solution)/shard_map/ppermute | solution.py:300
  66.1 1.8 %collective-permute-start.16 = (bf16[2,2,3,32,256]{4,3,2,1,0:T(8,128)(2,1)S(1)}, bf16[2,2,3,32,256]{4,3,2,1,0:T(8,128)(2,1)S(1)}, u32[]{:S(2)}, u32[]{:S(2)}) collective-permute-start(bf16[2,2,3,32,256]{4,3,2,1,0:T(8,128)(2,1)S(1)} %get-tuple-element.93), channel_id=1, source_target_pairs={{0,4},{1,5},{2,6},{3,7},{4,0},{5,1},{6,2},{7,3},{8,12},{9,13},{10,... | collective-permute-start | bytes 589832 | tf_op jit(solution)/shard_map/ppermute | solution.py:300
  68.0 0.8 collective-permute-done.11.refs_3_
  69.4 2.6 %collective-permute-done.7.got = bf16[2,2,3,32,256]{4,3,2,1,0:T(8,128)(2,1)S(1)} collective-permute-done((bf16[2,2,3,32,256]{4,3,2,1,0:T(8,128)(2,1)S(1)}, bf16[2,2,3,32,256]{4,3,2,1,0:T(8,128)(2,1)S(1)}, u32[]{:S(2)}, u32[]{:S(2)}) %collective-permute-start.7) | collective-permute-done | bytes 196640 | tf_op jit(solution)/shard_map/ppermute | solution.py:300
  72.0 1.3 %collective-permute-done.16.refs_1_ = bf16[2,2,3,32,256]{4,3,2,1,0:T(8,128)(2,1)S(1)} collective-permute-done((bf16[2,2,3,32,256]{4,3,2,1,0:T(8,128)(2,1)S(1)}, bf16[2,2,3,32,256]{4,3,2,1,0:T(8,128)(2,1)S(1)}, u32[]{:S(2)}, u32[]{:S(2)}) %collective-permute-start.16) | collective-permute-done | bytes 196640 | tf_op jit(solution)/shard_map/ppermute | solution.py:300
  73.4 0.8 collective-permute-start.17
  74.2 1.9 %collective-permute-start.14 = (bf16[1,2,2,3,32,256]{5,4,3,2,1,0:T(8,128)(2,1)S(1)}, bf16[1,2,2,3,32,256]{5,4,3,2,1,0:T(8,128)(2,1)S(1)}, u32[]{:S(2)}, u32[]{:S(2)}) collective-permute-start(bf16[1,2,2,3,32,256]{5,4,3,2,1,0:T(8,128)(2,1)S(1)} %get-tuple-element.89), channel_id=1, source_target_pairs={{0,4},{1,5},{2,6},{3,7},{4,0},{5,1},{6,2},{7,3},{8,12},{9,13},{10,... | collective-permute-start | bytes 589832 | tf_op jit(solution)/shard_map/ppermute | solution.py:300
  76.2 1.4 %collective-permute-start.20 = (bf16[1,2,2,3,32,256]{5,4,3,2,1,0:T(8,128)(2,1)S(1)}, bf16[1,2,2,3,32,256]{5,4,3,2,1,0:T(8,128)(2,1)S(1)}, u32[]{:S(2)}, u32[]{:S(2)}) collective-permute-start(bf16[1,2,2,3,32,256]{5,4,3,2,1,0:T(8,128)(2,1)S(1)} %get-tuple-element.105), channel_id=1, source_target_pairs={{0,3},{1,2},{2,1},{3,0},{4,7},{5,6},{6,5},{7,4},{8,11},{9,10},{10,... | collective-permute-start | bytes 589832 | tf_op jit(solution)/shard_map/ppermute | solution.py:300
  77.6 1.6 %collective-permute-done.17.refs_3_ = bf16[1,2,2,3,32,256]{5,4,3,2,1,0:T(8,128)(2,1)S(1)} collective-permute-done((bf16[1,2,2,3,32,256]{5,4,3,2,1,0:T(8,128)(2,1)S(1)}, bf16[1,2,2,3,32,256]{5,4,3,2,1,0:T(8,128)(2,1)S(1)}, u32[]{:S(2)}, u32[]{:S(2)}) %collective-permute-start.17) | collective-permute-done | bytes 196640 | tf_op jit(solution)/shard_map/ppermute | solution.py:300
  79.2 2.2 %collective-permute-done.14.refs_1_ = bf16[1,2,2,3,32,256]{5,4,3,2,1,0:T(8,128)(2,1)S(1)} collective-permute-done((bf16[1,2,2,3,32,256]{5,4,3,2,1,0:T(8,128)(2,1)S(1)}, bf16[1,2,2,3,32,256]{5,4,3,2,1,0:T(8,128)(2,1)S(1)}, u32[]{:S(2)}, u32[]{:S(2)}) %collective-permute-start.14) | collective-permute-done | bytes 196640 | tf_op jit(solution)/shard_map/ppermute | solution.py:300
  81.5 1.6 %collective-permute-done.20.got = bf16[1,2,2,3,32,256]{5,4,3,2,1,0:T(8,128)(2,1)S(1)} collective-permute-done((bf16[1,2,2,3,32,256]{5,4,3,2,1,0:T(8,128)(2,1)S(1)}, bf16[1,2,2,3,32,256]{5,4,3,2,1,0:T(8,128)(2,1)S(1)}, u32[]{:S(2)}, u32[]{:S(2)}) %collective-permute-start.20) | collective-permute-done | bytes 196640 | tf_op jit(solution)/shard_map/ppermute | solution.py:300
  83.2 1.1 %finish.1 = f32[2,2,9,32,256]{4,3,2,1,0:T(8,128)} custom-call(f32[2,2,6,32,256]{4,3,2,1,0:T(8,128)S(1)} %finish_some.1.some, bf16[1,2,2,3,32,256]{5,4,3,2,1,0:T(8,128)(2,1)S(1)} %get-tuple-element.104.keep, bf16[1,2,2,3,32,256]{5,4,3,2,1,0:T(8,128)(2,1)S(1)} %collective-permute-done.20.got), custom_call_target="tpu_custom_call" | custom-call | flops 603979776 | bytes 1024 | tf_op jit(solution)/shard_map/finish/pallas_call | solution.py:52
  (41 shorter events, 5.4 us)
Async XLA Ops:
  0.6 2.9 %slice-start = ((s8[4718592]{0:T(1024)(128)(4,1)}), s8[4194304]{0:T(1024)(128)(4,1)S(1)}, s32[]{:S(2)}) async-start(s8[4718592]{0:T(1024)(128)(4,1)} %bitcast.12), calls=%async_computation | async-start | bytes 8388608
  0.6 0.8 copy-start.4
  1.5 2.1 %slice-start.1 = ((s8[4718592]{0:T(1024)(128)(4,1)}), s8[524288]{0:T(1024)(128)(4,1)S(1)}, s32[]{:S(2)}) async-start(s8[4718592]{0:T(1024)(128)(4,1)} %bitcast.12), calls=%async_computation.1 | async-start | bytes 1048576
  5.2 6.6 %collective-permute-start = (bf16[512,256]{1,0:T(8,128)(2,1)S(1)}, bf16[512,256]{1,0:T(8,128)(2,1)S(1)}, u32[]{:S(2)}, u32[]{:S(2)}) collective-permute-start(bf16[512,256]{1,0:T(8,128)(2,1)S(1)} %late_1_0.1.refs_1_), channel_id=1, source_target_pairs={{0,8},{16,24},{32,40},{48,56},{64,72},{80,88},{96,104},{112,120},{... | collective-permute-start | bytes 786440 | tf_op jit(solution)/shard_map/ppermute | solution.py:296
  6.1 5.7 %copy-start = (bf16[2,1,4,1,16,32,256]{6,5,4,3,2,1,0:T(8,128)(2,1)S(1)}, bf16[2,1,4,1,16,32,256]{6,5,4,3,2,1,0:T(8,128)(2,1)}, u32[]{:S(2)}) copy-start(bf16[2,1,4,1,16,32,256]{6,5,4,3,2,1,0:T(8,128)(2,1)} %param.10) | copy-start | bytes 6291460
  6.2 5.7 %copy-start.1 = (bf16[2,1,4,1,16,32,256]{6,5,4,3,2,1,0:T(8,128)(2,1)S(1)}, bf16[2,1,4,1,16,32,256]{6,5,4,3,2,1,0:T(8,128)(2,1)}, u32[]{:S(2)}) copy-start(bf16[2,1,4,1,16,32,256]{6,5,4,3,2,1,0:T(8,128)(2,1)} %param.11) | copy-start | bytes 6291460
  7.0 9.9 %collective-permute-start.2 = (bf16[512,256]{1,0:T(8,128)(2,1)S(1)}, bf16[512,256]{1,0:T(8,128)(2,1)S(1)}, u32[]{:S(2)}, u32[]{:S(2)}) collective-permute-start(bf16[512,256]{1,0:T(8,128)(2,1)S(1)} %late_0_0.1.refs_1_), channel_id=1, source_target_pairs={{8,16},{24,32},{40,48},{56,64},{72,80},{88,96},{104,112},{16,8},{3... | collective-permute-start | bytes 786440 | tf_op jit(solution)/shard_map/ppermute | solution.py:296
  12.8 4.1 %copy-start.3 = (bf16[3,1,16,32,256]{4,3,2,1,0:T(8,128)(2,1)S(1)}, bf16[3,1,16,32,256]{4,3,2,1,0:T(8,128)(2,1)}, u32[]{:S(2)}) copy-start(bf16[3,1,16,32,256]{4,3,2,1,0:T(8,128)(2,1)} %param.8) | copy-start | bytes 2359300
  13.7 9.8 %collective-permute-start.1 = (bf16[512,256]{1,0:T(8,128)(2,1)S(1)}, bf16[512,256]{1,0:T(8,128)(2,1)S(1)}, u32[]{:S(2)}, u32[]{:S(2)}) collective-permute-start(bf16[512,256]{1,0:T(8,128)(2,1)S(1)} %late_0_1.1.refs_5_), channel_id=1, source_target_pairs={{8,16},{24,32},{40,48},{56,64},{72,80},{88,96},{104,112},{16,8},{3... | collective-permute-start | bytes 786440 | tf_op jit(solution)/shard_map/ppermute | solution.py:296
  18.0 1.6 %copy-start.2 = (bf16[2,1,4,1,16,32,256]{6,5,4,3,2,1,0:T(8,128)(2,1)S(1)}, bf16[2,1,4,1,16,32,256]{6,5,4,3,2,1,0:T(8,128)(2,1)}, u32[]{:S(2)}) copy-start(bf16[2,1,4,1,16,32,256]{6,5,4,3,2,1,0:T(8,128)(2,1)} %param.9) | copy-start | bytes 6291460
  18.8 6.5 %collective-permute-start.4 = (bf16[512,256]{1,0:T(8,128)(2,1)S(1)}, bf16[512,256]{1,0:T(8,128)(2,1)S(1)}, u32[]{:S(2)}, u32[]{:S(2)}) collective-permute-start(bf16[512,256]{1,0:T(8,128)(2,1)S(1)} %late_1_1.1.refs_5_), channel_id=1, source_target_pairs={{0,8},{16,24},{32,40},{48,56},{64,72},{80,88},{96,104},{112,120},{... | collective-permute-start | bytes 786440 | tf_op jit(solution)/shard_map/ppermute | solution.py:296
  27.2 9.8 %collective-permute-start.5 = (bf16[512,256]{1,0:T(8,128)(2,1)S(1)}, bf16[512,256]{1,0:T(8,128)(2,1)S(1)}, u32[]{:S(2)}, u32[]{:S(2)}) collective-permute-start(bf16[512,256]{1,0:T(8,128)(2,1)S(1)} %late_0_2.1.refs_2_), channel_id=1, source_target_pairs={{8,16},{24,32},{40,48},{56,64},{72,80},{88,96},{104,112},{16,8},{3... | collective-permute-start | bytes 786440 | tf_op jit(solution)/shard_map/ppermute | solution.py:296
  31.1 5.9 %collective-permute-start.3 = (bf16[512,256]{1,0:T(8,128)(2,1)S(1)}, bf16[512,256]{1,0:T(8,128)(2,1)S(1)}, u32[]{:S(2)}, u32[]{:S(2)}) collective-permute-start(bf16[512,256]{1,0:T(8,128)(2,1)S(1)} %late_1_2.1.refs_3_), channel_id=1, source_target_pairs={{0,8},{16,24},{32,40},{48,56},{64,72},{80,88},{96,104},{112,120},{... | collective-permute-start | bytes 786440 | tf_op jit(solution)/shard_map/ppermute | solution.py:296
  39.3 13.9 %collective-permute-start.8 = (bf16[4,2,3,32,256]{4,3,2,1,0:T(8,128)(2,1)S(1)}, bf16[4,2,3,32,256]{4,3,2,1,0:T(8,128)(2,1)S(1)}, u32[]{:S(2)}, u32[]{:S(2)}) collective-permute-start(bf16[4,2,3,32,256]{4,3,2,1,0:T(8,128)(2,1)S(1)} %get-tuple-element.77), channel_id=1, source_target_pairs={{0,1},{1,0},{2,3},{3,2},{4,5},{5,4},{6,7},{7,6},{8,9},{9,8},{10,11... | collective-permute-start | bytes 1179656 | tf_op jit(solution)/shard_map/ppermute | solution.py:300
  41.3 12.8 %collective-permute-start.9 = (bf16[4,2,3,32,256]{4,3,2,1,0:T(8,128)(2,1)S(1)}, bf16[4,2,3,32,256]{4,3,2,1,0:T(8,128)(2,1)S(1)}, u32[]{:S(2)}, u32[]{:S(2)}) collective-permute-start(bf16[4,2,3,32,256]{4,3,2,1,0:T(8,128)(2,1)S(1)} %get-tuple-element.78), channel_id=1, source_target_pairs={{0,3},{1,2},{2,1},{3,0},{4,7},{5,6},{6,5},{7,4},{8,11},{9,10},{10,... | collective-permute-start | bytes 1179656 | tf_op jit(solution)/shard_map/ppermute | solution.py:300
  43.9 11.5 %collective-permute-start.10 = (bf16[4,2,3,32,256]{4,3,2,1,0:T(8,128)(2,1)S(1)}, bf16[4,2,3,32,256]{4,3,2,1,0:T(8,128)(2,1)S(1)}, u32[]{:S(2)}, u32[]{:S(2)}) collective-permute-start(bf16[4,2,3,32,256]{4,3,2,1,0:T(8,128)(2,1)S(1)} %get-tuple-element.79), channel_id=1, source_target_pairs={{0,4},{1,5},{2,6},{3,7},{4,0},{5,1},{6,2},{7,3},{8,12},{9,13},{10,... | collective-permute-start | bytes 1179656 | tf_op jit(solution)/shard_map/ppermute | solution.py:300
  51.5 9.8 %collective-permute-start.6 = (bf16[4,2,3,32,256]{4,3,2,1,0:T(8,128)(2,1)S(1)}, bf16[4,2,3,32,256]{4,3,2,1,0:T(8,128)(2,1)S(1)}, u32[]{:S(2)}, u32[]{:S(2)}) collective-permute-start(bf16[4,2,3,32,256]{4,3,2,1,0:T(8,128)(2,1)S(1)} %get-tuple-element.70), channel_id=1, source_target_pairs={{0,1},{1,0},{2,3},{3,2},{4,5},{5,4},{6,7},{7,6},{8,9},{9,8},{10,11... | collective-permute-start | bytes 1179656 | tf_op jit(solution)/shard_map/ppermute | solution.py:300
  52.6 12.5 %collective-permute-start.15 = (bf16[4,2,3,32,256]{4,3,2,1,0:T(8,128)(2,1)S(1)}, bf16[4,2,3,32,256]{4,3,2,1,0:T(8,128)(2,1)S(1)}, u32[]{:S(2)}, u32[]{:S(2)}) collective-permute-start(bf16[4,2,3,32,256]{4,3,2,1,0:T(8,128)(2,1)S(1)} %get-tuple-element.91), channel_id=1, source_target_pairs={{0,3},{1,2},{2,1},{3,0},{4,7},{5,6},{6,5},{7,4},{8,11},{9,10},{10,... | collective-permute-start | bytes 1179656 | tf_op jit(solution)/shard_map/ppermute | solution.py:300
  53.2 12.9 %collective-permute-start.18 = (bf16[4,2,3,32,256]{4,3,2,1,0:T(8,128)(2,1)S(1)}, bf16[4,2,3,32,256]{4,3,2,1,0:T(8,128)(2,1)S(1)}, u32[]{:S(2)}, u32[]{:S(2)}) collective-permute-start(bf16[4,2,3,32,256]{4,3,2,1,0:T(8,128)(2,1)S(1)} %get-tuple-element.99), channel_id=1, source_target_pairs={{0,4},{1,5},{2,6},{3,7},{4,0},{5,1},{6,2},{7,3},{8,12},{9,13},{10,... | collective-permute-start | bytes 1179656 | tf_op jit(solution)/shard_map/ppermute | solution.py:300
  55.6 13.2 %collective-permute-start.11 = (bf16[2,2,3,32,256]{4,3,2,1,0:T(8,128)(2,1)S(1)}, bf16[2,2,3,32,256]{4,3,2,1,0:T(8,128)(2,1)S(1)}, u32[]{:S(2)}, u32[]{:S(2)}) collective-permute-start(bf16[2,2,3,32,256]{4,3,2,1,0:T(8,128)(2,1)S(1)} %get-tuple-element.83), channel_id=1, source_target_pairs={{0,3},{1,2},{2,1},{3,0},{4,7},{5,6},{6,5},{7,4},{8,11},{9,10},{10,... | collective-permute-start | bytes 589832 | tf_op jit(solution)/shard_map/ppermute | solution.py:300
  58.5 10.7 %collective-permute-start.12 = (bf16[2,2,3,32,256]{4,3,2,1,0:T(8,128)(2,1)S(1)}, bf16[2,2,3,32,256]{4,3,2,1,0:T(8,128)(2,1)S(1)}, u32[]{:S(2)}, u32[]{:S(2)}) collective-permute-start(bf16[2,2,3,32,256]{4,3,2,1,0:T(8,128)(2,1)S(1)} %get-tuple-element.84), channel_id=1, source_target_pairs={{0,4},{1,5},{2,6},{3,7},{4,0},{5,1},{6,2},{7,3},{8,12},{9,13},{10,... | collective-permute-start | bytes 589832 | tf_op jit(solution)/shard_map/ppermute | solution.py:300
  61.2 8.0 %collective-permute-start.13 = (bf16[2,2,3,32,256]{4,3,2,1,0:T(8,128)(2,1)S(1)}, bf16[2,2,3,32,256]{4,3,2,1,0:T(8,128)(2,1)S(1)}, u32[]{:S(2)}, u32[]{:S(2)}) collective-permute-start(bf16[2,2,3,32,256]{4,3,2,1,0:T(8,128)(2,1)S(1)} %get-tuple-element.85), channel_id=1, source_target_pairs={{0,1},{1,0},{2,3},{3,2},{4,5},{5,4},{6,7},{7,6},{8,9},{9,8},{10,11... | collective-permute-start | bytes 589832 | tf_op jit(solution)/shard_map/ppermute | solution.py:300
  65.1 6.9 %collective-permute-start.7 = (bf16[2,2,3,32,256]{4,3,2,1,0:T(8,128)(2,1)S(1)}, bf16[2,2,3,32,256]{4,3,2,1,0:T(8,128)(2,1)S(1)}, u32[]{:S(2)}, u32[]{:S(2)}) collective-permute-start(bf16[2,2,3,32,256]{4,3,2,1,0:T(8,128)(2,1)S(1)} %get-tuple-element.73), channel_id=1, source_target_pairs={{0,3},{1,2},{2,1},{3,0},{4,7},{5,6},{6,5},{7,4},{8,11},{9,10},{10,... | collective-permute-start | bytes 589832 | tf_op jit(solution)/shard_map/ppermute | solution.py:300
  66.1 7.3 %collective-permute-start.16 = (bf16[2,2,3,32,256]{4,3,2,1,0:T(8,128)(2,1)S(1)}, bf16[2,2,3,32,256]{4,3,2,1,0:T(8,128)(2,1)S(1)}, u32[]{:S(2)}, u32[]{:S(2)}) collective-permute-start(bf16[2,2,3,32,256]{4,3,2,1,0:T(8,128)(2,1)S(1)} %get-tuple-element.93), channel_id=1, source_target_pairs={{0,4},{1,5},{2,6},{3,7},{4,0},{5,1},{6,2},{7,3},{8,12},{9,13},{10,... | collective-permute-start | bytes 589832 | tf_op jit(solution)/shard_map/ppermute | solution.py:300
  68.8 7.3 %collective-permute-start.19 = (bf16[2,2,3,32,256]{4,3,2,1,0:T(8,128)(2,1)S(1)}, bf16[2,2,3,32,256]{4,3,2,1,0:T(8,128)(2,1)S(1)}, u32[]{:S(2)}, u32[]{:S(2)}) collective-permute-start(bf16[2,2,3,32,256]{4,3,2,1,0:T(8,128)(2,1)S(1)} %get-tuple-element.101), channel_id=1, source_target_pairs={{0,1},{1,0},{2,3},{3,2},{4,5},{5,4},{6,7},{7,6},{8,9},{9,8},{10,11... | collective-permute-start | bytes 589832 | tf_op jit(solution)/shard_map/ppermute | solution.py:300
  73.4 5.8 %collective-permute-start.17 = (bf16[1,2,2,3,32,256]{5,4,3,2,1,0:T(8,128)(2,1)S(1)}, bf16[1,2,2,3,32,256]{5,4,3,2,1,0:T(8,128)(2,1)S(1)}, u32[]{:S(2)}, u32[]{:S(2)}) collective-permute-start(bf16[1,2,2,3,32,256]{5,4,3,2,1,0:T(8,128)(2,1)S(1)} %get-tuple-element.97), channel_id=1, source_target_pairs={{0,1},{1,0},{2,3},{3,2},{4,5},{5,4},{6,7},{7,6},{8,9},{9,8},{10,11... | collective-permute-start | bytes 589832 | tf_op jit(solution)/shard_map/ppermute | solution.py:300
  74.2 7.2 %collective-permute-start.14 = (bf16[1,2,2,3,32,256]{5,4,3,2,1,0:T(8,128)(2,1)S(1)}, bf16[1,2,2,3,32,256]{5,4,3,2,1,0:T(8,128)(2,1)S(1)}, u32[]{:S(2)}, u32[]{:S(2)}) collective-permute-start(bf16[1,2,2,3,32,256]{5,4,3,2,1,0:T(8,128)(2,1)S(1)} %get-tuple-element.89), channel_id=1, source_target_pairs={{0,4},{1,5},{2,6},{3,7},{4,0},{5,1},{6,2},{7,3},{8,12},{9,13},{10,... | collective-permute-start | bytes 589832 | tf_op jit(solution)/shard_map/ppermute | solution.py:300
  76.2 7.0 %collective-permute-start.20 = (bf16[1,2,2,3,32,256]{5,4,3,2,1,0:T(8,128)(2,1)S(1)}, bf16[1,2,2,3,32,256]{5,4,3,2,1,0:T(8,128)(2,1)S(1)}, u32[]{:S(2)}, u32[]{:S(2)}) collective-permute-start(bf16[1,2,2,3,32,256]{5,4,3,2,1,0:T(8,128)(2,1)S(1)} %get-tuple-element.105), channel_id=1, source_target_pairs={{0,3},{1,2},{2,1},{3,0},{4,7},{5,6},{6,5},{7,4},{8,11},{9,10},{10,... | collective-permute-start | bytes 589832 | tf_op jit(solution)/shard_map/ppermute | solution.py:300

commit v5 on v4

--- a/solution.py
+++ b/solution.py
@@ -28,6 +28,8 @@
     "y": [(d, d ^ 4) for d in range(DP)],
 }
 ORDERS = ("aby", "bya", "yab")
+TAPS = ((2, 2, 5), (5, 4, 0))
+FIRST = tuple(tuple(sum(taps[:o]) for o in range(3)) for taps in TAPS)
 
 VM = pl.BlockSpec(memory_space=pltpu.VMEM)
 SM = pl.BlockSpec(memory_space=pltpu.SMEM)
@@ -197,8 +199,9 @@
     return (y ^ bit["y"]) * 4 + 2 * beta + (alpha ^ beta)
 
 
-def put_shares(staged, k, sends, keeps, role):
-    o, at = divmod(k, 3)
+def put_shares(staged, piece, k, sends, keeps, role):
+    o = sum(k >= first for first in FIRST[piece][1:])
+    at = k - FIRST[piece][o]
     for r in range(DP):
         row = pl.multiple_of(replica_at(ORDERS[o], r) * SHARE, SHARE)
         share = staged[k, pl.ds(row, SHARE), :].astype(BF)
@@ -210,8 +213,8 @@
 
 def last_two_kernel(table, pre1, pre2, objective, *refs):
     given, olds = refs[:4], refs[4:6]
-    sends, keeps, g2s = refs[6:9], refs[9:12], refs[12:14]
-    wins, staged = refs[14:16], refs[16:18]
+    sends, keeps, g2s = refs[6:8], refs[8:10], refs[10:12]
+    wins, staged = refs[12:14], refs[14:16]
     tick = TICKS - 1
     for role in range(2):
         slot = slot_of(table, role, tick)
@@ -220,7 +223,7 @@
         g2s[role][...] = g2.astype(BF)
         for k, term in tap_grads(wins[role : role + 1], [left_side(1, pre1, slot)], [g2]):
             staged[role][k] = olds[role][k] + term
-            put_shares(staged[role], k, sends, keeps, role)
+            put_shares(staged[role], 1, k, sends, keeps, role)
 
 
 def last_early_kernel(role, table, pre1, taps, g2, g1_out, win):
@@ -238,7 +241,7 @@
         fields = [befores[role][...].astype(F32), g1s[role][...].astype(F32)]
         for k, term in tap_grads(wins[2 * role : 2 * role + 2], xs, fields):
             staged[role][k] = olds[role][k] + term
-            put_shares(staged[role], k, sends, keeps, role)
+            put_shares(staged[role], 0, k, sends, keeps, role)
 
 
 def last_late_kernel(taps, g1_zero, g1_one, out, mark, *wins):
@@ -256,38 +259,43 @@
     send[...] = total[half:].astype(BF)
 
 
-def fold_kernel(*refs):
-    for o in range(3):
-        fold_in(*refs[o::3])
+def fold_two_kernel(*refs):
+    for o in range(2):
+        fold_in(*refs[o::2])
 
 
 def fold_two_last_kernel(*refs):
-    for o in range(3):
-        keep, got, send, left = refs[o::3]
-        fold_in(keep, got, send.at[:, 1], left.at[:, 1])
-
-
-def fold_one_last_kernel(keep, got, old_send, old_left, send, left):
-    del old_send, old_left
-    fold_in(keep, got, send.at[:, 0], left.at[:, 0])
-
-
-def finish_some_kernel(scale, *refs):
-    out = refs[-1]
     for o in range(2):
-        keep, got = refs[2 * o : 2 * o + 2]
-        total = keep[0].astype(F32) + got[0].astype(F32)
-        for role in range(2):
-            for piece in range(2):
-                out[half_of(role), piece, 3 * o : 3 * o + 3] = total[piece, role] * scale
-
-
-def finish_kernel(scale, some, keep, got, out):
-    out[:, :, 0:6] = some[...]
+        keep, got, send, left = refs[o::2]
+        fold_in(keep, got, send.at[:, :, TAPS[0][o] :], left.at[:, :, TAPS[0][o] :])
+
+
+def fold_one_last_kernel(o, *refs):
+    keep, got = refs[:2]
+    send, left = refs[-2:]
+    fold_in(keep, got, send.at[:, :, : TAPS[0][o]], left.at[:, :, : TAPS[0][o]])
+
+
+def finish_order(scale, o, keep, got, out):
     total = keep[0].astype(F32) + got[0].astype(F32)
     for role in range(2):
         for piece in range(2):
-            out[half_of(role), piece, 6:9] = total[piece, role] * scale
+            taps, first = TAPS[piece][o], FIRST[piece][o]
+            if taps:
+                low = TAPS[0][o] * piece
+                out[half_of(role), piece, first : first + taps] = total[role, low : low + taps] * scale
+
+
+def finish_some_kernel(scale, *refs):
+    for o in range(2):
+        finish_order(scale, o, *refs[2 * o : 2 * o + 2], refs[-1])
+
+
+def finish_kernel(scale, some, keep, got, out):
+    for piece in range(2):
+        first = FIRST[piece][2]
+        out[:, piece, 0:first] = some[:, piece, 0:first]
+    finish_order(scale, 2, keep, got, out)
 
 
 def relay(block, role):
@@ -370,19 +378,21 @@
             sums1 = early_sums(0, entries, all_g1s)
     sums2 = early_sums(1, pre1, all_g2s)
 
-    part = jax.ShapeDtypeStruct((4, 2, 3, SHARE, CH), BF)
+    def part(chunks, taps):
+        return jax.ShapeDtypeStruct((chunks, 2, taps, SHARE, CH), BF)
+
     staged = [pltpu.VMEM((9, CH, CH), F32)] * 2
     res = call(
         last_two_kernel,
         "last_two",
         (table, pre1, pre2, objective, gots[1], gots[0], *outs, *sums2),
-        (part,) * 6 + (FIELD,) * 2,
+        tuple(part(4, taps) for taps in TAPS[1][:2] * 2) + (FIELD,) * 2,
         scratch=windows * 2 + staged,
         mib=16,
         ops=2,
     )
-    keeps2, g2s = res[3:6], res[6:8]
-    gots2 = [exchange(res[o], ORDERS[o][0]) for o in range(3)]
+    keeps2, g2s = res[2:4], res[4:6]
+    gots2 = [exchange(res[o], ORDERS[o][0]) for o in range(2)]
     g1s = [
         call(
             functools.partial(last_early_kernel, role),
@@ -397,13 +407,15 @@
         last_one_kernel,
         "last_one",
         (table, entries, *all_g1s[-1], *g1s, *sums1),
-        (part,) * 6,
+        tuple(part(4, taps) for taps in TAPS[0] * 2),
         scratch=windows * 4 + staged,
         mib=16,
         ops=4,
     )
     keeps1 = res[3:6]
-    gots1 = [exchange(res[o], ORDERS[o][0]) for o in range(3)]
+    gots1 = [None] * 3
+    for o in (2, 0, 1):
+        gots1[o] = exchange(res[o], ORDERS[o][0])
     final, mark = call(
         last_late_kernel,
         f"late_{TICKS - 1}",
@@ -414,26 +426,26 @@
     )
 
     parts = []
-    part2 = jax.ShapeDtypeStruct((2, 2, 3, SHARE, CH), BF)
-    part3 = jax.ShapeDtypeStruct((1, 2, 2, 3, SHARE, CH), BF)
-    res = call(fold_kernel, "fold_two", (*keeps2, *gots2), (part2,) * 6, ops=FOLD_COST)
-    gots2 = [exchange(res[o], ORDERS[o][1]) for o in range(3)]
-    begun = call(fold_two_last_kernel, "fold_two_last", (*res[3:6], *gots2), (part3,) * 6, ops=FOLD_COST)
+    twos = tuple(part(2, taps) for taps in TAPS[1][:2])
+    both = [part(1, TAPS[0][o] + TAPS[1][o]) for o in range(3)]
+    res = call(fold_two_kernel, "fold_two", (*keeps2, *gots2), twos * 2, ops=FOLD_COST)
+    gots2 = [exchange(res[o], ORDERS[o][1]) for o in range(2)]
+    begun = call(fold_two_last_kernel, "fold_two_last", (*res[2:4], *gots2), tuple(both[:2] * 2), ops=FOLD_COST)
     firsts = []
     order = [mark]
     for o in range(3):
-        send, keep = call(fold_in, f"fold_one_{o}", (keeps1[o], gots1[o]), (part2, part2), after=order[-1:])
+        send, keep = call(fold_in, f"fold_one_{o}", (keeps1[o], gots1[o]), (part(2, TAPS[0][o]),) * 2, after=order[-1:])
         firsts.append(keep)
         order.append(keep)
         gots1[o] = exchange(send, ORDERS[o][1])
     lasts = []
     for o in range(3):
         send, keep = call(
-            fold_one_last_kernel,
+            functools.partial(fold_one_last_kernel, o),
             f"fold_one_last_{o}",
-            (firsts[o], gots1[o], begun[o], begun[3 + o]),
-            (part3, part3),
-            aliases={2: 0, 3: 1},
+            (firsts[o], gots1[o], *(begun[o::2] if o < 2 else ())),
+            (both[o],) * 2,
+            aliases={2: 0, 3: 1} if o < 2 else {},
             after=lasts[-1:],
         )
         lasts.append(keep)
@@ -443,7 +455,7 @@
         functools.partial(finish_some_kernel, scale),
         "finish_some",
         tuple(parts[:4]),
-        jax.ShapeDtypeStruct((2, 2, 6, SHARE, CH), F32),
+        jax.ShapeDtypeStruct((2, 2, 9, SHARE, CH), F32),
         ops=FOLD_COST,
     )
     grads = call(

time: 85.8 us -> 86.6 us (level); the launches traced: 84.3 us -> 86.1 us
  starting transfers between devices: 33.9 us -> 36.1 us
    ppermute x15 -> x13, starting transfers between devices: 21.8 us -> 23.9 us  [exchange(): return lax.ppermute(block, 'dp', PAIRS[step])]
    ppermute x15 -> x13, waiting for transfers between devices: 13.8 us -> 13.5 us  [exchange(): return lax.ppermute(block, 'dp', PAIRS[step])]
  transfers between devices with their start and end apart: 21 -> 19, of which waited for: 13 -> 9; matrix products, arithmetic and copies ran while one was open for 0% -> 0% of each run, Pallas kernels for 27% -> 27%
where the time goes in v5:
time: 86.6 us; the launch traced here: 86.1 us
  starting transfers between devices  36.1 us (42%)
  Pallas kernels  32 us (37%)
  waiting for transfers between devices  15.7 us (18%)
  local copies, waits for them, and re-layouts  1.33 us (2%)
  between operations  0.98 us (1%)
    pallas_call x31, Pallas kernels, call(): pl.pallas_call(body if after else kernel, out_shape=outs, in_specs=[VM] *...  30 us
    ppermute x13, starting transfers between devices, exchange(): return lax.ppermute(block, 'dp', PAIRS[step])  23.9 us
    ppermute x13, waiting for transfers between devices, exchange(): return lax.ppermute(block, 'dp', PAIRS[step])  13.5 us
    ppermute x6, starting transfers between devices, relay(): return lax.ppermute(block, 'section', pairs + [(b, a) for a, b in pairs])  12.2 us
    ppermute x6, waiting for transfers between devices, relay(): return lax.ppermute(block, 'section', pairs + [(b, a) for a, b in pairs])  2.22 us
    pallas_call x1, Pallas kernels, prepare(): pl.pallas_call(prepare_kernel, grid_spec=pltpu.PrefetchScalarGridSpec(num...  2.04 us
  transfers between devices with their start and end apart: 19, of which 9 were waited for; matrix products, arithmetic and copies ran while one was open for 0% of the time, Pallas kernels for 27%

profile of v5, /device:TPU:8, one launch (start us, length us, event | category | flops | bytes accessed | tf_op | source)
XLA Modules:
  0.0 86.1 jit_solution(6123481114620618218)
XLA Ops:
  0.7 0.8 copy-done.4
  1.5 2.0 %prepare.1 = (bf16[512,256]{1,0:T(8,128)(2,1)S(1)}, bf16[512,256]{1,0:T(8,128)(2,1)S(1)}, bf16[512,256]{1,0:T(8,128)(2,1)S(1)}, bf16[512,256]{1,0:T(8,128)(2,1)S(1)}) custom-call(s32[4,32]{1,0:T(4,128)S(1)} %copy-done.4, bf16[2,512,256]{2,1,0:T(8,128)(2,1)} %bitcast.53, bf16[2,512,256]{2,1,0:T(8,128)(2,1)} %bitcast.54, bf16[8,512,256]{2,1,0:T(8,128)(2,1)} %bitcast.40, ...), custom_call_target="tpu_custom_call" | custom-call | flops 1 | bytes 1024 | tf_op jit(solution)/shard_map/prepare/pallas_call | solution.py:132
  3.5 0.8 early_1_0.1.g1.refs_0_
  4.4 0.8 late_1_0.1.refs_1_
  5.3 0.8 early_0_0.1.refs_0_.g1
  6.2 0.8 late_0_0.1.refs_1_
  7.0 4.8 %collective-permute-start.2 = (bf16[512,256]{1,0:T(8,128)(2,1)S(1)}, bf16[512,256]{1,0:T(8,128)(2,1)S(1)}, u32[]{:S(2)}, u32[]{:S(2)}) collective-permute-start(bf16[512,256]{1,0:T(8,128)(2,1)S(1)} %late_0_0.1.refs_1_), channel_id=1, source_target_pairs={{8,16},{24,32},{40,48},{56,64},{72,80},{88,96},{104,112},{16,8},{3... | collective-permute-start | bytes 786440 | tf_op jit(solution)/shard_map/ppermute | solution.py:304
  11.8 1.0 %early_0_1.1 = (bf16[512,256]{1,0:T(8,128)(2,1)S(1)}, bf16[512,256]{1,0:T(8,128)(2,1)S(1)}) custom-call(s32[4,32]{1,0:T(4,128)S(1)} %copy-done.4, bf16[8,512,256]{2,1,0:T(8,128)(2,1)S(1)} %bitcast.31, bf16[8,512,256]{2,1,0:T(8,128)(2,1)S(1)} %bitcast.42, bf16[36,256,256]{2,1,0:T(8,128)(2,1)S(1)} %bitcast.18, ...), custom_call_target="tpu_custom_call" | custom-call | flops 603979776 | bytes 1024 | tf_op jit(solution)/shard_map/early_0_1/pallas_call | solution.py:54
  12.8 0.8 late_0_1.1.refs_5_
  13.7 3.0 %collective-permute-start.1 = (bf16[512,256]{1,0:T(8,128)(2,1)S(1)}, bf16[512,256]{1,0:T(8,128)(2,1)S(1)}, u32[]{:S(2)}, u32[]{:S(2)}) collective-permute-start(bf16[512,256]{1,0:T(8,128)(2,1)S(1)} %late_0_1.1.refs_5_), channel_id=1, source_target_pairs={{8,16},{24,32},{40,48},{56,64},{72,80},{88,96},{104,112},{16,8},{3... | collective-permute-start | bytes 786440 | tf_op jit(solution)/shard_map/ppermute | solution.py:304
  16.9 1.0 %early_1_1.1 = (bf16[512,256]{1,0:T(8,128)(2,1)S(1)}, bf16[512,256]{1,0:T(8,128)(2,1)S(1)}) custom-call(s32[4,32]{1,0:T(4,128)S(1)} %copy-done.4, bf16[8,512,256]{2,1,0:T(8,128)(2,1)S(1)} %bitcast.32, bf16[8,512,256]{2,1,0:T(8,128)(2,1)S(1)} %bitcast.43, bf16[36,256,256]{2,1,0:T(8,128)(2,1)S(1)} %bitcast.20, ...), custom_call_target="tpu_custom_call" | custom-call | flops 603979776 | bytes 1024 | tf_op jit(solution)/shard_map/early_1_1/pallas_call | solution.py:54
  18.0 0.8 late_1_1.1.refs_5_
  19.1 0.5 copy-done.2
  19.6 1.6 %wgrad1_1.1.refs_8_.refs_7_.refs_5_ = f32[9,256,256]{2,1,0:T(8,128)S(1)} custom-call(s32[4,32]{1,0:T(4,128)S(1)} %copy-done.4, bf16[8,512,256]{2,1,0:T(8,128)(2,1)S(1)} %bitcast.47, bf16[512,256]{1,0:T(8,128)(2,1)S(1)} %early_1_0.1.g1.refs_0_, bf16[512,256]{1,0:T(8,128)(2,1)S(1)} %get-tuple-element.53.refs_1_.g1), custom_call_target="tpu_custom_call" | custom-call | flops 1207959552 | bytes 1024 | tf_op jit(solution)/shard_map/wgrad1_1/pallas_call | solution.py:54
  21.1 1.6 %wgrad1_0.1.refs_7_.refs_6_.refs_4_ = f32[9,256,256]{2,1,0:T(8,128)S(1)} custom-call(s32[4,32]{1,0:T(4,128)S(1)} %copy-done.4, bf16[8,512,256]{2,1,0:T(8,128)(2,1)S(1)} %bitcast.48, bf16[512,256]{1,0:T(8,128)(2,1)S(1)} %early_0_0.1.refs_0_.g1, bf16[512,256]{1,0:T(8,128)(2,1)S(1)} %get-tuple-element.50.g1.refs_1_), custom_call_target="tpu_custom_call" | custom-call | flops 1207959552 | bytes 1024 | tf_op jit(solution)/shard_map/wgrad1_0/pallas_call | solution.py:54
  22.7 0.7 collective-permute-done.1.refs_4_
  23.5 1.0 %early_1_2.1 = (bf16[512,256]{1,0:T(8,128)(2,1)S(1)}, bf16[512,256]{1,0:T(8,128)(2,1)S(1)}) custom-call(s32[4,32]{1,0:T(4,128)S(1)} %copy-done.4, bf16[8,512,256]{2,1,0:T(8,128)(2,1)S(1)} %bitcast.33, bf16[8,512,256]{2,1,0:T(8,128)(2,1)S(1)} %bitcast.44, bf16[36,256,256]{2,1,0:T(8,128)(2,1)S(1)} %bitcast.22, ...), custom_call_target="tpu_custom_call" | custom-call | flops 603979776 | bytes 1024 | tf_op jit(solution)/shard_map/early_1_2/pallas_call | solution.py:54
  24.5 0.8 late_1_2.1.refs_3_
  25.3 1.0 %early_0_2.1 = (bf16[512,256]{1,0:T(8,128)(2,1)S(1)}, bf16[512,256]{1,0:T(8,128)(2,1)S(1)}) custom-call(s32[4,32]{1,0:T(4,128)S(1)} %copy-done.4, bf16[8,512,256]{2,1,0:T(8,128)(2,1)S(1)} %bitcast.34, bf16[8,512,256]{2,1,0:T(8,128)(2,1)S(1)} %bitcast.45, bf16[36,256,256]{2,1,0:T(8,128)(2,1)S(1)} %bitcast.24, ...), custom_call_target="tpu_custom_call" | custom-call | flops 603979776 | bytes 1024 | tf_op jit(solution)/shard_map/early_0_2/pallas_call | solution.py:54
  26.3 0.8 late_0_2.1.refs_2_
  27.2 3.9 %collective-permute-start.5 = (bf16[512,256]{1,0:T(8,128)(2,1)S(1)}, bf16[512,256]{1,0:T(8,128)(2,1)S(1)}, u32[]{:S(2)}, u32[]{:S(2)}) collective-permute-start(bf16[512,256]{1,0:T(8,128)(2,1)S(1)} %late_0_2.1.refs_2_), channel_id=1, source_target_pairs={{8,16},{24,32},{40,48},{56,64},{72,80},{88,96},{104,112},{16,8},{3... | collective-permute-start | bytes 786440 | tf_op jit(solution)/shard_map/ppermute | solution.py:304
  31.2 2.3 %wgrad2_1.1.refs_5_ = f32[9,256,256]{2,1,0:T(8,128)S(1)} custom-call(s32[4,32]{1,0:T(4,128)S(1)} %copy-done.4, bf16[8,512,256]{2,1,0:T(8,128)(2,1)S(1)} %bitcast.35, bf16[512,256]{1,0:T(8,128)(2,1)S(1)} %get-tuple-element.49.g2.refs_0_, bf16[512,256]{1,0:T(8,128)(2,1)S(1)} %get-tuple-element.58.refs_1_, bf16[512,256]{1,0:T(8,128)(2,1)S(1)} %get-tuple-element.59.refs_2_), custom_call_target="tpu_custom_call" | custom-call | flops 1811939328 | bytes 1024 | tf_op jit(solution)/shard_map/wgrad2_1/pallas_call | solution.py:54
  33.5 2.3 %wgrad2_0.1.refs_4_ = f32[9,256,256]{2,1,0:T(8,128)S(1)} custom-call(s32[4,32]{1,0:T(4,128)S(1)} %copy-done.4, bf16[8,512,256]{2,1,0:T(8,128)(2,1)S(1)} %bitcast.36, bf16[512,256]{1,0:T(8,128)(2,1)S(1)} %get-tuple-element.52.g2.refs_0_, bf16[512,256]{1,0:T(8,128)(2,1)S(1)} %get-tuple-element.56.refs_1_, bf16[512,256]{1,0:T(8,128)(2,1)S(1)} %get-tuple-element.57.refs_2_), custom_call_target="tpu_custom_call" | custom-call | flops 1811939328 | bytes 1024 | tf_op jit(solution)/shard_map/wgrad2_0/pallas_call | solution.py:54
  35.7 1.2 %collective-permute-done.5.refs_1_ = bf16[512,256]{1,0:T(8,128)(2,1)S(1)} collective-permute-done((bf16[512,256]{1,0:T(8,128)(2,1)S(1)}, bf16[512,256]{1,0:T(8,128)(2,1)S(1)}, u32[]{:S(2)}, u32[]{:S(2)}) %collective-permute-start.5) | collective-permute-done | bytes 262176 | tf_op jit(solution)/shard_map/ppermute | solution.py:304
  37.0 2.3 %last_two.1 = (bf16[4,2,5,32,256]{4,3,2,1,0:T(8,128)(2,1)S(1)}, bf16[4,2,4,32,256]{4,3,2,1,0:T(8,128)(2,1)S(1)}, bf16[4,2,5,32,256]{4,3,2,1,0:T(8,128)(2,1)S(1)}...) custom-call(s32[4,32]{1,0:T(4,128)S(1)} %copy-done.4, ...), custom_call_target="tpu_custom_call" | custom-call | flops 1207959552 | bytes 1024 | tf_op jit(solution)/shard_map/last_two/pallas_call | solution.py:54
  39.3 2.0 %collective-permute-start.8 = (bf16[4,2,5,32,256]{4,3,2,1,0:T(8,128)(2,1)S(1)}, bf16[4,2,5,32,256]{4,3,2,1,0:T(8,128)(2,1)S(1)}, u32[]{:S(2)}, u32[]{:S(2)}) collective-permute-start(bf16[4,2,5,32,256]{4,3,2,1,0:T(8,128)(2,1)S(1)} %get-tuple-element.70), channel_id=1, source_target_pairs={{0,1},{1,0},{2,3},{3,2},{4,5},{5,4},{6,7},{7,6},{8,9},{9,8},{10,11... | collective-permute-start | bytes 1966088 | tf_op jit(solution)/shard_map/ppermute | solution.py:308
  41.3 2.5 %collective-permute-start.9 = (bf16[4,2,4,32,256]{4,3,2,1,0:T(8,128)(2,1)S(1)}, bf16[4,2,4,32,256]{4,3,2,1,0:T(8,128)(2,1)S(1)}, u32[]{:S(2)}, u32[]{:S(2)}) collective-permute-start(bf16[4,2,4,32,256]{4,3,2,1,0:T(8,128)(2,1)S(1)} %get-tuple-element.71), channel_id=1, source_target_pairs={{0,3},{1,2},{2,1},{3,0},{4,7},{5,6},{6,5},{7,4},{8,11},{9,10},{10,... | collective-permute-start | bytes 1572872 | tf_op jit(solution)/shard_map/ppermute | solution.py:308
  43.9 0.8 early_0_3.1.g1_zero.refs_2_
  44.7 0.8 early_1_3.1.g1_one.refs_3_
  45.5 3.3 %last_one.1 = (bf16[4,2,2,32,256]{4,3,2,1,0:T(8,128)(2,1)S(1)}, bf16[4,2,2,32,256]{4,3,2,1,0:T(8,128)(2,1)S(1)}, bf16[4,2,5,32,256]{4,3,2,1,0:T(8,128)(2,1)S(1)}...) custom-call(s32[4,32]{1,0:T(4,128)S(1)} %copy-done.4, ...), custom_call_target="tpu_custom_call" | custom-call | flops 2415919104 | bytes 1024 | tf_op jit(solution)/shard_map/last_one/pallas_call | solution.py:54
  48.9 1.1 %collective-permute-start.6 = (bf16[4,2,2,32,256]{4,3,2,1,0:T(8,128)(2,1)S(1)}, bf16[4,2,2,32,256]{4,3,2,1,0:T(8,128)(2,1)S(1)}, u32[]{:S(2)}, u32[]{:S(2)}) collective-permute-start(bf16[4,2,2,32,256]{4,3,2,1,0:T(8,128)(2,1)S(1)} %get-tuple-element.64), channel_id=1, source_target_pairs={{0,1},{1,0},{2,3},{3,2},{4,5},{5,4},{6,7},{7,6},{8,9},{9,8},{10,11... | collective-permute-start | bytes 786440 | tf_op jit(solution)/shard_map/ppermute | solution.py:308
  50.0 0.6 collective-permute-start.13
  50.6 2.6 %collective-permute-start.16 = (bf16[4,2,5,32,256]{4,3,2,1,0:T(8,128)(2,1)S(1)}, bf16[4,2,5,32,256]{4,3,2,1,0:T(8,128)(2,1)S(1)}, u32[]{:S(2)}, u32[]{:S(2)}) collective-permute-start(bf16[4,2,5,32,256]{4,3,2,1,0:T(8,128)(2,1)S(1)} %get-tuple-element.89), channel_id=1, source_target_pairs={{0,4},{1,5},{2,6},{3,7},{4,0},{5,1},{6,2},{7,3},{8,12},{9,13},{10,... | collective-permute-start | bytes 1966088 | tf_op jit(solution)/shard_map/ppermute | solution.py:308
  53.3 4.2 %collective-permute-done.9.refs_3_ = bf16[4,2,4,32,256]{4,3,2,1,0:T(8,128)(2,1)S(1)} collective-permute-done((bf16[4,2,4,32,256]{4,3,2,1,0:T(8,128)(2,1)S(1)}, bf16[4,2,4,32,256]{4,3,2,1,0:T(8,128)(2,1)S(1)}, u32[]{:S(2)}, u32[]{:S(2)}) %collective-permute-start.9) | collective-permute-done | bytes 524320 | tf_op jit(solution)/shard_map/ppermute | solution.py:308
  57.7 3.8 %collective-permute-start.10 = (bf16[2,2,5,32,256]{4,3,2,1,0:T(8,128)(2,1)S(1)}, bf16[2,2,5,32,256]{4,3,2,1,0:T(8,128)(2,1)S(1)}, u32[]{:S(2)}, u32[]{:S(2)}) collective-permute-start(bf16[2,2,5,32,256]{4,3,2,1,0:T(8,128)(2,1)S(1)} %get-tuple-element.74), channel_id=1, source_target_pairs={{0,3},{1,2},{2,1},{3,0},{4,7},{5,6},{6,5},{7,4},{8,11},{9,10},{10,... | collective-permute-start | bytes 983048 | tf_op jit(solution)/shard_map/ppermute | solution.py:308
  61.5 2.6 %collective-permute-start.11 = (bf16[2,2,4,32,256]{4,3,2,1,0:T(8,128)(2,1)S(1)}, bf16[2,2,4,32,256]{4,3,2,1,0:T(8,128)(2,1)S(1)}, u32[]{:S(2)}, u32[]{:S(2)}) collective-permute-start(bf16[2,2,4,32,256]{4,3,2,1,0:T(8,128)(2,1)S(1)} %get-tuple-element.75), channel_id=1, source_target_pairs={{0,4},{1,5},{2,6},{3,7},{4,0},{5,1},{6,2},{7,3},{8,12},{9,13},{10,... | collective-permute-start | bytes 786440 | tf_op jit(solution)/shard_map/ppermute | solution.py:308
  64.1 2.2 %late_3.1 = (bf16[2,512,256]{2,1,0:T(8,128)(2,1)}, f32[8,128]{1,0:T(8,128)S(1)}) custom-call(bf16[36,256,256]{2,1,0:T(8,128)(2,1)S(1)} %bitcast.28, bf16[512,256]{1,0:T(8,128)(2,1)S(1)} %early_0_3.1.g1_zero.refs_2_, bf16[512,256]{1,0:T(8,128)(2,1)S(1)} %early_1_3.1.g1_one.refs_3_), custom_call_target="tpu_custom_call" | custom-call | flops 1207959552 | bytes 1024 | tf_op jit(solution)/shard_map/late_3/pallas_call | solution.py:54
  66.6 1.3 %collective-permute-start.14 = (bf16[2,2,2,32,256]{4,3,2,1,0:T(8,128)(2,1)S(1)}, bf16[2,2,2,32,256]{4,3,2,1,0:T(8,128)(2,1)S(1)}, u32[]{:S(2)}, u32[]{:S(2)}) collective-permute-start(bf16[2,2,2,32,256]{4,3,2,1,0:T(8,128)(2,1)S(1)} %get-tuple-element.83), channel_id=1, source_target_pairs={{0,4},{1,5},{2,6},{3,7},{4,0},{5,1},{6,2},{7,3},{8,12},{9,13},{10,... | collective-permute-start | bytes 393224 | tf_op jit(solution)/shard_map/ppermute | solution.py:308
  67.9 1.9 %collective-permute-done.16.refs_1_ = bf16[4,2,5,32,256]{4,3,2,1,0:T(8,128)(2,1)S(1)} collective-permute-done((bf16[4,2,5,32,256]{4,3,2,1,0:T(8,128)(2,1)S(1)}, bf16[4,2,5,32,256]{4,3,2,1,0:T(8,128)(2,1)S(1)}, u32[]{:S(2)}, u32[]{:S(2)}) %collective-permute-start.16) | collective-permute-done | bytes 655392 | tf_op jit(solution)/shard_map/ppermute | solution.py:308
  69.9 0.6 collective-permute-start.17
  70.5 3.7 %collective-permute-done.11.refs_3_ = bf16[2,2,4,32,256]{4,3,2,1,0:T(8,128)(2,1)S(1)} collective-permute-done((bf16[2,2,4,32,256]{4,3,2,1,0:T(8,128)(2,1)S(1)}, bf16[2,2,4,32,256]{4,3,2,1,0:T(8,128)(2,1)S(1)}, u32[]{:S(2)}, u32[]{:S(2)}) %collective-permute-start.11) | collective-permute-done | bytes 262176 | tf_op jit(solution)/shard_map/ppermute | solution.py:308
  74.4 2.7 %collective-permute-start.12 = (bf16[1,2,7,32,256]{4,3,2,1,0:T(8,128)(2,1)S(1)}, bf16[1,2,7,32,256]{4,3,2,1,0:T(8,128)(2,1)S(1)}, u32[]{:S(2)}, u32[]{:S(2)}) collective-permute-start(bf16[1,2,7,32,256]{4,3,2,1,0:T(8,128)(2,1)S(1)} %get-tuple-element.79), channel_id=1, source_target_pairs={{0,4},{1,5},{2,6},{3,7},{4,0},{5,1},{6,2},{7,3},{8,12},{9,13},{10,... | collective-permute-start | bytes 688136 | tf_op jit(solution)/shard_map/ppermute | solution.py:308
  77.2 0.7 collective-permute-start.15
  77.8 0.5 collective-permute-done.17.refs_1_
  78.4 3.2 %collective-permute-start.18 = (bf16[1,2,5,32,256]{4,3,2,1,0:T(8,128)(2,1)S(1)}, bf16[1,2,5,32,256]{4,3,2,1,0:T(8,128)(2,1)S(1)}, u32[]{:S(2)}, u32[]{:S(2)}) collective-permute-start(bf16[1,2,5,32,256]{4,3,2,1,0:T(8,128)(2,1)S(1)} %get-tuple-element.93), channel_id=1, source_target_pairs={{0,3},{1,2},{2,1},{3,0},{4,7},{5,6},{6,5},{7,4},{8,11},{9,10},{10,... | collective-permute-start | bytes 491528 | tf_op jit(solution)/shard_map/ppermute | solution.py:308
  81.6 1.3 %collective-permute-done.15.refs_3_ = bf16[1,2,6,32,256]{4,3,2,1,0:T(8,128)(2,1)S(1)} collective-permute-done((bf16[1,2,6,32,256]{4,3,2,1,0:T(8,128)(2,1)S(1)}, bf16[1,2,6,32,256]{4,3,2,1,0:T(8,128)(2,1)S(1)}, u32[]{:S(2)}, u32[]{:S(2)}) %collective-permute-start.15) | collective-permute-done | bytes 196640 | tf_op jit(solution)/shard_map/ppermute | solution.py:308
  83.0 2.0 %collective-permute-done.18.got = bf16[1,2,5,32,256]{4,3,2,1,0:T(8,128)(2,1)S(1)} collective-permute-done((bf16[1,2,5,32,256]{4,3,2,1,0:T(8,128)(2,1)S(1)}, bf16[1,2,5,32,256]{4,3,2,1,0:T(8,128)(2,1)S(1)}, u32[]{:S(2)}, u32[]{:S(2)}) %collective-permute-start.18) | collective-permute-done | bytes 163872 | tf_op jit(solution)/shard_map/ppermute | solution.py:308
  85.0 1.1 %finish.1 = f32[2,2,9,32,256]{4,3,2,1,0:T(8,128)} custom-call(f32[2,2,9,32,256]{4,3,2,1,0:T(8,128)S(1)} %finish_some.1.some, bf16[1,2,5,32,256]{4,3,2,1,0:T(8,128)(2,1)S(1)} %get-tuple-element.92.keep, bf16[1,2,5,32,256]{4,3,2,1,0:T(8,128)(2,1)S(1)} %collective-permute-done.18.got), custom_call_target="tpu_custom_call" | custom-call | flops 603979776 | bytes 1024 | tf_op jit(solution)/shard_map/finish/pallas_call | solution.py:54
  (37 shorter events, 1.9 us)
Async XLA Ops:
  0.6 2.9 %slice-start = ((s8[4718592]{0:T(1024)(128)(4,1)}), s8[4194304]{0:T(1024)(128)(4,1)S(1)}, s32[]{:S(2)}) async-start(s8[4718592]{0:T(1024)(128)(4,1)} %bitcast.12), calls=%async_computation | async-start | bytes 8388608
  0.6 0.8 copy-start.4
  1.5 2.1 %slice-start.1 = ((s8[4718592]{0:T(1024)(128)(4,1)}), s8[524288]{0:T(1024)(128)(4,1)S(1)}, s32[]{:S(2)}) async-start(s8[4718592]{0:T(1024)(128)(4,1)} %bitcast.12), calls=%async_computation.1 | async-start | bytes 1048576
  5.2 6.6 %collective-permute-start = (bf16[512,256]{1,0:T(8,128)(2,1)S(1)}, bf16[512,256]{1,0:T(8,128)(2,1)S(1)}, u32[]{:S(2)}, u32[]{:S(2)}) collective-permute-start(bf16[512,256]{1,0:T(8,128)(2,1)S(1)} %late_1_0.1.refs_1_), channel_id=1, source_target_pairs={{0,8},{16,24},{32,40},{48,56},{64,72},{80,88},{96,104},{112,120},{... | collective-permute-start | bytes 786440 | tf_op jit(solution)/shard_map/ppermute | solution.py:304
  6.1 5.7 %copy-start = (bf16[2,1,4,1,16,32,256]{6,5,4,3,2,1,0:T(8,128)(2,1)S(1)}, bf16[2,1,4,1,16,32,256]{6,5,4,3,2,1,0:T(8,128)(2,1)}, u32[]{:S(2)}) copy-start(bf16[2,1,4,1,16,32,256]{6,5,4,3,2,1,0:T(8,128)(2,1)} %param.10) | copy-start | bytes 6291460
  6.2 5.7 %copy-start.1 = (bf16[2,1,4,1,16,32,256]{6,5,4,3,2,1,0:T(8,128)(2,1)S(1)}, bf16[2,1,4,1,16,32,256]{6,5,4,3,2,1,0:T(8,128)(2,1)}, u32[]{:S(2)}) copy-start(bf16[2,1,4,1,16,32,256]{6,5,4,3,2,1,0:T(8,128)(2,1)} %param.11) | copy-start | bytes 6291460
  7.0 9.9 %collective-permute-start.2 = (bf16[512,256]{1,0:T(8,128)(2,1)S(1)}, bf16[512,256]{1,0:T(8,128)(2,1)S(1)}, u32[]{:S(2)}, u32[]{:S(2)}) collective-permute-start(bf16[512,256]{1,0:T(8,128)(2,1)S(1)} %late_0_0.1.refs_1_), channel_id=1, source_target_pairs={{8,16},{24,32},{40,48},{56,64},{72,80},{88,96},{104,112},{16,8},{3... | collective-permute-start | bytes 786440 | tf_op jit(solution)/shard_map/ppermute | solution.py:304
  12.8 4.1 %copy-start.3 = (bf16[3,1,16,32,256]{4,3,2,1,0:T(8,128)(2,1)S(1)}, bf16[3,1,16,32,256]{4,3,2,1,0:T(8,128)(2,1)}, u32[]{:S(2)}) copy-start(bf16[3,1,16,32,256]{4,3,2,1,0:T(8,128)(2,1)} %param.8) | copy-start | bytes 2359300
  13.7 9.8 %collective-permute-start.1 = (bf16[512,256]{1,0:T(8,128)(2,1)S(1)}, bf16[512,256]{1,0:T(8,128)(2,1)S(1)}, u32[]{:S(2)}, u32[]{:S(2)}) collective-permute-start(bf16[512,256]{1,0:T(8,128)(2,1)S(1)} %late_0_1.1.refs_5_), channel_id=1, source_target_pairs={{8,16},{24,32},{40,48},{56,64},{72,80},{88,96},{104,112},{16,8},{3... | collective-permute-start | bytes 786440 | tf_op jit(solution)/shard_map/ppermute | solution.py:304
  18.0 1.6 %copy-start.2 = (bf16[2,1,4,1,16,32,256]{6,5,4,3,2,1,0:T(8,128)(2,1)S(1)}, bf16[2,1,4,1,16,32,256]{6,5,4,3,2,1,0:T(8,128)(2,1)}, u32[]{:S(2)}) copy-start(bf16[2,1,4,1,16,32,256]{6,5,4,3,2,1,0:T(8,128)(2,1)} %param.9) | copy-start | bytes 6291460
  18.8 6.5 %collective-permute-start.4 = (bf16[512,256]{1,0:T(8,128)(2,1)S(1)}, bf16[512,256]{1,0:T(8,128)(2,1)S(1)}, u32[]{:S(2)}, u32[]{:S(2)}) collective-permute-start(bf16[512,256]{1,0:T(8,128)(2,1)S(1)} %late_1_1.1.refs_5_), channel_id=1, source_target_pairs={{0,8},{16,24},{32,40},{48,56},{64,72},{80,88},{96,104},{112,120},{... | collective-permute-start | bytes 786440 | tf_op jit(solution)/shard_map/ppermute | solution.py:304
  27.2 9.8 %collective-permute-start.5 = (bf16[512,256]{1,0:T(8,128)(2,1)S(1)}, bf16[512,256]{1,0:T(8,128)(2,1)S(1)}, u32[]{:S(2)}, u32[]{:S(2)}) collective-permute-start(bf16[512,256]{1,0:T(8,128)(2,1)S(1)} %late_0_2.1.refs_2_), channel_id=1, source_target_pairs={{8,16},{24,32},{40,48},{56,64},{72,80},{88,96},{104,112},{16,8},{3... | collective-permute-start | bytes 786440 | tf_op jit(solution)/shard_map/ppermute | solution.py:304
  31.1 5.9 %collective-permute-start.3 = (bf16[512,256]{1,0:T(8,128)(2,1)S(1)}, bf16[512,256]{1,0:T(8,128)(2,1)S(1)}, u32[]{:S(2)}, u32[]{:S(2)}) collective-permute-start(bf16[512,256]{1,0:T(8,128)(2,1)S(1)} %late_1_2.1.refs_3_), channel_id=1, source_target_pairs={{0,8},{16,24},{32,40},{48,56},{64,72},{80,88},{96,104},{112,120},{... | collective-permute-start | bytes 786440 | tf_op jit(solution)/shard_map/ppermute | solution.py:304
  39.3 18.1 %collective-permute-start.8 = (bf16[4,2,5,32,256]{4,3,2,1,0:T(8,128)(2,1)S(1)}, bf16[4,2,5,32,256]{4,3,2,1,0:T(8,128)(2,1)S(1)}, u32[]{:S(2)}, u32[]{:S(2)}) collective-permute-start(bf16[4,2,5,32,256]{4,3,2,1,0:T(8,128)(2,1)S(1)} %get-tuple-element.70), channel_id=1, source_target_pairs={{0,1},{1,0},{2,3},{3,2},{4,5},{5,4},{6,7},{7,6},{8,9},{9,8},{10,11... | collective-permute-start | bytes 1966088 | tf_op jit(solution)/shard_map/ppermute | solution.py:308
  41.3 16.1 %collective-permute-start.9 = (bf16[4,2,4,32,256]{4,3,2,1,0:T(8,128)(2,1)S(1)}, bf16[4,2,4,32,256]{4,3,2,1,0:T(8,128)(2,1)S(1)}, u32[]{:S(2)}, u32[]{:S(2)}) collective-permute-start(bf16[4,2,4,32,256]{4,3,2,1,0:T(8,128)(2,1)S(1)} %get-tuple-element.71), channel_id=1, source_target_pairs={{0,3},{1,2},{2,1},{3,0},{4,7},{5,6},{6,5},{7,4},{8,11},{9,10},{10,... | collective-permute-start | bytes 1572872 | tf_op jit(solution)/shard_map/ppermute | solution.py:308
  48.9 17.4 %collective-permute-start.6 = (bf16[4,2,2,32,256]{4,3,2,1,0:T(8,128)(2,1)S(1)}, bf16[4,2,2,32,256]{4,3,2,1,0:T(8,128)(2,1)S(1)}, u32[]{:S(2)}, u32[]{:S(2)}) collective-permute-start(bf16[4,2,2,32,256]{4,3,2,1,0:T(8,128)(2,1)S(1)} %get-tuple-element.64), channel_id=1, source_target_pairs={{0,1},{1,0},{2,3},{3,2},{4,5},{5,4},{6,7},{7,6},{8,9},{9,8},{10,11... | collective-permute-start | bytes 786440 | tf_op jit(solution)/shard_map/ppermute | solution.py:308
  50.0 16.6 %collective-permute-start.13 = (bf16[4,2,2,32,256]{4,3,2,1,0:T(8,128)(2,1)S(1)}, bf16[4,2,2,32,256]{4,3,2,1,0:T(8,128)(2,1)S(1)}, u32[]{:S(2)}, u32[]{:S(2)}) collective-permute-start(bf16[4,2,2,32,256]{4,3,2,1,0:T(8,128)(2,1)S(1)} %get-tuple-element.81), channel_id=1, source_target_pairs={{0,3},{1,2},{2,1},{3,0},{4,7},{5,6},{6,5},{7,4},{8,11},{9,10},{10,... | collective-permute-start | bytes 786440 | tf_op jit(solution)/shard_map/ppermute | solution.py:308
  50.6 19.2 %collective-permute-start.16 = (bf16[4,2,5,32,256]{4,3,2,1,0:T(8,128)(2,1)S(1)}, bf16[4,2,5,32,256]{4,3,2,1,0:T(8,128)(2,1)S(1)}, u32[]{:S(2)}, u32[]{:S(2)}) collective-permute-start(bf16[4,2,5,32,256]{4,3,2,1,0:T(8,128)(2,1)S(1)} %get-tuple-element.89), channel_id=1, source_target_pairs={{0,4},{1,5},{2,6},{3,7},{4,0},{5,1},{6,2},{7,3},{8,12},{9,13},{10,... | collective-permute-start | bytes 1966088 | tf_op jit(solution)/shard_map/ppermute | solution.py:308
  57.7 16.5 %collective-permute-start.10 = (bf16[2,2,5,32,256]{4,3,2,1,0:T(8,128)(2,1)S(1)}, bf16[2,2,5,32,256]{4,3,2,1,0:T(8,128)(2,1)S(1)}, u32[]{:S(2)}, u32[]{:S(2)}) collective-permute-start(bf16[2,2,5,32,256]{4,3,2,1,0:T(8,128)(2,1)S(1)} %get-tuple-element.74), channel_id=1, source_target_pairs={{0,3},{1,2},{2,1},{3,0},{4,7},{5,6},{6,5},{7,4},{8,11},{9,10},{10,... | collective-permute-start | bytes 983048 | tf_op jit(solution)/shard_map/ppermute | solution.py:308
  61.5 12.7 %collective-permute-start.11 = (bf16[2,2,4,32,256]{4,3,2,1,0:T(8,128)(2,1)S(1)}, bf16[2,2,4,32,256]{4,3,2,1,0:T(8,128)(2,1)S(1)}, u32[]{:S(2)}, u32[]{:S(2)}) collective-permute-start(bf16[2,2,4,32,256]{4,3,2,1,0:T(8,128)(2,1)S(1)} %get-tuple-element.75), channel_id=1, source_target_pairs={{0,4},{1,5},{2,6},{3,7},{4,0},{5,1},{6,2},{7,3},{8,12},{9,13},{10,... | collective-permute-start | bytes 786440 | tf_op jit(solution)/shard_map/ppermute | solution.py:308
  66.4 8.0 %collective-permute-start.7 = (bf16[2,2,2,32,256]{4,3,2,1,0:T(8,128)(2,1)S(1)}, bf16[2,2,2,32,256]{4,3,2,1,0:T(8,128)(2,1)S(1)}, u32[]{:S(2)}, u32[]{:S(2)}) collective-permute-start(bf16[2,2,2,32,256]{4,3,2,1,0:T(8,128)(2,1)S(1)} %get-tuple-element.67), channel_id=1, source_target_pairs={{0,3},{1,2},{2,1},{3,0},{4,7},{5,6},{6,5},{7,4},{8,11},{9,10},{10,... | collective-permute-start | bytes 393224 | tf_op jit(solution)/shard_map/ppermute | solution.py:308
  66.6 10.5 %collective-permute-start.14 = (bf16[2,2,2,32,256]{4,3,2,1,0:T(8,128)(2,1)S(1)}, bf16[2,2,2,32,256]{4,3,2,1,0:T(8,128)(2,1)S(1)}, u32[]{:S(2)}, u32[]{:S(2)}) collective-permute-start(bf16[2,2,2,32,256]{4,3,2,1,0:T(8,128)(2,1)S(1)} %get-tuple-element.83), channel_id=1, source_target_pairs={{0,4},{1,5},{2,6},{3,7},{4,0},{5,1},{6,2},{7,3},{8,12},{9,13},{10,... | collective-permute-start | bytes 393224 | tf_op jit(solution)/shard_map/ppermute | solution.py:308
  69.9 8.4 %collective-permute-start.17 = (bf16[2,2,5,32,256]{4,3,2,1,0:T(8,128)(2,1)S(1)}, bf16[2,2,5,32,256]{4,3,2,1,0:T(8,128)(2,1)S(1)}, u32[]{:S(2)}, u32[]{:S(2)}) collective-permute-start(bf16[2,2,5,32,256]{4,3,2,1,0:T(8,128)(2,1)S(1)} %get-tuple-element.91), channel_id=1, source_target_pairs={{0,1},{1,0},{2,3},{3,2},{4,5},{5,4},{6,7},{7,6},{8,9},{9,8},{10,11... | collective-permute-start | bytes 983048 | tf_op jit(solution)/shard_map/ppermute | solution.py:308
  74.4 8.5 %collective-permute-start.12 = (bf16[1,2,7,32,256]{4,3,2,1,0:T(8,128)(2,1)S(1)}, bf16[1,2,7,32,256]{4,3,2,1,0:T(8,128)(2,1)S(1)}, u32[]{:S(2)}, u32[]{:S(2)}) collective-permute-start(bf16[1,2,7,32,256]{4,3,2,1,0:T(8,128)(2,1)S(1)} %get-tuple-element.79), channel_id=1, source_target_pairs={{0,4},{1,5},{2,6},{3,7},{4,0},{5,1},{6,2},{7,3},{8,12},{9,13},{10,... | collective-permute-start | bytes 688136 | tf_op jit(solution)/shard_map/ppermute | solution.py:308
  77.2 5.8 %collective-permute-start.15 = (bf16[1,2,6,32,256]{4,3,2,1,0:T(8,128)(2,1)S(1)}, bf16[1,2,6,32,256]{4,3,2,1,0:T(8,128)(2,1)S(1)}, u32[]{:S(2)}, u32[]{:S(2)}) collective-permute-start(bf16[1,2,6,32,256]{4,3,2,1,0:T(8,128)(2,1)S(1)} %get-tuple-element.87), channel_id=1, source_target_pairs={{0,1},{1,0},{2,3},{3,2},{4,5},{5,4},{6,7},{7,6},{8,9},{9,8},{10,11... | collective-permute-start | bytes 589832 | tf_op jit(solution)/shard_map/ppermute | solution.py:308
  78.4 6.6 %collective-permute-start.18 = (bf16[1,2,5,32,256]{4,3,2,1,0:T(8,128)(2,1)S(1)}, bf16[1,2,5,32,256]{4,3,2,1,0:T(8,128)(2,1)S(1)}, u32[]{:S(2)}, u32[]{:S(2)}) collective-permute-start(bf16[1,2,5,32,256]{4,3,2,1,0:T(8,128)(2,1)S(1)} %get-tuple-element.93), channel_id=1, source_target_pairs={{0,3},{1,2},{2,1},{3,0},{4,7},{5,6},{6,5},{7,4},{8,11},{9,10},{10,... | collective-permute-start | bytes 491528 | tf_op jit(solution)/shard_map/ppermute | solution.py:308

commit v6 on v5

--- a/solution.py
+++ b/solution.py
@@ -28,7 +28,7 @@
     "y": [(d, d ^ 4) for d in range(DP)],
 }
 ORDERS = ("aby", "bya", "yab")
-TAPS = ((2, 2, 5), (5, 4, 0))
+TAPS = ((3, 2, 4), (5, 4, 0))
 FIRST = tuple(tuple(sum(taps[:o]) for o in range(3)) for taps in TAPS)
 
 VM = pl.BlockSpec(memory_space=pltpu.VMEM)

time: 86.6 us -> 87.4 us (level)
  waiting for transfers between devices: 15.7 us -> 18.1 us
  starting transfers between devices: 36.1 us -> 34.1 us
    ppermute x13, waiting for transfers between devices: 13.5 us -> 15.9 us  [exchange(): return lax.ppermute(block, 'dp', PAIRS[step])]
    ppermute x13, starting transfers between devices: 23.9 us -> 21.9 us  [exchange(): return lax.ppermute(block, 'dp', PAIRS[step])]
  transfers between devices with their start and end apart: 19 -> 19, of which waited for: 9 -> 8; matrix products, arithmetic and copies ran while one was open for 0% -> 0% of each run, Pallas kernels for 27% -> 27%
where the time goes in v6:
time: 87.4 us; the launch traced here: 86.6 us
  starting transfers between devices  34.1 us (39%)
  Pallas kernels  32 us (37%)
  waiting for transfers between devices  18.1 us (21%)
  local copies, waits for them, and re-layouts  1.33 us (2%)
  between operations  1.02 us (1%)
    pallas_call x31, Pallas kernels, call(): pl.pallas_call(body if after else kernel, out_shape=outs, in_specs=[VM] *...  30 us
    ppermute x13, starting transfers between devices, exchange(): return lax.ppermute(block, 'dp', PAIRS[step])  21.9 us
    ppermute x13, waiting for transfers between devices, exchange(): return lax.ppermute(block, 'dp', PAIRS[step])  15.9 us
    ppermute x6, starting transfers between devices, relay(): return lax.ppermute(block, 'section', pairs + [(b, a) for a, b in pairs])  12.2 us
    ppermute x6, waiting for transfers between devices, relay(): return lax.ppermute(block, 'section', pairs + [(b, a) for a, b in pairs])  2.22 us
    pallas_call x1, Pallas kernels, prepare(): pl.pallas_call(prepare_kernel, grid_spec=pltpu.PrefetchScalarGridSpec(num...  2.04 us
  transfers between devices with their start and end apart: 19, of which 8 were waited for; matrix products, arithmetic and copies ran while one was open for 0% of the time, Pallas kernels for 27%

profile of v6, /device:TPU:8, one launch (start us, length us, event | category | flops | bytes accessed | tf_op | source)
XLA Modules:
  0.0 86.6 jit_solution(7843832944792362530)
XLA Ops:
  0.7 0.8 copy-done.4
  1.5 2.0 %prepare.1 = (bf16[512,256]{1,0:T(8,128)(2,1)S(1)}, bf16[512,256]{1,0:T(8,128)(2,1)S(1)}, bf16[512,256]{1,0:T(8,128)(2,1)S(1)}, bf16[512,256]{1,0:T(8,128)(2,1)S(1)}) custom-call(s32[4,32]{1,0:T(4,128)S(1)} %copy-done.4, bf16[2,512,256]{2,1,0:T(8,128)(2,1)} %bitcast.53, bf16[2,512,256]{2,1,0:T(8,128)(2,1)} %bitcast.54, bf16[8,512,256]{2,1,0:T(8,128)(2,1)} %bitcast.40, ...), custom_call_target="tpu_custom_call" | custom-call | flops 1 | bytes 1024 | tf_op jit(solution)/shard_map/prepare/pallas_call | solution.py:132
  3.5 0.8 early_1_0.1.g1.refs_0_
  4.4 0.8 late_1_0.1.refs_1_
  5.3 0.8 early_0_0.1.refs_0_.g1
  6.2 0.8 late_0_0.1.refs_1_
  7.0 4.8 %collective-permute-start.2 = (bf16[512,256]{1,0:T(8,128)(2,1)S(1)}, bf16[512,256]{1,0:T(8,128)(2,1)S(1)}, u32[]{:S(2)}, u32[]{:S(2)}) collective-permute-start(bf16[512,256]{1,0:T(8,128)(2,1)S(1)} %late_0_0.1.refs_1_), channel_id=1, source_target_pairs={{8,16},{24,32},{40,48},{56,64},{72,80},{88,96},{104,112},{16,8},{3... | collective-permute-start | bytes 786440 | tf_op jit(solution)/shard_map/ppermute | solution.py:304
  11.8 1.0 %early_0_1.1 = (bf16[512,256]{1,0:T(8,128)(2,1)S(1)}, bf16[512,256]{1,0:T(8,128)(2,1)S(1)}) custom-call(s32[4,32]{1,0:T(4,128)S(1)} %copy-done.4, bf16[8,512,256]{2,1,0:T(8,128)(2,1)S(1)} %bitcast.31, bf16[8,512,256]{2,1,0:T(8,128)(2,1)S(1)} %bitcast.42, bf16[36,256,256]{2,1,0:T(8,128)(2,1)S(1)} %bitcast.18, ...), custom_call_target="tpu_custom_call" | custom-call | flops 603979776 | bytes 1024 | tf_op jit(solution)/shard_map/early_0_1/pallas_call | solution.py:54
  12.8 0.8 late_0_1.1.refs_5_
  13.7 3.0 %collective-permute-start.1 = (bf16[512,256]{1,0:T(8,128)(2,1)S(1)}, bf16[512,256]{1,0:T(8,128)(2,1)S(1)}, u32[]{:S(2)}, u32[]{:S(2)}) collective-permute-start(bf16[512,256]{1,0:T(8,128)(2,1)S(1)} %late_0_1.1.refs_5_), channel_id=1, source_target_pairs={{8,16},{24,32},{40,48},{56,64},{72,80},{88,96},{104,112},{16,8},{3... | collective-permute-start | bytes 786440 | tf_op jit(solution)/shard_map/ppermute | solution.py:304
  16.7 0.2 collective-permute-done.2.refs_0_
  16.9 1.0 %early_1_1.1 = (bf16[512,256]{1,0:T(8,128)(2,1)S(1)}, bf16[512,256]{1,0:T(8,128)(2,1)S(1)}) custom-call(s32[4,32]{1,0:T(4,128)S(1)} %copy-done.4, bf16[8,512,256]{2,1,0:T(8,128)(2,1)S(1)} %bitcast.32, bf16[8,512,256]{2,1,0:T(8,128)(2,1)S(1)} %bitcast.43, bf16[36,256,256]{2,1,0:T(8,128)(2,1)S(1)} %bitcast.20, ...), custom_call_target="tpu_custom_call" | custom-call | flops 603979776 | bytes 1024 | tf_op jit(solution)/shard_map/early_1_1/pallas_call | solution.py:54
  18.0 0.8 late_1_1.1.refs_5_
  18.8 0.3 collective-permute-start.4
  19.1 0.5 copy-done.2
  19.6 1.6 %wgrad1_1.1.refs_8_.refs_7_.refs_5_ = f32[9,256,256]{2,1,0:T(8,128)S(1)} custom-call(s32[4,32]{1,0:T(4,128)S(1)} %copy-done.4, bf16[8,512,256]{2,1,0:T(8,128)(2,1)S(1)} %bitcast.47, bf16[512,256]{1,0:T(8,128)(2,1)S(1)} %early_1_0.1.g1.refs_0_, bf16[512,256]{1,0:T(8,128)(2,1)S(1)} %get-tuple-element.53.refs_1_.g1), custom_call_target="tpu_custom_call" | custom-call | flops 1207959552 | bytes 1024 | tf_op jit(solution)/shard_map/wgrad1_1/pallas_call | solution.py:54
  21.1 1.6 %wgrad1_0.1.refs_7_.refs_6_.refs_4_ = f32[9,256,256]{2,1,0:T(8,128)S(1)} custom-call(s32[4,32]{1,0:T(4,128)S(1)} %copy-done.4, bf16[8,512,256]{2,1,0:T(8,128)(2,1)S(1)} %bitcast.48, bf16[512,256]{1,0:T(8,128)(2,1)S(1)} %early_0_0.1.refs_0_.g1, bf16[512,256]{1,0:T(8,128)(2,1)S(1)} %get-tuple-element.50.g1.refs_1_), custom_call_target="tpu_custom_call" | custom-call | flops 1207959552 | bytes 1024 | tf_op jit(solution)/shard_map/wgrad1_0/pallas_call | solution.py:54
  22.7 0.7 collective-permute-done.1.refs_4_
  23.5 1.0 %early_1_2.1 = (bf16[512,256]{1,0:T(8,128)(2,1)S(1)}, bf16[512,256]{1,0:T(8,128)(2,1)S(1)}) custom-call(s32[4,32]{1,0:T(4,128)S(1)} %copy-done.4, bf16[8,512,256]{2,1,0:T(8,128)(2,1)S(1)} %bitcast.33, bf16[8,512,256]{2,1,0:T(8,128)(2,1)S(1)} %bitcast.44, bf16[36,256,256]{2,1,0:T(8,128)(2,1)S(1)} %bitcast.22, ...), custom_call_target="tpu_custom_call" | custom-call | flops 603979776 | bytes 1024 | tf_op jit(solution)/shard_map/early_1_2/pallas_call | solution.py:54
  24.5 0.8 late_1_2.1.refs_3_
  25.3 1.0 %early_0_2.1 = (bf16[512,256]{1,0:T(8,128)(2,1)S(1)}, bf16[512,256]{1,0:T(8,128)(2,1)S(1)}) custom-call(s32[4,32]{1,0:T(4,128)S(1)} %copy-done.4, bf16[8,512,256]{2,1,0:T(8,128)(2,1)S(1)} %bitcast.34, bf16[8,512,256]{2,1,0:T(8,128)(2,1)S(1)} %bitcast.45, bf16[36,256,256]{2,1,0:T(8,128)(2,1)S(1)} %bitcast.24, ...), custom_call_target="tpu_custom_call" | custom-call | flops 603979776 | bytes 1024 | tf_op jit(solution)/shard_map/early_0_2/pallas_call | solution.py:54
  26.3 0.8 late_0_2.1.refs_2_
  27.2 3.9 %collective-permute-start.5 = (bf16[512,256]{1,0:T(8,128)(2,1)S(1)}, bf16[512,256]{1,0:T(8,128)(2,1)S(1)}, u32[]{:S(2)}, u32[]{:S(2)}) collective-permute-start(bf16[512,256]{1,0:T(8,128)(2,1)S(1)} %late_0_2.1.refs_2_), channel_id=1, source_target_pairs={{8,16},{24,32},{40,48},{56,64},{72,80},{88,96},{104,112},{16,8},{3... | collective-permute-start | bytes 786440 | tf_op jit(solution)/shard_map/ppermute | solution.py:304
  31.2 2.3 %wgrad2_1.1.refs_5_ = f32[9,256,256]{2,1,0:T(8,128)S(1)} custom-call(s32[4,32]{1,0:T(4,128)S(1)} %copy-done.4, bf16[8,512,256]{2,1,0:T(8,128)(2,1)S(1)} %bitcast.35, bf16[512,256]{1,0:T(8,128)(2,1)S(1)} %get-tuple-element.49.g2.refs_0_, bf16[512,256]{1,0:T(8,128)(2,1)S(1)} %get-tuple-element.58.refs_1_, bf16[512,256]{1,0:T(8,128)(2,1)S(1)} %get-tuple-element.59.refs_2_), custom_call_target="tpu_custom_call" | custom-call | flops 1811939328 | bytes 1024 | tf_op jit(solution)/shard_map/wgrad2_1/pallas_call | solution.py:54
  33.5 2.3 %wgrad2_0.1.refs_4_ = f32[9,256,256]{2,1,0:T(8,128)S(1)} custom-call(s32[4,32]{1,0:T(4,128)S(1)} %copy-done.4, bf16[8,512,256]{2,1,0:T(8,128)(2,1)S(1)} %bitcast.36, bf16[512,256]{1,0:T(8,128)(2,1)S(1)} %get-tuple-element.52.g2.refs_0_, bf16[512,256]{1,0:T(8,128)(2,1)S(1)} %get-tuple-element.56.refs_1_, bf16[512,256]{1,0:T(8,128)(2,1)S(1)} %get-tuple-element.57.refs_2_), custom_call_target="tpu_custom_call" | custom-call | flops 1811939328 | bytes 1024 | tf_op jit(solution)/shard_map/wgrad2_0/pallas_call | solution.py:54
  35.7 1.2 %collective-permute-done.5.refs_1_ = bf16[512,256]{1,0:T(8,128)(2,1)S(1)} collective-permute-done((bf16[512,256]{1,0:T(8,128)(2,1)S(1)}, bf16[512,256]{1,0:T(8,128)(2,1)S(1)}, u32[]{:S(2)}, u32[]{:S(2)}) %collective-permute-start.5) | collective-permute-done | bytes 262176 | tf_op jit(solution)/shard_map/ppermute | solution.py:304
  37.0 2.3 %last_two.1 = (bf16[4,2,5,32,256]{4,3,2,1,0:T(8,128)(2,1)S(1)}, bf16[4,2,4,32,256]{4,3,2,1,0:T(8,128)(2,1)S(1)}, bf16[4,2,5,32,256]{4,3,2,1,0:T(8,128)(2,1)S(1)}...) custom-call(s32[4,32]{1,0:T(4,128)S(1)} %copy-done.4, ...), custom_call_target="tpu_custom_call" | custom-call | flops 1207959552 | bytes 1024 | tf_op jit(solution)/shard_map/last_two/pallas_call | solution.py:54
  39.3 2.0 %collective-permute-start.8 = (bf16[4,2,5,32,256]{4,3,2,1,0:T(8,128)(2,1)S(1)}, bf16[4,2,5,32,256]{4,3,2,1,0:T(8,128)(2,1)S(1)}, u32[]{:S(2)}, u32[]{:S(2)}) collective-permute-start(bf16[4,2,5,32,256]{4,3,2,1,0:T(8,128)(2,1)S(1)} %get-tuple-element.70), channel_id=1, source_target_pairs={{0,1},{1,0},{2,3},{3,2},{4,5},{5,4},{6,7},{7,6},{8,9},{9,8},{10,11... | collective-permute-start | bytes 1966088 | tf_op jit(solution)/shard_map/ppermute | solution.py:308
  41.3 2.5 %collective-permute-start.9 = (bf16[4,2,4,32,256]{4,3,2,1,0:T(8,128)(2,1)S(1)}, bf16[4,2,4,32,256]{4,3,2,1,0:T(8,128)(2,1)S(1)}, u32[]{:S(2)}, u32[]{:S(2)}) collective-permute-start(bf16[4,2,4,32,256]{4,3,2,1,0:T(8,128)(2,1)S(1)} %get-tuple-element.71), channel_id=1, source_target_pairs={{0,3},{1,2},{2,1},{3,0},{4,7},{5,6},{6,5},{7,4},{8,11},{9,10},{10,... | collective-permute-start | bytes 1572872 | tf_op jit(solution)/shard_map/ppermute | solution.py:308
  43.9 0.8 early_0_3.1.g1_zero.refs_2_
  44.7 0.8 early_1_3.1.g1_one.refs_3_
  45.5 3.4 %last_one.1 = (bf16[4,2,3,32,256]{4,3,2,1,0:T(8,128)(2,1)S(1)}, bf16[4,2,2,32,256]{4,3,2,1,0:T(8,128)(2,1)S(1)}, bf16[4,2,4,32,256]{4,3,2,1,0:T(8,128)(2,1)S(1)}...) custom-call(s32[4,32]{1,0:T(4,128)S(1)} %copy-done.4, ...), custom_call_target="tpu_custom_call" | custom-call | flops 2415919104 | bytes 1024 | tf_op jit(solution)/shard_map/last_one/pallas_call | solution.py:54
  48.9 0.8 collective-permute-start.13
  49.7 0.4 collective-permute-start.6
  50.1 2.6 %collective-permute-start.16 = (bf16[4,2,4,32,256]{4,3,2,1,0:T(8,128)(2,1)S(1)}, bf16[4,2,4,32,256]{4,3,2,1,0:T(8,128)(2,1)S(1)}, u32[]{:S(2)}, u32[]{:S(2)}) collective-permute-start(bf16[4,2,4,32,256]{4,3,2,1,0:T(8,128)(2,1)S(1)} %get-tuple-element.89), channel_id=1, source_target_pairs={{0,4},{1,5},{2,6},{3,7},{4,0},{5,1},{6,2},{7,3},{8,12},{9,13},{10,... | collective-permute-start | bytes 1572872 | tf_op jit(solution)/shard_map/ppermute | solution.py:308
  52.7 4.7 %collective-permute-done.9.refs_3_ = bf16[4,2,4,32,256]{4,3,2,1,0:T(8,128)(2,1)S(1)} collective-permute-done((bf16[4,2,4,32,256]{4,3,2,1,0:T(8,128)(2,1)S(1)}, bf16[4,2,4,32,256]{4,3,2,1,0:T(8,128)(2,1)S(1)}, u32[]{:S(2)}, u32[]{:S(2)}) %collective-permute-start.9) | collective-permute-done | bytes 524320 | tf_op jit(solution)/shard_map/ppermute | solution.py:308
  57.4 0.3 fold_two.1
  57.7 3.8 %collective-permute-start.10 = (bf16[2,2,5,32,256]{4,3,2,1,0:T(8,128)(2,1)S(1)}, bf16[2,2,5,32,256]{4,3,2,1,0:T(8,128)(2,1)S(1)}, u32[]{:S(2)}, u32[]{:S(2)}) collective-permute-start(bf16[2,2,5,32,256]{4,3,2,1,0:T(8,128)(2,1)S(1)} %get-tuple-element.74), channel_id=1, source_target_pairs={{0,3},{1,2},{2,1},{3,0},{4,7},{5,6},{6,5},{7,4},{8,11},{9,10},{10,... | collective-permute-start | bytes 983048 | tf_op jit(solution)/shard_map/ppermute | solution.py:308
  61.5 2.6 %collective-permute-start.11 = (bf16[2,2,4,32,256]{4,3,2,1,0:T(8,128)(2,1)S(1)}, bf16[2,2,4,32,256]{4,3,2,1,0:T(8,128)(2,1)S(1)}, u32[]{:S(2)}, u32[]{:S(2)}) collective-permute-start(bf16[2,2,4,32,256]{4,3,2,1,0:T(8,128)(2,1)S(1)} %get-tuple-element.75), channel_id=1, source_target_pairs={{0,4},{1,5},{2,6},{3,7},{4,0},{5,1},{6,2},{7,3},{8,12},{9,13},{10,... | collective-permute-start | bytes 786440 | tf_op jit(solution)/shard_map/ppermute | solution.py:308
  64.1 2.2 %late_3.1 = (bf16[2,512,256]{2,1,0:T(8,128)(2,1)}, f32[8,128]{1,0:T(8,128)S(1)}) custom-call(bf16[36,256,256]{2,1,0:T(8,128)(2,1)S(1)} %bitcast.28, bf16[512,256]{1,0:T(8,128)(2,1)S(1)} %early_0_3.1.g1_zero.refs_2_, bf16[512,256]{1,0:T(8,128)(2,1)S(1)} %early_1_3.1.g1_one.refs_3_), custom_call_target="tpu_custom_call" | custom-call | flops 1207959552 | bytes 1024 | tf_op jit(solution)/shard_map/late_3/pallas_call | solution.py:54
  66.5 1.0 %collective-permute-start.14 = (bf16[2,2,2,32,256]{4,3,2,1,0:T(8,128)(2,1)S(1)}, bf16[2,2,2,32,256]{4,3,2,1,0:T(8,128)(2,1)S(1)}, u32[]{:S(2)}, u32[]{:S(2)}) collective-permute-start(bf16[2,2,2,32,256]{4,3,2,1,0:T(8,128)(2,1)S(1)} %get-tuple-element.83), channel_id=1, source_target_pairs={{0,4},{1,5},{2,6},{3,7},{4,0},{5,1},{6,2},{7,3},{8,12},{9,13},{10,... | collective-permute-start | bytes 393224 | tf_op jit(solution)/shard_map/ppermute | solution.py:308
  67.5 3.2 %collective-permute-start.7 = (bf16[2,2,3,32,256]{4,3,2,1,0:T(8,128)(2,1)S(1)}, bf16[2,2,3,32,256]{4,3,2,1,0:T(8,128)(2,1)S(1)}, u32[]{:S(2)}, u32[]{:S(2)}) collective-permute-start(bf16[2,2,3,32,256]{4,3,2,1,0:T(8,128)(2,1)S(1)} %get-tuple-element.67), channel_id=1, source_target_pairs={{0,3},{1,2},{2,1},{3,0},{4,7},{5,6},{6,5},{7,4},{8,11},{9,10},{10,... | collective-permute-start | bytes 589832 | tf_op jit(solution)/shard_map/ppermute | solution.py:308
  71.1 3.3 %collective-permute-done.7.refs_1_ = bf16[2,2,3,32,256]{4,3,2,1,0:T(8,128)(2,1)S(1)} collective-permute-done((bf16[2,2,3,32,256]{4,3,2,1,0:T(8,128)(2,1)S(1)}, bf16[2,2,3,32,256]{4,3,2,1,0:T(8,128)(2,1)S(1)}, u32[]{:S(2)}, u32[]{:S(2)}) %collective-permute-start.7) | collective-permute-done | bytes 196640 | tf_op jit(solution)/shard_map/ppermute | solution.py:308
  74.4 2.7 %collective-permute-start.12 = (bf16[1,2,8,32,256]{4,3,2,1,0:T(8,128)(2,1)S(1)}, bf16[1,2,8,32,256]{4,3,2,1,0:T(8,128)(2,1)S(1)}, u32[]{:S(2)}, u32[]{:S(2)}) collective-permute-start(bf16[1,2,8,32,256]{4,3,2,1,0:T(8,128)(2,1)S(1)} %get-tuple-element.79), channel_id=1, source_target_pairs={{0,4},{1,5},{2,6},{3,7},{4,0},{5,1},{6,2},{7,3},{8,12},{9,13},{10,... | collective-permute-start | bytes 786440 | tf_op jit(solution)/shard_map/ppermute | solution.py:308
  77.3 1.9 %collective-permute-done.17.refs_1_ = bf16[2,2,4,32,256]{4,3,2,1,0:T(8,128)(2,1)S(1)} collective-permute-done((bf16[2,2,4,32,256]{4,3,2,1,0:T(8,128)(2,1)S(1)}, bf16[2,2,4,32,256]{4,3,2,1,0:T(8,128)(2,1)S(1)}, u32[]{:S(2)}, u32[]{:S(2)}) %collective-permute-start.17) | collective-permute-done | bytes 262176 | tf_op jit(solution)/shard_map/ppermute | solution.py:308
  79.3 3.6 %collective-permute-done.15.refs_3_ = bf16[1,2,6,32,256]{4,3,2,1,0:T(8,128)(2,1)S(1)} collective-permute-done((bf16[1,2,6,32,256]{4,3,2,1,0:T(8,128)(2,1)S(1)}, bf16[1,2,6,32,256]{4,3,2,1,0:T(8,128)(2,1)S(1)}, u32[]{:S(2)}, u32[]{:S(2)}) %collective-permute-start.15) | collective-permute-done | bytes 196640 | tf_op jit(solution)/shard_map/ppermute | solution.py:308
  83.0 2.4 %collective-permute-done.18.got = bf16[1,2,4,32,256]{4,3,2,1,0:T(8,128)(2,1)S(1)} collective-permute-done((bf16[1,2,4,32,256]{4,3,2,1,0:T(8,128)(2,1)S(1)}, bf16[1,2,4,32,256]{4,3,2,1,0:T(8,128)(2,1)S(1)}, u32[]{:S(2)}, u32[]{:S(2)}) %collective-permute-start.18) | collective-permute-done | bytes 131104 | tf_op jit(solution)/shard_map/ppermute | solution.py:308
  85.5 1.1 %finish.1 = f32[2,2,9,32,256]{4,3,2,1,0:T(8,128)} custom-call(f32[2,2,9,32,256]{4,3,2,1,0:T(8,128)S(1)} %finish_some.1.some, bf16[1,2,4,32,256]{4,3,2,1,0:T(8,128)(2,1)S(1)} %get-tuple-element.92.keep, bf16[1,2,4,32,256]{4,3,2,1,0:T(8,128)(2,1)S(1)} %collective-permute-done.18.got), custom_call_target="tpu_custom_call" | custom-call | flops 603979776 | bytes 1024 | tf_op jit(solution)/shard_map/finish/pallas_call | solution.py:54
  (37 shorter events, 1.2 us)
Async XLA Ops:
  0.6 2.9 %slice-start = ((s8[4718592]{0:T(1024)(128)(4,1)}), s8[4194304]{0:T(1024)(128)(4,1)S(1)}, s32[]{:S(2)}) async-start(s8[4718592]{0:T(1024)(128)(4,1)} %bitcast.12), calls=%async_computation | async-start | bytes 8388608
  0.6 0.8 copy-start.4
  1.5 2.1 %slice-start.1 = ((s8[4718592]{0:T(1024)(128)(4,1)}), s8[524288]{0:T(1024)(128)(4,1)S(1)}, s32[]{:S(2)}) async-start(s8[4718592]{0:T(1024)(128)(4,1)} %bitcast.12), calls=%async_computation.1 | async-start | bytes 1048576
  5.2 6.6 %collective-permute-start = (bf16[512,256]{1,0:T(8,128)(2,1)S(1)}, bf16[512,256]{1,0:T(8,128)(2,1)S(1)}, u32[]{:S(2)}, u32[]{:S(2)}) collective-permute-start(bf16[512,256]{1,0:T(8,128)(2,1)S(1)} %late_1_0.1.refs_1_), channel_id=1, source_target_pairs={{0,8},{16,24},{32,40},{48,56},{64,72},{80,88},{96,104},{112,120},{... | collective-permute-start | bytes 786440 | tf_op jit(solution)/shard_map/ppermute | solution.py:304
  6.1 5.7 %copy-start = (bf16[2,1,4,1,16,32,256]{6,5,4,3,2,1,0:T(8,128)(2,1)S(1)}, bf16[2,1,4,1,16,32,256]{6,5,4,3,2,1,0:T(8,128)(2,1)}, u32[]{:S(2)}) copy-start(bf16[2,1,4,1,16,32,256]{6,5,4,3,2,1,0:T(8,128)(2,1)} %param.10) | copy-start | bytes 6291460
  6.2 5.7 %copy-start.1 = (bf16[2,1,4,1,16,32,256]{6,5,4,3,2,1,0:T(8,128)(2,1)S(1)}, bf16[2,1,4,1,16,32,256]{6,5,4,3,2,1,0:T(8,128)(2,1)}, u32[]{:S(2)}) copy-start(bf16[2,1,4,1,16,32,256]{6,5,4,3,2,1,0:T(8,128)(2,1)} %param.11) | copy-start | bytes 6291460
  7.0 9.9 %collective-permute-start.2 = (bf16[512,256]{1,0:T(8,128)(2,1)S(1)}, bf16[512,256]{1,0:T(8,128)(2,1)S(1)}, u32[]{:S(2)}, u32[]{:S(2)}) collective-permute-start(bf16[512,256]{1,0:T(8,128)(2,1)S(1)} %late_0_0.1.refs_1_), channel_id=1, source_target_pairs={{8,16},{24,32},{40,48},{56,64},{72,80},{88,96},{104,112},{16,8},{3... | collective-permute-start | bytes 786440 | tf_op jit(solution)/shard_map/ppermute | solution.py:304
  12.8 4.1 %copy-start.3 = (bf16[3,1,16,32,256]{4,3,2,1,0:T(8,128)(2,1)S(1)}, bf16[3,1,16,32,256]{4,3,2,1,0:T(8,128)(2,1)}, u32[]{:S(2)}) copy-start(bf16[3,1,16,32,256]{4,3,2,1,0:T(8,128)(2,1)} %param.8) | copy-start | bytes 2359300
  13.7 9.8 %collective-permute-start.1 = (bf16[512,256]{1,0:T(8,128)(2,1)S(1)}, bf16[512,256]{1,0:T(8,128)(2,1)S(1)}, u32[]{:S(2)}, u32[]{:S(2)}) collective-permute-start(bf16[512,256]{1,0:T(8,128)(2,1)S(1)} %late_0_1.1.refs_5_), channel_id=1, source_target_pairs={{8,16},{24,32},{40,48},{56,64},{72,80},{88,96},{104,112},{16,8},{3... | collective-permute-start | bytes 786440 | tf_op jit(solution)/shard_map/ppermute | solution.py:304
  18.0 1.6 %copy-start.2 = (bf16[2,1,4,1,16,32,256]{6,5,4,3,2,1,0:T(8,128)(2,1)S(1)}, bf16[2,1,4,1,16,32,256]{6,5,4,3,2,1,0:T(8,128)(2,1)}, u32[]{:S(2)}) copy-start(bf16[2,1,4,1,16,32,256]{6,5,4,3,2,1,0:T(8,128)(2,1)} %param.9) | copy-start | bytes 6291460
  18.8 6.5 %collective-permute-start.4 = (bf16[512,256]{1,0:T(8,128)(2,1)S(1)}, bf16[512,256]{1,0:T(8,128)(2,1)S(1)}, u32[]{:S(2)}, u32[]{:S(2)}) collective-permute-start(bf16[512,256]{1,0:T(8,128)(2,1)S(1)} %late_1_1.1.refs_5_), channel_id=1, source_target_pairs={{0,8},{16,24},{32,40},{48,56},{64,72},{80,88},{96,104},{112,120},{... | collective-permute-start | bytes 786440 | tf_op jit(solution)/shard_map/ppermute | solution.py:304
  27.2 9.8 %collective-permute-start.5 = (bf16[512,256]{1,0:T(8,128)(2,1)S(1)}, bf16[512,256]{1,0:T(8,128)(2,1)S(1)}, u32[]{:S(2)}, u32[]{:S(2)}) collective-permute-start(bf16[512,256]{1,0:T(8,128)(2,1)S(1)} %late_0_2.1.refs_2_), channel_id=1, source_target_pairs={{8,16},{24,32},{40,48},{56,64},{72,80},{88,96},{104,112},{16,8},{3... | collective-permute-start | bytes 786440 | tf_op jit(solution)/shard_map/ppermute | solution.py:304
  31.1 5.9 %collective-permute-start.3 = (bf16[512,256]{1,0:T(8,128)(2,1)S(1)}, bf16[512,256]{1,0:T(8,128)(2,1)S(1)}, u32[]{:S(2)}, u32[]{:S(2)}) collective-permute-start(bf16[512,256]{1,0:T(8,128)(2,1)S(1)} %late_1_2.1.refs_3_), channel_id=1, source_target_pairs={{0,8},{16,24},{32,40},{48,56},{64,72},{80,88},{96,104},{112,120},{... | collective-permute-start | bytes 786440 | tf_op jit(solution)/shard_map/ppermute | solution.py:304
  39.3 18.1 %collective-permute-start.8 = (bf16[4,2,5,32,256]{4,3,2,1,0:T(8,128)(2,1)S(1)}, bf16[4,2,5,32,256]{4,3,2,1,0:T(8,128)(2,1)S(1)}, u32[]{:S(2)}, u32[]{:S(2)}) collective-permute-start(bf16[4,2,5,32,256]{4,3,2,1,0:T(8,128)(2,1)S(1)} %get-tuple-element.70), channel_id=1, source_target_pairs={{0,1},{1,0},{2,3},{3,2},{4,5},{5,4},{6,7},{7,6},{8,9},{9,8},{10,11... | collective-permute-start | bytes 1966088 | tf_op jit(solution)/shard_map/ppermute | solution.py:308
  41.3 16.1 %collective-permute-start.9 = (bf16[4,2,4,32,256]{4,3,2,1,0:T(8,128)(2,1)S(1)}, bf16[4,2,4,32,256]{4,3,2,1,0:T(8,128)(2,1)S(1)}, u32[]{:S(2)}, u32[]{:S(2)}) collective-permute-start(bf16[4,2,4,32,256]{4,3,2,1,0:T(8,128)(2,1)S(1)} %get-tuple-element.71), channel_id=1, source_target_pairs={{0,3},{1,2},{2,1},{3,0},{4,7},{5,6},{6,5},{7,4},{8,11},{9,10},{10,... | collective-permute-start | bytes 1572872 | tf_op jit(solution)/shard_map/ppermute | solution.py:308
  48.9 17.5 %collective-permute-start.13 = (bf16[4,2,2,32,256]{4,3,2,1,0:T(8,128)(2,1)S(1)}, bf16[4,2,2,32,256]{4,3,2,1,0:T(8,128)(2,1)S(1)}, u32[]{:S(2)}, u32[]{:S(2)}) collective-permute-start(bf16[4,2,2,32,256]{4,3,2,1,0:T(8,128)(2,1)S(1)} %get-tuple-element.81), channel_id=1, source_target_pairs={{0,3},{1,2},{2,1},{3,0},{4,7},{5,6},{6,5},{7,4},{8,11},{9,10},{10,... | collective-permute-start | bytes 786440 | tf_op jit(solution)/shard_map/ppermute | solution.py:308
  49.7 16.6 %collective-permute-start.6 = (bf16[4,2,3,32,256]{4,3,2,1,0:T(8,128)(2,1)S(1)}, bf16[4,2,3,32,256]{4,3,2,1,0:T(8,128)(2,1)S(1)}, u32[]{:S(2)}, u32[]{:S(2)}) collective-permute-start(bf16[4,2,3,32,256]{4,3,2,1,0:T(8,128)(2,1)S(1)} %get-tuple-element.64), channel_id=1, source_target_pairs={{0,1},{1,0},{2,3},{3,2},{4,5},{5,4},{6,7},{7,6},{8,9},{9,8},{10,11... | collective-permute-start | bytes 1179656 | tf_op jit(solution)/shard_map/ppermute | solution.py:308
  50.1 20.6 %collective-permute-start.16 = (bf16[4,2,4,32,256]{4,3,2,1,0:T(8,128)(2,1)S(1)}, bf16[4,2,4,32,256]{4,3,2,1,0:T(8,128)(2,1)S(1)}, u32[]{:S(2)}, u32[]{:S(2)}) collective-permute-start(bf16[4,2,4,32,256]{4,3,2,1,0:T(8,128)(2,1)S(1)} %get-tuple-element.89), channel_id=1, source_target_pairs={{0,4},{1,5},{2,6},{3,7},{4,0},{5,1},{6,2},{7,3},{8,12},{9,13},{10,... | collective-permute-start | bytes 1572872 | tf_op jit(solution)/shard_map/ppermute | solution.py:308
  57.7 13.2 %collective-permute-start.10 = (bf16[2,2,5,32,256]{4,3,2,1,0:T(8,128)(2,1)S(1)}, bf16[2,2,5,32,256]{4,3,2,1,0:T(8,128)(2,1)S(1)}, u32[]{:S(2)}, u32[]{:S(2)}) collective-permute-start(bf16[2,2,5,32,256]{4,3,2,1,0:T(8,128)(2,1)S(1)} %get-tuple-element.74), channel_id=1, source_target_pairs={{0,3},{1,2},{2,1},{3,0},{4,7},{5,6},{6,5},{7,4},{8,11},{9,10},{10,... | collective-permute-start | bytes 983048 | tf_op jit(solution)/shard_map/ppermute | solution.py:308
  61.5 9.4 %collective-permute-start.11 = (bf16[2,2,4,32,256]{4,3,2,1,0:T(8,128)(2,1)S(1)}, bf16[2,2,4,32,256]{4,3,2,1,0:T(8,128)(2,1)S(1)}, u32[]{:S(2)}, u32[]{:S(2)}) collective-permute-start(bf16[2,2,4,32,256]{4,3,2,1,0:T(8,128)(2,1)S(1)} %get-tuple-element.75), channel_id=1, source_target_pairs={{0,4},{1,5},{2,6},{3,7},{4,0},{5,1},{6,2},{7,3},{8,12},{9,13},{10,... | collective-permute-start | bytes 786440 | tf_op jit(solution)/shard_map/ppermute | solution.py:308
  66.5 10.6 %collective-permute-start.14 = (bf16[2,2,2,32,256]{4,3,2,1,0:T(8,128)(2,1)S(1)}, bf16[2,2,2,32,256]{4,3,2,1,0:T(8,128)(2,1)S(1)}, u32[]{:S(2)}, u32[]{:S(2)}) collective-permute-start(bf16[2,2,2,32,256]{4,3,2,1,0:T(8,128)(2,1)S(1)} %get-tuple-element.83), channel_id=1, source_target_pairs={{0,4},{1,5},{2,6},{3,7},{4,0},{5,1},{6,2},{7,3},{8,12},{9,13},{10,... | collective-permute-start | bytes 393224 | tf_op jit(solution)/shard_map/ppermute | solution.py:308
  67.5 6.9 %collective-permute-start.7 = (bf16[2,2,3,32,256]{4,3,2,1,0:T(8,128)(2,1)S(1)}, bf16[2,2,3,32,256]{4,3,2,1,0:T(8,128)(2,1)S(1)}, u32[]{:S(2)}, u32[]{:S(2)}) collective-permute-start(bf16[2,2,3,32,256]{4,3,2,1,0:T(8,128)(2,1)S(1)} %get-tuple-element.67), channel_id=1, source_target_pairs={{0,3},{1,2},{2,1},{3,0},{4,7},{5,6},{6,5},{7,4},{8,11},{9,10},{10,... | collective-permute-start | bytes 589832 | tf_op jit(solution)/shard_map/ppermute | solution.py:308
  70.8 8.3 %collective-permute-start.17 = (bf16[2,2,4,32,256]{4,3,2,1,0:T(8,128)(2,1)S(1)}, bf16[2,2,4,32,256]{4,3,2,1,0:T(8,128)(2,1)S(1)}, u32[]{:S(2)}, u32[]{:S(2)}) collective-permute-start(bf16[2,2,4,32,256]{4,3,2,1,0:T(8,128)(2,1)S(1)} %get-tuple-element.91), channel_id=1, source_target_pairs={{0,1},{1,0},{2,3},{3,2},{4,5},{5,4},{6,7},{7,6},{8,9},{9,8},{10,11... | collective-permute-start | bytes 786440 | tf_op jit(solution)/shard_map/ppermute | solution.py:308
  74.4 8.5 %collective-permute-start.12 = (bf16[1,2,8,32,256]{4,3,2,1,0:T(8,128)(2,1)S(1)}, bf16[1,2,8,32,256]{4,3,2,1,0:T(8,128)(2,1)S(1)}, u32[]{:S(2)}, u32[]{:S(2)}) collective-permute-start(bf16[1,2,8,32,256]{4,3,2,1,0:T(8,128)(2,1)S(1)} %get-tuple-element.79), channel_id=1, source_target_pairs={{0,4},{1,5},{2,6},{3,7},{4,0},{5,1},{6,2},{7,3},{8,12},{9,13},{10,... | collective-permute-start | bytes 786440 | tf_op jit(solution)/shard_map/ppermute | solution.py:308
  77.2 5.8 %collective-permute-start.15 = (bf16[1,2,6,32,256]{4,3,2,1,0:T(8,128)(2,1)S(1)}, bf16[1,2,6,32,256]{4,3,2,1,0:T(8,128)(2,1)S(1)}, u32[]{:S(2)}, u32[]{:S(2)}) collective-permute-start(bf16[1,2,6,32,256]{4,3,2,1,0:T(8,128)(2,1)S(1)} %get-tuple-element.87), channel_id=1, source_target_pairs={{0,1},{1,0},{2,3},{3,2},{4,5},{5,4},{6,7},{7,6},{8,9},{9,8},{10,11... | collective-permute-start | bytes 589832 | tf_op jit(solution)/shard_map/ppermute | solution.py:308
  79.2 6.3 %collective-permute-start.18 = (bf16[1,2,4,32,256]{4,3,2,1,0:T(8,128)(2,1)S(1)}, bf16[1,2,4,32,256]{4,3,2,1,0:T(8,128)(2,1)S(1)}, u32[]{:S(2)}, u32[]{:S(2)}) collective-permute-start(bf16[1,2,4,32,256]{4,3,2,1,0:T(8,128)(2,1)S(1)} %get-tuple-element.93), channel_id=1, source_target_pairs={{0,3},{1,2},{2,1},{3,0},{4,7},{5,6},{6,5},{7,4},{8,11},{9,10},{10,... | collective-permute-start | bytes 393224 | tf_op jit(solution)/shard_map/ppermute | solution.py:308

commit v7 on v4

--- a/solution.py
+++ b/solution.py
@@ -27,7 +27,7 @@
     "b": [(d, (d & 4) + 3 - (d & 3)) for d in range(DP)],
     "y": [(d, d ^ 4) for d in range(DP)],
 }
-ORDERS = ("aby", "bya", "yab")
+ORDERS = ("ayb", "bay", "yba")
 
 VM = pl.BlockSpec(memory_space=pltpu.VMEM)
 SM = pl.BlockSpec(memory_space=pltpu.SMEM)

time: 85.8 us -> 86.3 us (level)
  starting transfers between devices: 33.9 us -> 36.7 us
  waiting for transfers between devices: 16 us -> 14.4 us
    ppermute x15, starting transfers between devices: 21.8 us -> 24.6 us  [exchange(): return lax.ppermute(block, 'dp', PAIRS[step])]
    ppermute x15, waiting for transfers between devices: 13.8 us -> 12.1 us  [exchange(): return lax.ppermute(block, 'dp', PAIRS[step])]
  transfers between devices with their start and end apart: 21 -> 21, of which waited for: 13 -> 11; matrix products, arithmetic and copies ran while one was open for 0% -> 0% of each run, Pallas kernels for 27% -> 27%
where the time goes in v7:
time: 86.3 us; the launch traced here: 85.4 us
  starting transfers between devices  36.7 us (43%)
  Pallas kernels  32 us (37%)
  waiting for transfers between devices  14.4 us (17%)
  local copies, waits for them, and re-layouts  1.33 us (2%)
  between operations  1 us (1%)
    pallas_call x31, Pallas kernels, call(): pl.pallas_call(body if after else kernel, out_shape=outs, in_specs=[VM] *...  30 us
    ppermute x15, starting transfers between devices, exchange(): return lax.ppermute(block, 'dp', PAIRS[step])  24.6 us
    ppermute x6, starting transfers between devices, relay(): return lax.ppermute(block, 'section', pairs + [(b, a) for a, b in pairs])  12.2 us
    ppermute x15, waiting for transfers between devices, exchange(): return lax.ppermute(block, 'dp', PAIRS[step])  12.1 us
    ppermute x6, waiting for transfers between devices, relay(): return lax.ppermute(block, 'section', pairs + [(b, a) for a, b in pairs])  2.22 us
    pallas_call x1, Pallas kernels, prepare(): pl.pallas_call(prepare_kernel, grid_spec=pltpu.PrefetchScalarGridSpec(num...  2.04 us
  transfers between devices with their start and end apart: 21, of which 11 were waited for; matrix products, arithmetic and copies ran while one was open for 0% of the time, Pallas kernels for 27%

profile of v7, /device:TPU:8, one launch (start us, length us, event | category | flops | bytes accessed | tf_op | source)
XLA Modules:
  0.0 85.4 jit_solution(9888373227991481656)
XLA Ops:
  0.7 0.8 copy-done.4
  1.5 2.0 %prepare.1 = (bf16[512,256]{1,0:T(8,128)(2,1)S(1)}, bf16[512,256]{1,0:T(8,128)(2,1)S(1)}, bf16[512,256]{1,0:T(8,128)(2,1)S(1)}, bf16[512,256]{1,0:T(8,128)(2,1)S(1)}) custom-call(s32[4,32]{1,0:T(4,128)S(1)} %copy-done.4, bf16[2,512,256]{2,1,0:T(8,128)(2,1)} %bitcast.53, bf16[2,512,256]{2,1,0:T(8,128)(2,1)} %bitcast.54, bf16[8,512,256]{2,1,0:T(8,128)(2,1)} %bitcast.40, ...), custom_call_target="tpu_custom_call" | custom-call | flops 1 | bytes 1024 | tf_op jit(solution)/shard_map/prepare/pallas_call | solution.py:130
  3.5 0.8 early_1_0.1.g1.refs_0_
  4.4 0.8 late_1_0.1.refs_1_
  5.3 0.8 early_0_0.1.refs_0_.g1
  6.2 0.8 late_0_0.1.refs_1_
  7.0 4.8 %collective-permute-start.2 = (bf16[512,256]{1,0:T(8,128)(2,1)S(1)}, bf16[512,256]{1,0:T(8,128)(2,1)S(1)}, u32[]{:S(2)}, u32[]{:S(2)}) collective-permute-start(bf16[512,256]{1,0:T(8,128)(2,1)S(1)} %late_0_0.1.refs_1_), channel_id=1, source_target_pairs={{8,16},{24,32},{40,48},{56,64},{72,80},{88,96},{104,112},{16,8},{3... | collective-permute-start | bytes 786440 | tf_op jit(solution)/shard_map/ppermute | solution.py:296
  11.8 1.0 %early_0_1.1 = (bf16[512,256]{1,0:T(8,128)(2,1)S(1)}, bf16[512,256]{1,0:T(8,128)(2,1)S(1)}) custom-call(s32[4,32]{1,0:T(4,128)S(1)} %copy-done.4, bf16[8,512,256]{2,1,0:T(8,128)(2,1)S(1)} %bitcast.31, bf16[8,512,256]{2,1,0:T(8,128)(2,1)S(1)} %bitcast.42, bf16[36,256,256]{2,1,0:T(8,128)(2,1)S(1)} %bitcast.18, ...), custom_call_target="tpu_custom_call" | custom-call | flops 603979776 | bytes 1024 | tf_op jit(solution)/shard_map/early_0_1/pallas_call | solution.py:52
  12.8 0.8 late_0_1.1.refs_5_
  13.7 3.0 %collective-permute-start.1 = (bf16[512,256]{1,0:T(8,128)(2,1)S(1)}, bf16[512,256]{1,0:T(8,128)(2,1)S(1)}, u32[]{:S(2)}, u32[]{:S(2)}) collective-permute-start(bf16[512,256]{1,0:T(8,128)(2,1)S(1)} %late_0_1.1.refs_5_), channel_id=1, source_target_pairs={{8,16},{24,32},{40,48},{56,64},{72,80},{88,96},{104,112},{16,8},{3... | collective-permute-start | bytes 786440 | tf_op jit(solution)/shard_map/ppermute | solution.py:296
  16.9 1.0 %early_1_1.1 = (bf16[512,256]{1,0:T(8,128)(2,1)S(1)}, bf16[512,256]{1,0:T(8,128)(2,1)S(1)}) custom-call(s32[4,32]{1,0:T(4,128)S(1)} %copy-done.4, bf16[8,512,256]{2,1,0:T(8,128)(2,1)S(1)} %bitcast.32, bf16[8,512,256]{2,1,0:T(8,128)(2,1)S(1)} %bitcast.43, bf16[36,256,256]{2,1,0:T(8,128)(2,1)S(1)} %bitcast.20, ...), custom_call_target="tpu_custom_call" | custom-call | flops 603979776 | bytes 1024 | tf_op jit(solution)/shard_map/early_1_1/pallas_call | solution.py:52
  18.0 0.8 late_1_1.1.refs_5_
  19.6 1.6 %wgrad1_1.1.refs_8_.refs_7_.refs_5_ = f32[9,256,256]{2,1,0:T(8,128)S(1)} custom-call(s32[4,32]{1,0:T(4,128)S(1)} %copy-done.4, bf16[8,512,256]{2,1,0:T(8,128)(2,1)S(1)} %bitcast.47, bf16[512,256]{1,0:T(8,128)(2,1)S(1)} %early_1_0.1.g1.refs_0_, bf16[512,256]{1,0:T(8,128)(2,1)S(1)} %get-tuple-element.59.refs_1_.g1), custom_call_target="tpu_custom_call" | custom-call | flops 1207959552 | bytes 1024 | tf_op jit(solution)/shard_map/wgrad1_1/pallas_call | solution.py:52
  21.1 1.6 %wgrad1_0.1.refs_7_.refs_6_.refs_4_ = f32[9,256,256]{2,1,0:T(8,128)S(1)} custom-call(s32[4,32]{1,0:T(4,128)S(1)} %copy-done.4, bf16[8,512,256]{2,1,0:T(8,128)(2,1)S(1)} %bitcast.48, bf16[512,256]{1,0:T(8,128)(2,1)S(1)} %early_0_0.1.refs_0_.g1, bf16[512,256]{1,0:T(8,128)(2,1)S(1)} %get-tuple-element.56.g1.refs_1_), custom_call_target="tpu_custom_call" | custom-call | flops 1207959552 | bytes 1024 | tf_op jit(solution)/shard_map/wgrad1_0/pallas_call | solution.py:52
  22.7 0.7 collective-permute-done.1.refs_4_
  23.5 1.0 %early_1_2.1 = (bf16[512,256]{1,0:T(8,128)(2,1)S(1)}, bf16[512,256]{1,0:T(8,128)(2,1)S(1)}) custom-call(s32[4,32]{1,0:T(4,128)S(1)} %copy-done.4, bf16[8,512,256]{2,1,0:T(8,128)(2,1)S(1)} %bitcast.33, bf16[8,512,256]{2,1,0:T(8,128)(2,1)S(1)} %bitcast.44, bf16[36,256,256]{2,1,0:T(8,128)(2,1)S(1)} %bitcast.22, ...), custom_call_target="tpu_custom_call" | custom-call | flops 603979776 | bytes 1024 | tf_op jit(solution)/shard_map/early_1_2/pallas_call | solution.py:52
  24.5 0.8 late_1_2.1.refs_3_
  25.3 1.0 %early_0_2.1 = (bf16[512,256]{1,0:T(8,128)(2,1)S(1)}, bf16[512,256]{1,0:T(8,128)(2,1)S(1)}) custom-call(s32[4,32]{1,0:T(4,128)S(1)} %copy-done.4, bf16[8,512,256]{2,1,0:T(8,128)(2,1)S(1)} %bitcast.34, bf16[8,512,256]{2,1,0:T(8,128)(2,1)S(1)} %bitcast.45, bf16[36,256,256]{2,1,0:T(8,128)(2,1)S(1)} %bitcast.24, ...), custom_call_target="tpu_custom_call" | custom-call | flops 603979776 | bytes 1024 | tf_op jit(solution)/shard_map/early_0_2/pallas_call | solution.py:52
  26.3 0.8 late_0_2.1.refs_2_
  27.2 3.9 %collective-permute-start.5 = (bf16[512,256]{1,0:T(8,128)(2,1)S(1)}, bf16[512,256]{1,0:T(8,128)(2,1)S(1)}, u32[]{:S(2)}, u32[]{:S(2)}) collective-permute-start(bf16[512,256]{1,0:T(8,128)(2,1)S(1)} %late_0_2.1.refs_2_), channel_id=1, source_target_pairs={{8,16},{24,32},{40,48},{56,64},{72,80},{88,96},{104,112},{16,8},{3... | collective-permute-start | bytes 786440 | tf_op jit(solution)/shard_map/ppermute | solution.py:296
  31.2 2.3 %wgrad2_1.1.refs_5_ = f32[9,256,256]{2,1,0:T(8,128)S(1)} custom-call(s32[4,32]{1,0:T(4,128)S(1)} %copy-done.4, bf16[8,512,256]{2,1,0:T(8,128)(2,1)S(1)} %bitcast.35, bf16[512,256]{1,0:T(8,128)(2,1)S(1)} %get-tuple-element.55.g2.refs_0_, bf16[512,256]{1,0:T(8,128)(2,1)S(1)} %get-tuple-element.64.refs_1_, bf16[512,256]{1,0:T(8,128)(2,1)S(1)} %get-tuple-element.65.refs_2_), custom_call_target="tpu_custom_call" | custom-call | flops 1811939328 | bytes 1024 | tf_op jit(solution)/shard_map/wgrad2_1/pallas_call | solution.py:52
  33.5 2.3 %wgrad2_0.1.refs_4_ = f32[9,256,256]{2,1,0:T(8,128)S(1)} custom-call(s32[4,32]{1,0:T(4,128)S(1)} %copy-done.4, bf16[8,512,256]{2,1,0:T(8,128)(2,1)S(1)} %bitcast.36, bf16[512,256]{1,0:T(8,128)(2,1)S(1)} %get-tuple-element.58.g2.refs_0_, bf16[512,256]{1,0:T(8,128)(2,1)S(1)} %get-tuple-element.62.refs_1_, bf16[512,256]{1,0:T(8,128)(2,1)S(1)} %get-tuple-element.63.refs_2_), custom_call_target="tpu_custom_call" | custom-call | flops 1811939328 | bytes 1024 | tf_op jit(solution)/shard_map/wgrad2_0/pallas_call | solution.py:52
  35.7 1.2 %collective-permute-done.5.refs_1_ = bf16[512,256]{1,0:T(8,128)(2,1)S(1)} collective-permute-done((bf16[512,256]{1,0:T(8,128)(2,1)S(1)}, bf16[512,256]{1,0:T(8,128)(2,1)S(1)}, u32[]{:S(2)}, u32[]{:S(2)}) %collective-permute-start.5) | collective-permute-done | bytes 262176 | tf_op jit(solution)/shard_map/ppermute | solution.py:296
  37.0 2.3 %last_two.1 = (bf16[4,2,3,32,256]{4,3,2,1,0:T(8,128)(2,1)S(1)}, bf16[4,2,3,32,256]{4,3,2,1,0:T(8,128)(2,1)S(1)}, bf16[4,2,3,32,256]{4,3,2,1,0:T(8,128)(2,1)S(1)}...) custom-call(s32[4,32]{1,0:T(4,128)S(1)} %copy-done.4, ...), custom_call_target="tpu_custom_call" | custom-call | flops 1207959552 | bytes 1024 | tf_op jit(solution)/shard_map/last_two/pallas_call | solution.py:52
  39.3 2.0 %collective-permute-start.8 = (bf16[4,2,3,32,256]{4,3,2,1,0:T(8,128)(2,1)S(1)}, bf16[4,2,3,32,256]{4,3,2,1,0:T(8,128)(2,1)S(1)}, u32[]{:S(2)}, u32[]{:S(2)}) collective-permute-start(bf16[4,2,3,32,256]{4,3,2,1,0:T(8,128)(2,1)S(1)} %get-tuple-element.77), channel_id=1, source_target_pairs={{0,1},{1,0},{2,3},{3,2},{4,5},{5,4},{6,7},{7,6},{8,9},{9,8},{10,11... | collective-permute-start | bytes 1179656 | tf_op jit(solution)/shard_map/ppermute | solution.py:300
  41.3 2.5 %collective-permute-start.9 = (bf16[4,2,3,32,256]{4,3,2,1,0:T(8,128)(2,1)S(1)}, bf16[4,2,3,32,256]{4,3,2,1,0:T(8,128)(2,1)S(1)}, u32[]{:S(2)}, u32[]{:S(2)}) collective-permute-start(bf16[4,2,3,32,256]{4,3,2,1,0:T(8,128)(2,1)S(1)} %get-tuple-element.78), channel_id=1, source_target_pairs={{0,3},{1,2},{2,1},{3,0},{4,7},{5,6},{6,5},{7,4},{8,11},{9,10},{10,... | collective-permute-start | bytes 1179656 | tf_op jit(solution)/shard_map/ppermute | solution.py:300
  43.9 2.6 %collective-permute-start.10 = (bf16[4,2,3,32,256]{4,3,2,1,0:T(8,128)(2,1)S(1)}, bf16[4,2,3,32,256]{4,3,2,1,0:T(8,128)(2,1)S(1)}, u32[]{:S(2)}, u32[]{:S(2)}) collective-permute-start(bf16[4,2,3,32,256]{4,3,2,1,0:T(8,128)(2,1)S(1)} %get-tuple-element.79), channel_id=1, source_target_pairs={{0,4},{1,5},{2,6},{3,7},{4,0},{5,1},{6,2},{7,3},{8,12},{9,13},{10,... | collective-permute-start | bytes 1179656 | tf_op jit(solution)/shard_map/ppermute | solution.py:300
  46.4 0.8 early_0_3.1.g1_zero.refs_2_
  47.3 0.8 early_1_3.1.g1_one.refs_3_
  48.1 3.4 %last_one.1 = (bf16[4,2,3,32,256]{4,3,2,1,0:T(8,128)(2,1)S(1)}, bf16[4,2,3,32,256]{4,3,2,1,0:T(8,128)(2,1)S(1)}, bf16[4,2,3,32,256]{4,3,2,1,0:T(8,128)(2,1)S(1)}...) custom-call(s32[4,32]{1,0:T(4,128)S(1)} %copy-done.4, ...), custom_call_target="tpu_custom_call" | custom-call | flops 2415919104 | bytes 1024 | tf_op jit(solution)/shard_map/last_one/pallas_call | solution.py:52
  51.5 1.1 %collective-permute-start.6 = (bf16[4,2,3,32,256]{4,3,2,1,0:T(8,128)(2,1)S(1)}, bf16[4,2,3,32,256]{4,3,2,1,0:T(8,128)(2,1)S(1)}, u32[]{:S(2)}, u32[]{:S(2)}) collective-permute-start(bf16[4,2,3,32,256]{4,3,2,1,0:T(8,128)(2,1)S(1)} %get-tuple-element.70), channel_id=1, source_target_pairs={{0,1},{1,0},{2,3},{3,2},{4,5},{5,4},{6,7},{7,6},{8,9},{9,8},{10,11... | collective-permute-start | bytes 1179656 | tf_op jit(solution)/shard_map/ppermute | solution.py:300
  53.2 0.9 %collective-permute-start.18 = (bf16[4,2,3,32,256]{4,3,2,1,0:T(8,128)(2,1)S(1)}, bf16[4,2,3,32,256]{4,3,2,1,0:T(8,128)(2,1)S(1)}, u32[]{:S(2)}, u32[]{:S(2)}) collective-permute-start(bf16[4,2,3,32,256]{4,3,2,1,0:T(8,128)(2,1)S(1)} %get-tuple-element.99), channel_id=1, source_target_pairs={{0,4},{1,5},{2,6},{3,7},{4,0},{5,1},{6,2},{7,3},{8,12},{9,13},{10,... | collective-permute-start | bytes 1179656 | tf_op jit(solution)/shard_map/ppermute | solution.py:300
  54.1 1.2 %collective-permute-done.10.refs_5_ = bf16[4,2,3,32,256]{4,3,2,1,0:T(8,128)(2,1)S(1)} collective-permute-done((bf16[4,2,3,32,256]{4,3,2,1,0:T(8,128)(2,1)S(1)}, bf16[4,2,3,32,256]{4,3,2,1,0:T(8,128)(2,1)S(1)}, u32[]{:S(2)}, u32[]{:S(2)}) %collective-permute-start.10) | collective-permute-done | bytes 393248 | tf_op jit(solution)/shard_map/ppermute | solution.py:300
  55.6 4.1 %collective-permute-start.11 = (bf16[2,2,3,32,256]{4,3,2,1,0:T(8,128)(2,1)S(1)}, bf16[2,2,3,32,256]{4,3,2,1,0:T(8,128)(2,1)S(1)}, u32[]{:S(2)}, u32[]{:S(2)}) collective-permute-start(bf16[2,2,3,32,256]{4,3,2,1,0:T(8,128)(2,1)S(1)} %get-tuple-element.83), channel_id=1, source_target_pairs={{0,4},{1,5},{2,6},{3,7},{4,0},{5,1},{6,2},{7,3},{8,12},{9,13},{10,... | collective-permute-start | bytes 589832 | tf_op jit(solution)/shard_map/ppermute | solution.py:300
  59.7 1.1 %collective-permute-start.12 = (bf16[2,2,3,32,256]{4,3,2,1,0:T(8,128)(2,1)S(1)}, bf16[2,2,3,32,256]{4,3,2,1,0:T(8,128)(2,1)S(1)}, u32[]{:S(2)}, u32[]{:S(2)}) collective-permute-start(bf16[2,2,3,32,256]{4,3,2,1,0:T(8,128)(2,1)S(1)} %get-tuple-element.84), channel_id=1, source_target_pairs={{0,1},{1,0},{2,3},{3,2},{4,5},{5,4},{6,7},{7,6},{8,9},{9,8},{10,11... | collective-permute-start | bytes 589832 | tf_op jit(solution)/shard_map/ppermute | solution.py:300
  60.8 2.6 %collective-permute-done.6.refs_1_ = bf16[4,2,3,32,256]{4,3,2,1,0:T(8,128)(2,1)S(1)} collective-permute-done((bf16[4,2,3,32,256]{4,3,2,1,0:T(8,128)(2,1)S(1)}, bf16[4,2,3,32,256]{4,3,2,1,0:T(8,128)(2,1)S(1)}, u32[]{:S(2)}, u32[]{:S(2)}) %collective-permute-start.6) | collective-permute-done | bytes 393248 | tf_op jit(solution)/shard_map/ppermute | solution.py:300
  63.4 0.9 %collective-permute-start.13 = (bf16[2,2,3,32,256]{4,3,2,1,0:T(8,128)(2,1)S(1)}, bf16[2,2,3,32,256]{4,3,2,1,0:T(8,128)(2,1)S(1)}, u32[]{:S(2)}, u32[]{:S(2)}) collective-permute-start(bf16[2,2,3,32,256]{4,3,2,1,0:T(8,128)(2,1)S(1)} %get-tuple-element.85), channel_id=1, source_target_pairs={{0,3},{1,2},{2,1},{3,0},{4,7},{5,6},{6,5},{7,4},{8,11},{9,10},{10,... | collective-permute-start | bytes 589832 | tf_op jit(solution)/shard_map/ppermute | solution.py:300
  64.3 2.2 %late_3.1 = (bf16[2,512,256]{2,1,0:T(8,128)(2,1)}, f32[8,128]{1,0:T(8,128)S(1)}) custom-call(bf16[36,256,256]{2,1,0:T(8,128)(2,1)S(1)} %bitcast.28, bf16[512,256]{1,0:T(8,128)(2,1)S(1)} %early_0_3.1.g1_zero.refs_2_, bf16[512,256]{1,0:T(8,128)(2,1)S(1)} %early_1_3.1.g1_one.refs_3_), custom_call_target="tpu_custom_call" | custom-call | flops 1207959552 | bytes 1024 | tf_op jit(solution)/shard_map/late_3/pallas_call | solution.py:52
  66.6 2.3 %collective-permute-start.7 = (bf16[2,2,3,32,256]{4,3,2,1,0:T(8,128)(2,1)S(1)}, bf16[2,2,3,32,256]{4,3,2,1,0:T(8,128)(2,1)S(1)}, u32[]{:S(2)}, u32[]{:S(2)}) collective-permute-start(bf16[2,2,3,32,256]{4,3,2,1,0:T(8,128)(2,1)S(1)} %get-tuple-element.73), channel_id=1, source_target_pairs={{0,4},{1,5},{2,6},{3,7},{4,0},{5,1},{6,2},{7,3},{8,12},{9,13},{10,... | collective-permute-start | bytes 589832 | tf_op jit(solution)/shard_map/ppermute | solution.py:300
  69.9 2.6 %collective-permute-start.19 = (bf16[2,2,3,32,256]{4,3,2,1,0:T(8,128)(2,1)S(1)}, bf16[2,2,3,32,256]{4,3,2,1,0:T(8,128)(2,1)S(1)}, u32[]{:S(2)}, u32[]{:S(2)}) collective-permute-start(bf16[2,2,3,32,256]{4,3,2,1,0:T(8,128)(2,1)S(1)} %get-tuple-element.101), channel_id=1, source_target_pairs={{0,3},{1,2},{2,1},{3,0},{4,7},{5,6},{6,5},{7,4},{8,11},{9,10},{10,... | collective-permute-start | bytes 589832 | tf_op jit(solution)/shard_map/ppermute | solution.py:300
  72.6 1.3 %collective-permute-done.7.got = bf16[2,2,3,32,256]{4,3,2,1,0:T(8,128)(2,1)S(1)} collective-permute-done((bf16[2,2,3,32,256]{4,3,2,1,0:T(8,128)(2,1)S(1)}, bf16[2,2,3,32,256]{4,3,2,1,0:T(8,128)(2,1)S(1)}, u32[]{:S(2)}, u32[]{:S(2)}) %collective-permute-start.7) | collective-permute-done | bytes 196640 | tf_op jit(solution)/shard_map/ppermute | solution.py:300
  73.9 0.9 %collective-permute-done.16.refs_1_ = bf16[2,2,3,32,256]{4,3,2,1,0:T(8,128)(2,1)S(1)} collective-permute-done((bf16[2,2,3,32,256]{4,3,2,1,0:T(8,128)(2,1)S(1)}, bf16[2,2,3,32,256]{4,3,2,1,0:T(8,128)(2,1)S(1)}, u32[]{:S(2)}, u32[]{:S(2)}) %collective-permute-start.16) | collective-permute-done | bytes 196640 | tf_op jit(solution)/shard_map/ppermute | solution.py:300
  74.9 1.5 %collective-permute-start.17 = (bf16[1,2,2,3,32,256]{5,4,3,2,1,0:T(8,128)(2,1)S(1)}, bf16[1,2,2,3,32,256]{5,4,3,2,1,0:T(8,128)(2,1)S(1)}, u32[]{:S(2)}, u32[]{:S(2)}) collective-permute-start(bf16[1,2,2,3,32,256]{5,4,3,2,1,0:T(8,128)(2,1)S(1)} %get-tuple-element.97), channel_id=1, source_target_pairs={{0,4},{1,5},{2,6},{3,7},{4,0},{5,1},{6,2},{7,3},{8,12},{9,13},{10,... | collective-permute-start | bytes 589832 | tf_op jit(solution)/shard_map/ppermute | solution.py:300
  76.3 2.2 %collective-permute-start.14 = (bf16[1,2,2,3,32,256]{5,4,3,2,1,0:T(8,128)(2,1)S(1)}, bf16[1,2,2,3,32,256]{5,4,3,2,1,0:T(8,128)(2,1)S(1)}, u32[]{:S(2)}, u32[]{:S(2)}) collective-permute-start(bf16[1,2,2,3,32,256]{5,4,3,2,1,0:T(8,128)(2,1)S(1)} %get-tuple-element.89), channel_id=1, source_target_pairs={{0,3},{1,2},{2,1},{3,0},{4,7},{5,6},{6,5},{7,4},{8,11},{9,10},{10,... | collective-permute-start | bytes 589832 | tf_op jit(solution)/shard_map/ppermute | solution.py:300
  78.7 3.5 %collective-permute-done.17.refs_3_ = bf16[1,2,2,3,32,256]{5,4,3,2,1,0:T(8,128)(2,1)S(1)} collective-permute-done((bf16[1,2,2,3,32,256]{5,4,3,2,1,0:T(8,128)(2,1)S(1)}, bf16[1,2,2,3,32,256]{5,4,3,2,1,0:T(8,128)(2,1)S(1)}, u32[]{:S(2)}, u32[]{:S(2)}) %collective-permute-start.17) | collective-permute-done | bytes 196640 | tf_op jit(solution)/shard_map/ppermute | solution.py:300
  82.1 1.1 %collective-permute-done.14.refs_1_ = bf16[1,2,2,3,32,256]{5,4,3,2,1,0:T(8,128)(2,1)S(1)} collective-permute-done((bf16[1,2,2,3,32,256]{5,4,3,2,1,0:T(8,128)(2,1)S(1)}, bf16[1,2,2,3,32,256]{5,4,3,2,1,0:T(8,128)(2,1)S(1)}, u32[]{:S(2)}, u32[]{:S(2)}) %collective-permute-start.14) | collective-permute-done | bytes 196640 | tf_op jit(solution)/shard_map/ppermute | solution.py:300
  83.3 1.0 %collective-permute-done.20.got = bf16[1,2,2,3,32,256]{5,4,3,2,1,0:T(8,128)(2,1)S(1)} collective-permute-done((bf16[1,2,2,3,32,256]{5,4,3,2,1,0:T(8,128)(2,1)S(1)}, bf16[1,2,2,3,32,256]{5,4,3,2,1,0:T(8,128)(2,1)S(1)}, u32[]{:S(2)}, u32[]{:S(2)}) %collective-permute-start.20) | collective-permute-done | bytes 196640 | tf_op jit(solution)/shard_map/ppermute | solution.py:300
  84.3 1.1 %finish.1 = f32[2,2,9,32,256]{4,3,2,1,0:T(8,128)} custom-call(f32[2,2,6,32,256]{4,3,2,1,0:T(8,128)S(1)} %finish_some.1.some, bf16[1,2,2,3,32,256]{5,4,3,2,1,0:T(8,128)(2,1)S(1)} %get-tuple-element.104.keep, bf16[1,2,2,3,32,256]{5,4,3,2,1,0:T(8,128)(2,1)S(1)} %collective-permute-done.20.got), custom_call_target="tpu_custom_call" | custom-call | flops 603979776 | bytes 1024 | tf_op jit(solution)/shard_map/finish/pallas_call | solution.py:52
  (41 shorter events, 3.5 us)
Async XLA Ops:
  0.6 2.9 %slice-start = ((s8[4718592]{0:T(1024)(128)(4,1)}), s8[4194304]{0:T(1024)(128)(4,1)S(1)}, s32[]{:S(2)}) async-start(s8[4718592]{0:T(1024)(128)(4,1)} %bitcast.12), calls=%async_computation | async-start | bytes 8388608
  0.6 0.8 copy-start.4
  1.5 2.1 %slice-start.1 = ((s8[4718592]{0:T(1024)(128)(4,1)}), s8[524288]{0:T(1024)(128)(4,1)S(1)}, s32[]{:S(2)}) async-start(s8[4718592]{0:T(1024)(128)(4,1)} %bitcast.12), calls=%async_computation.1 | async-start | bytes 1048576
  5.2 6.6 %collective-permute-start = (bf16[512,256]{1,0:T(8,128)(2,1)S(1)}, bf16[512,256]{1,0:T(8,128)(2,1)S(1)}, u32[]{:S(2)}, u32[]{:S(2)}) collective-permute-start(bf16[512,256]{1,0:T(8,128)(2,1)S(1)} %late_1_0.1.refs_1_), channel_id=1, source_target_pairs={{0,8},{16,24},{32,40},{48,56},{64,72},{80,88},{96,104},{112,120},{... | collective-permute-start | bytes 786440 | tf_op jit(solution)/shard_map/ppermute | solution.py:296
  6.1 5.7 %copy-start = (bf16[2,1,4,1,16,32,256]{6,5,4,3,2,1,0:T(8,128)(2,1)S(1)}, bf16[2,1,4,1,16,32,256]{6,5,4,3,2,1,0:T(8,128)(2,1)}, u32[]{:S(2)}) copy-start(bf16[2,1,4,1,16,32,256]{6,5,4,3,2,1,0:T(8,128)(2,1)} %param.10) | copy-start | bytes 6291460
  6.2 5.7 %copy-start.1 = (bf16[2,1,4,1,16,32,256]{6,5,4,3,2,1,0:T(8,128)(2,1)S(1)}, bf16[2,1,4,1,16,32,256]{6,5,4,3,2,1,0:T(8,128)(2,1)}, u32[]{:S(2)}) copy-start(bf16[2,1,4,1,16,32,256]{6,5,4,3,2,1,0:T(8,128)(2,1)} %param.11) | copy-start | bytes 6291460
  7.0 9.9 %collective-permute-start.2 = (bf16[512,256]{1,0:T(8,128)(2,1)S(1)}, bf16[512,256]{1,0:T(8,128)(2,1)S(1)}, u32[]{:S(2)}, u32[]{:S(2)}) collective-permute-start(bf16[512,256]{1,0:T(8,128)(2,1)S(1)} %late_0_0.1.refs_1_), channel_id=1, source_target_pairs={{8,16},{24,32},{40,48},{56,64},{72,80},{88,96},{104,112},{16,8},{3... | collective-permute-start | bytes 786440 | tf_op jit(solution)/shard_map/ppermute | solution.py:296
  12.8 4.1 %copy-start.3 = (bf16[3,1,16,32,256]{4,3,2,1,0:T(8,128)(2,1)S(1)}, bf16[3,1,16,32,256]{4,3,2,1,0:T(8,128)(2,1)}, u32[]{:S(2)}) copy-start(bf16[3,1,16,32,256]{4,3,2,1,0:T(8,128)(2,1)} %param.8) | copy-start | bytes 2359300
  13.7 9.8 %collective-permute-start.1 = (bf16[512,256]{1,0:T(8,128)(2,1)S(1)}, bf16[512,256]{1,0:T(8,128)(2,1)S(1)}, u32[]{:S(2)}, u32[]{:S(2)}) collective-permute-start(bf16[512,256]{1,0:T(8,128)(2,1)S(1)} %late_0_1.1.refs_5_), channel_id=1, source_target_pairs={{8,16},{24,32},{40,48},{56,64},{72,80},{88,96},{104,112},{16,8},{3... | collective-permute-start | bytes 786440 | tf_op jit(solution)/shard_map/ppermute | solution.py:296
  18.0 1.6 %copy-start.2 = (bf16[2,1,4,1,16,32,256]{6,5,4,3,2,1,0:T(8,128)(2,1)S(1)}, bf16[2,1,4,1,16,32,256]{6,5,4,3,2,1,0:T(8,128)(2,1)}, u32[]{:S(2)}) copy-start(bf16[2,1,4,1,16,32,256]{6,5,4,3,2,1,0:T(8,128)(2,1)} %param.9) | copy-start | bytes 6291460
  18.8 6.5 %collective-permute-start.4 = (bf16[512,256]{1,0:T(8,128)(2,1)S(1)}, bf16[512,256]{1,0:T(8,128)(2,1)S(1)}, u32[]{:S(2)}, u32[]{:S(2)}) collective-permute-start(bf16[512,256]{1,0:T(8,128)(2,1)S(1)} %late_1_1.1.refs_5_), channel_id=1, source_target_pairs={{0,8},{16,24},{32,40},{48,56},{64,72},{80,88},{96,104},{112,120},{... | collective-permute-start | bytes 786440 | tf_op jit(solution)/shard_map/ppermute | solution.py:296
  27.2 9.8 %collective-permute-start.5 = (bf16[512,256]{1,0:T(8,128)(2,1)S(1)}, bf16[512,256]{1,0:T(8,128)(2,1)S(1)}, u32[]{:S(2)}, u32[]{:S(2)}) collective-permute-start(bf16[512,256]{1,0:T(8,128)(2,1)S(1)} %late_0_2.1.refs_2_), channel_id=1, source_target_pairs={{8,16},{24,32},{40,48},{56,64},{72,80},{88,96},{104,112},{16,8},{3... | collective-permute-start | bytes 786440 | tf_op jit(solution)/shard_map/ppermute | solution.py:296
  31.1 5.9 %collective-permute-start.3 = (bf16[512,256]{1,0:T(8,128)(2,1)S(1)}, bf16[512,256]{1,0:T(8,128)(2,1)S(1)}, u32[]{:S(2)}, u32[]{:S(2)}) collective-permute-start(bf16[512,256]{1,0:T(8,128)(2,1)S(1)} %late_1_2.1.refs_3_), channel_id=1, source_target_pairs={{0,8},{16,24},{32,40},{48,56},{64,72},{80,88},{96,104},{112,120},{... | collective-permute-start | bytes 786440 | tf_op jit(solution)/shard_map/ppermute | solution.py:296
  39.3 13.9 %collective-permute-start.8 = (bf16[4,2,3,32,256]{4,3,2,1,0:T(8,128)(2,1)S(1)}, bf16[4,2,3,32,256]{4,3,2,1,0:T(8,128)(2,1)S(1)}, u32[]{:S(2)}, u32[]{:S(2)}) collective-permute-start(bf16[4,2,3,32,256]{4,3,2,1,0:T(8,128)(2,1)S(1)} %get-tuple-element.77), channel_id=1, source_target_pairs={{0,1},{1,0},{2,3},{3,2},{4,5},{5,4},{6,7},{7,6},{8,9},{9,8},{10,11... | collective-permute-start | bytes 1179656 | tf_op jit(solution)/shard_map/ppermute | solution.py:300
  41.3 12.8 %collective-permute-start.9 = (bf16[4,2,3,32,256]{4,3,2,1,0:T(8,128)(2,1)S(1)}, bf16[4,2,3,32,256]{4,3,2,1,0:T(8,128)(2,1)S(1)}, u32[]{:S(2)}, u32[]{:S(2)}) collective-permute-start(bf16[4,2,3,32,256]{4,3,2,1,0:T(8,128)(2,1)S(1)} %get-tuple-element.78), channel_id=1, source_target_pairs={{0,3},{1,2},{2,1},{3,0},{4,7},{5,6},{6,5},{7,4},{8,11},{9,10},{10,... | collective-permute-start | bytes 1179656 | tf_op jit(solution)/shard_map/ppermute | solution.py:300
  43.9 11.5 %collective-permute-start.10 = (bf16[4,2,3,32,256]{4,3,2,1,0:T(8,128)(2,1)S(1)}, bf16[4,2,3,32,256]{4,3,2,1,0:T(8,128)(2,1)S(1)}, u32[]{:S(2)}, u32[]{:S(2)}) collective-permute-start(bf16[4,2,3,32,256]{4,3,2,1,0:T(8,128)(2,1)S(1)} %get-tuple-element.79), channel_id=1, source_target_pairs={{0,4},{1,5},{2,6},{3,7},{4,0},{5,1},{6,2},{7,3},{8,12},{9,13},{10,... | collective-permute-start | bytes 1179656 | tf_op jit(solution)/shard_map/ppermute | solution.py:300
  51.5 11.9 %collective-permute-start.6 = (bf16[4,2,3,32,256]{4,3,2,1,0:T(8,128)(2,1)S(1)}, bf16[4,2,3,32,256]{4,3,2,1,0:T(8,128)(2,1)S(1)}, u32[]{:S(2)}, u32[]{:S(2)}) collective-permute-start(bf16[4,2,3,32,256]{4,3,2,1,0:T(8,128)(2,1)S(1)} %get-tuple-element.70), channel_id=1, source_target_pairs={{0,1},{1,0},{2,3},{3,2},{4,5},{5,4},{6,7},{7,6},{8,9},{9,8},{10,11... | collective-permute-start | bytes 1179656 | tf_op jit(solution)/shard_map/ppermute | solution.py:300
  52.6 14.0 %collective-permute-start.15 = (bf16[4,2,3,32,256]{4,3,2,1,0:T(8,128)(2,1)S(1)}, bf16[4,2,3,32,256]{4,3,2,1,0:T(8,128)(2,1)S(1)}, u32[]{:S(2)}, u32[]{:S(2)}) collective-permute-start(bf16[4,2,3,32,256]{4,3,2,1,0:T(8,128)(2,1)S(1)} %get-tuple-element.91), channel_id=1, source_target_pairs={{0,3},{1,2},{2,1},{3,0},{4,7},{5,6},{6,5},{7,4},{8,11},{9,10},{10,... | collective-permute-start | bytes 1179656 | tf_op jit(solution)/shard_map/ppermute | solution.py:300
  53.2 15.8 %collective-permute-start.18 = (bf16[4,2,3,32,256]{4,3,2,1,0:T(8,128)(2,1)S(1)}, bf16[4,2,3,32,256]{4,3,2,1,0:T(8,128)(2,1)S(1)}, u32[]{:S(2)}, u32[]{:S(2)}) collective-permute-start(bf16[4,2,3,32,256]{4,3,2,1,0:T(8,128)(2,1)S(1)} %get-tuple-element.99), channel_id=1, source_target_pairs={{0,4},{1,5},{2,6},{3,7},{4,0},{5,1},{6,2},{7,3},{8,12},{9,13},{10,... | collective-permute-start | bytes 1179656 | tf_op jit(solution)/shard_map/ppermute | solution.py:300
  55.6 14.2 %collective-permute-start.11 = (bf16[2,2,3,32,256]{4,3,2,1,0:T(8,128)(2,1)S(1)}, bf16[2,2,3,32,256]{4,3,2,1,0:T(8,128)(2,1)S(1)}, u32[]{:S(2)}, u32[]{:S(2)}) collective-permute-start(bf16[2,2,3,32,256]{4,3,2,1,0:T(8,128)(2,1)S(1)} %get-tuple-element.83), channel_id=1, source_target_pairs={{0,4},{1,5},{2,6},{3,7},{4,0},{5,1},{6,2},{7,3},{8,12},{9,13},{10,... | collective-permute-start | bytes 589832 | tf_op jit(solution)/shard_map/ppermute | solution.py:300
  59.7 12.7 %collective-permute-start.12 = (bf16[2,2,3,32,256]{4,3,2,1,0:T(8,128)(2,1)S(1)}, bf16[2,2,3,32,256]{4,3,2,1,0:T(8,128)(2,1)S(1)}, u32[]{:S(2)}, u32[]{:S(2)}) collective-permute-start(bf16[2,2,3,32,256]{4,3,2,1,0:T(8,128)(2,1)S(1)} %get-tuple-element.84), channel_id=1, source_target_pairs={{0,1},{1,0},{2,3},{3,2},{4,5},{5,4},{6,7},{7,6},{8,9},{9,8},{10,11... | collective-permute-start | bytes 589832 | tf_op jit(solution)/shard_map/ppermute | solution.py:300
  63.4 9.1 %collective-permute-start.13 = (bf16[2,2,3,32,256]{4,3,2,1,0:T(8,128)(2,1)S(1)}, bf16[2,2,3,32,256]{4,3,2,1,0:T(8,128)(2,1)S(1)}, u32[]{:S(2)}, u32[]{:S(2)}) collective-permute-start(bf16[2,2,3,32,256]{4,3,2,1,0:T(8,128)(2,1)S(1)} %get-tuple-element.85), channel_id=1, source_target_pairs={{0,3},{1,2},{2,1},{3,0},{4,7},{5,6},{6,5},{7,4},{8,11},{9,10},{10,... | collective-permute-start | bytes 589832 | tf_op jit(solution)/shard_map/ppermute | solution.py:300
  66.6 7.3 %collective-permute-start.7 = (bf16[2,2,3,32,256]{4,3,2,1,0:T(8,128)(2,1)S(1)}, bf16[2,2,3,32,256]{4,3,2,1,0:T(8,128)(2,1)S(1)}, u32[]{:S(2)}, u32[]{:S(2)}) collective-permute-start(bf16[2,2,3,32,256]{4,3,2,1,0:T(8,128)(2,1)S(1)} %get-tuple-element.73), channel_id=1, source_target_pairs={{0,4},{1,5},{2,6},{3,7},{4,0},{5,1},{6,2},{7,3},{8,12},{9,13},{10,... | collective-permute-start | bytes 589832 | tf_op jit(solution)/shard_map/ppermute | solution.py:300
  69.1 5.8 %collective-permute-start.16 = (bf16[2,2,3,32,256]{4,3,2,1,0:T(8,128)(2,1)S(1)}, bf16[2,2,3,32,256]{4,3,2,1,0:T(8,128)(2,1)S(1)}, u32[]{:S(2)}, u32[]{:S(2)}) collective-permute-start(bf16[2,2,3,32,256]{4,3,2,1,0:T(8,128)(2,1)S(1)} %get-tuple-element.93), channel_id=1, source_target_pairs={{0,1},{1,0},{2,3},{3,2},{4,5},{5,4},{6,7},{7,6},{8,9},{9,8},{10,11... | collective-permute-start | bytes 589832 | tf_op jit(solution)/shard_map/ppermute | solution.py:300
  69.9 8.7 %collective-permute-start.19 = (bf16[2,2,3,32,256]{4,3,2,1,0:T(8,128)(2,1)S(1)}, bf16[2,2,3,32,256]{4,3,2,1,0:T(8,128)(2,1)S(1)}, u32[]{:S(2)}, u32[]{:S(2)}) collective-permute-start(bf16[2,2,3,32,256]{4,3,2,1,0:T(8,128)(2,1)S(1)} %get-tuple-element.101), channel_id=1, source_target_pairs={{0,3},{1,2},{2,1},{3,0},{4,7},{5,6},{6,5},{7,4},{8,11},{9,10},{10,... | collective-permute-start | bytes 589832 | tf_op jit(solution)/shard_map/ppermute | solution.py:300
  74.9 7.3 %collective-permute-start.17 = (bf16[1,2,2,3,32,256]{5,4,3,2,1,0:T(8,128)(2,1)S(1)}, bf16[1,2,2,3,32,256]{5,4,3,2,1,0:T(8,128)(2,1)S(1)}, u32[]{:S(2)}, u32[]{:S(2)}) collective-permute-start(bf16[1,2,2,3,32,256]{5,4,3,2,1,0:T(8,128)(2,1)S(1)} %get-tuple-element.97), channel_id=1, source_target_pairs={{0,4},{1,5},{2,6},{3,7},{4,0},{5,1},{6,2},{7,3},{8,12},{9,13},{10,... | collective-permute-start | bytes 589832 | tf_op jit(solution)/shard_map/ppermute | solution.py:300
  76.3 6.9 %collective-permute-start.14 = (bf16[1,2,2,3,32,256]{5,4,3,2,1,0:T(8,128)(2,1)S(1)}, bf16[1,2,2,3,32,256]{5,4,3,2,1,0:T(8,128)(2,1)S(1)}, u32[]{:S(2)}, u32[]{:S(2)}) collective-permute-start(bf16[1,2,2,3,32,256]{5,4,3,2,1,0:T(8,128)(2,1)S(1)} %get-tuple-element.89), channel_id=1, source_target_pairs={{0,3},{1,2},{2,1},{3,0},{4,7},{5,6},{6,5},{7,4},{8,11},{9,10},{10,... | collective-permute-start | bytes 589832 | tf_op jit(solution)/shard_map/ppermute | solution.py:300
  78.6 5.8 %collective-permute-start.20 = (bf16[1,2,2,3,32,256]{5,4,3,2,1,0:T(8,128)(2,1)S(1)}, bf16[1,2,2,3,32,256]{5,4,3,2,1,0:T(8,128)(2,1)S(1)}, u32[]{:S(2)}, u32[]{:S(2)}) collective-permute-start(bf16[1,2,2,3,32,256]{5,4,3,2,1,0:T(8,128)(2,1)S(1)} %get-tuple-element.105), channel_id=1, source_target_pairs={{0,1},{1,0},{2,3},{3,2},{4,5},{5,4},{6,7},{7,6},{8,9},{9,8},{10,11... | collective-permute-start | bytes 589832 | tf_op jit(solution)/shard_map/ppermute | solution.py:300
